TPU v7x, 32 devices: a whole 2x2x4 slice. The times are simulated.
32 devices in a mesh: dp: 4 (over y, x), seq: 4 (over z), mp: 2 (over core).
Axes of the slice: x: 2, y: 2, z: 4, core: 2. Of those that a mesh axis runs over, the one named last changes fastest.
Arguments:
- src: bfloat16 [8, 1024, 1024], P('dp', 'seq'), may hold values from -6 to 6
- tgt: bfloat16 [8, 1024, 1024], P('dp', 'seq'), may hold values from -6 to 6
- cotangent: bfloat16 [8, 1024, 1024], P('dp', 'seq'), may hold values from -6 to 6
- lengths: int32 [8, 8], P('dp'), may hold values from 1 to 800, as said below
- groups: int32 [8, 8], P('dp'), may hold values from 0 to 3, as said below
- enc_gains: bfloat16 [2, 1024], P(None, ('dp', 'seq')), may hold values from 0.5 to 1.5
- enc_biases: bfloat16 [2, 1024], P(None, ('dp', 'seq')), may hold values from -3 to 3
- enc_qkv: bfloat16 [3, 1024, 1024], P(None, ('dp', 'seq'), 'mp'), may hold values from -0.1875 to 0.1875
- enc_out: bfloat16 [1024, 1024], P('mp', ('dp', 'seq')), may hold values from -0.75 to 0.75
- enc_up: bfloat16 [1024, 4096], P(('dp', 'seq'), 'mp'), may hold values from -0.1875 to 0.1875
- enc_down: bfloat16 [4096, 1024], P('mp', ('dp', 'seq')), may hold values from -0.09375 to 0.09375
- dec_gains: bfloat16 [3, 1024], P(None, ('dp', 'seq')), may hold values from 0.5 to 1.5
- dec_biases: bfloat16 [3, 1024], P(None, ('dp', 'seq')), may hold values from -3 to 3
- dec_self_qkv: bfloat16 [3, 1024, 1024], P(None, ('dp', 'seq'), 'mp'), may hold values from -0.1875 to 0.1875
- dec_cross_qkv: bfloat16 [3, 1024, 1024], P(None, ('dp', 'seq'), 'mp'), may hold values from -0.1875 to 0.1875
- dec_outs: bfloat16 [2, 1024, 1024], P(None, 'mp', ('dp', 'seq')), may hold values from -0.75 to 0.75
- dec_up: bfloat16 [1024, 4096], P(('dp', 'seq'), 'mp'), may hold values from -0.1875 to 0.1875
- dec_down: bfloat16 [4096, 1024], P('mp', ('dp', 'seq')), may hold values from -0.09375 to 0.09375
Outputs:
- decoded: bfloat16 [8, 1024, 1024], P('dp', 'seq')
- src_grad: float32 [8, 1024, 1024], P('dp', 'seq')
- tgt_grad: float32 [8, 1024, 1024], P('dp', 'seq')
- memory_grad: float32 [8, 1024, 1024], P('dp', 'seq')
- enc_gains_grad: float32 [2, 1024], P(None, ('dp', 'seq'))
- enc_biases_grad: float32 [2, 1024], P(None, ('dp', 'seq'))
- enc_qkv_grad: float32 [3, 1024, 1024], P(None, ('dp', 'seq'), 'mp')
- enc_out_grad: float32 [1024, 1024], P('mp', ('dp', 'seq'))
- enc_up_grad: float32 [1024, 4096], P(('dp', 'seq'), 'mp')
- enc_down_grad: float32 [4096, 1024], P('mp', ('dp', 'seq'))
- dec_gains_grad: float32 [3, 1024], P(None, ('dp', 'seq'))
- dec_biases_grad: float32 [3, 1024], P(None, ('dp', 'seq'))
- dec_self_qkv_grad: float32 [3, 1024, 1024], P(None, ('dp', 'seq'), 'mp')
- dec_cross_qkv_grad: float32 [3, 1024, 1024], P(None, ('dp', 'seq'), 'mp')
- dec_outs_grad: float32 [2, 1024, 1024], P(None, 'mp', ('dp', 'seq'))
- dec_up_grad: float32 [1024, 4096], P(('dp', 'seq'), 'mp')
- dec_down_grad: float32 [4096, 1024], P('mp', ('dp', 'seq'))
Inputs may be any that keep to these rules, and one draw needn't show every extreme that they name: `lengths`: each row has 8 segments; one of them, in a slot drawn per row, has more than 256 tokens, each other one at most 32; the segments never fill more than 1024 positions, the rest is padding. `groups`: every group is named by one segment or more.
All inputs are finite; a program needn't handle non-finite values.
Results may differ from a plain program's by a relative error of at most 0.022.
Values may be sent and summed in bfloat16 or wider, within the bound.
No kernel may reach another device: no remote copies, remote signals or barrier semaphores. Data moves between devices by JAX's collectives and lax.ppermute only.
A program may use at most 320 MiB of HBM per device.

v0:
```python
import jax
import jax.numpy as jnp
from jax import lax
from jax.sharding import PartitionSpec as P

HEAD = 64
NSEG = 8
LANGS = 4


def layer_norm(values, gain, bias):
    center = values - jnp.mean(values, axis=-1, keepdims=True)
    spread = jnp.mean(center * center, axis=-1, keepdims=True)
    return center * lax.rsqrt(spread + 1e-05) * gain + bias


def gelu_exact(values):
    return jax.nn.gelu(values, approximate=False)


def matmul(left, right):
    return jnp.dot(left, right, preferred_element_type=jnp.float32)


def inner_rows(left, right):
    return lax.dot_general(
        left, right, (((0,), (0,)), ((), ())), preferred_element_type=jnp.float32
    )


def outer_cols(left, right):
    return lax.dot_general(
        left, right, (((1,), (1,)), ((), ())), preferred_element_type=jnp.float32
    )


def head_total(partial_value):
    return lax.psum(partial_value, "mp")


def feature_total(partial_value):
    return lax.psum(partial_value, "mp")


def score_table(query, keys, mask):
    scores = jnp.einsum(
        "rqhe,rkhe->rhqk", query, keys, preferred_element_type=jnp.float32
    ) * HEAD ** (-0.5)
    return jnp.where(mask[:, None], scores, -1e30)


def attn_forward(inputs, gain, bias, qkv, out_weight, mask, memory):
    rows, length, width = inputs.shape
    flat = inputs.reshape(rows * length, width)
    normed = layer_norm(flat, gain, bias).astype(jnp.bfloat16)
    if memory is None:
        source = normed
    else:
        source = memory.reshape(rows * length, width).astype(jnp.bfloat16)
    query = matmul(normed, qkv[0]).astype(jnp.bfloat16).reshape(rows, length, -1, HEAD)
    pair = jnp.einsum("nd,jdm->jnm", source, qkv[1:], preferred_element_type=jnp.float32).astype(
        jnp.bfloat16
    )
    pair = pair.reshape(2, rows, length, -1, HEAD)
    gathered = lax.all_gather(pair, "seq", axis=2, tiled=True)
    scores = score_table(query, gathered[0], mask)
    top = jnp.max(scores, axis=-1, keepdims=True)
    expd = jnp.exp(scores - top)
    total = jnp.sum(expd, axis=-1, keepdims=True)
    probs = (expd / total).astype(jnp.bfloat16)
    context = jnp.einsum("rhqk,rkhe->rqhe", probs, gathered[1], preferred_element_type=jnp.float32)
    context = context.astype(jnp.bfloat16).reshape(rows * length, -1)
    branch = head_total(matmul(context, out_weight))
    saved = (flat, normed, source, query, gathered, top + jnp.log(total), context)
    return (inputs + branch.reshape(inputs.shape), saved)


def attn_backward(grad, saved, gain, bias, qkv, out_weight, mask, cross):
    flat, normed, source, query, gathered, logsum, context = saved
    rows, length, width = grad.shape
    grad_low = grad.reshape(rows * length, width).astype(jnp.bfloat16)
    out_grad = inner_rows(context, grad_low)
    ctx_grad = outer_cols(grad_low, out_weight).astype(jnp.bfloat16).reshape(rows, length, -1, HEAD)
    scores = score_table(query, gathered[0], mask)
    probs = jnp.exp(scores - logsum)
    probs_low = probs.astype(jnp.bfloat16)
    value_part = jnp.einsum(
        "rhqk,rqhe->rkhe", probs_low, ctx_grad, preferred_element_type=jnp.float32
    )
    prob_grad = jnp.einsum(
        "rqhe,rkhe->rhqk", ctx_grad, gathered[1], preferred_element_type=jnp.float32
    )
    delta = jnp.sum(prob_grad * probs, axis=-1, keepdims=True)
    score_grad = (probs * (prob_grad - delta)).astype(jnp.bfloat16)
    query_grad = jnp.einsum(
        "rhqk,rkhe->rqhe", score_grad, gathered[0], preferred_element_type=jnp.float32
    ) * HEAD ** (-0.5)
    key_part = jnp.einsum(
        "rhqk,rqhe->rkhe", score_grad, query, preferred_element_type=jnp.float32
    ) * HEAD ** (-0.5)
    pair_grad = lax.psum_scatter(
        jnp.stack([key_part, value_part]).astype(jnp.bfloat16),
        "seq",
        scatter_dimension=2,
        tiled=True,
    )
    query_low = query_grad.astype(jnp.bfloat16).reshape(rows * length, -1)
    pair_low = pair_grad.reshape(2, rows * length, -1)
    first_grad = inner_rows(normed, query_low)
    rest_grad = jnp.einsum("nd,jnm->jdm", source, pair_low, preferred_element_type=jnp.float32)
    qkv_grad = jnp.concatenate([first_grad[None], rest_grad], axis=0)
    normed_part = outer_cols(query_low, qkv[0])
    source_part = jnp.einsum("jnm,jdm->nd", pair_low, qkv[1:], preferred_element_type=jnp.float32)
    if cross:
        summed = feature_total(jnp.stack([normed_part, source_part]))
        normed_grad = summed[0]
        memory_grad = summed[1].reshape(grad.shape)
    else:
        normed_grad = feature_total(normed_part + source_part)
        memory_grad = None
    _, pull = jax.vjp(layer_norm, flat, gain, bias)
    flat_grad, gain_grad, bias_grad = pull(normed_grad)
    return (
        grad + flat_grad.reshape(grad.shape),
        memory_grad,
        (gain_grad, bias_grad, qkv_grad, out_grad),
    )


def ffn_forward(inputs, gain, bias, up, down):
    rows, length, width = inputs.shape
    flat = inputs.reshape(rows * length, width)
    normed = layer_norm(flat, gain, bias).astype(jnp.bfloat16)
    pre = matmul(normed, up)
    act = gelu_exact(pre).astype(jnp.bfloat16)
    branch = head_total(matmul(act, down))
    return (inputs + branch.reshape(inputs.shape), (flat, normed, pre, act))


def ffn_backward(grad, saved, gain, bias, up, down):
    flat, normed, pre, act = saved
    rows, length, width = grad.shape
    grad_low = grad.reshape(rows * length, width).astype(jnp.bfloat16)
    down_grad = inner_rows(act, grad_low)
    _, gelu_pull = jax.vjp(gelu_exact, pre)
    (pre_grad,) = gelu_pull(outer_cols(grad_low, down))
    pre_low = pre_grad.astype(jnp.bfloat16)
    up_grad = inner_rows(normed, pre_low)
    normed_grad = feature_total(outer_cols(pre_low, up))
    _, norm_pull = jax.vjp(layer_norm, flat, gain, bias)
    flat_grad, gain_grad, bias_grad = norm_pull(normed_grad)
    return (grad + flat_grad.reshape(grad.shape), (gain_grad, bias_grad, up_grad, down_grad))


def norm_rows(fetched):
    return (
        fetched[0].astype(jnp.float32),
        fetched[1].astype(jnp.float32),
        fetched[6].astype(jnp.float32),
        fetched[7].astype(jnp.float32),
    )


def per_device(
    src,
    tgt,
    cotangent,
    lengths,
    groups,
    enc_gains,
    enc_biases,
    enc_qkv,
    enc_out,
    enc_up,
    enc_down,
    dec_gains,
    dec_biases,
    dec_self_qkv,
    dec_cross_qkv,
    dec_outs,
    dec_up,
    dec_down,
):
    rows, local_len, width = src.shape
    full_len = local_len * lax.axis_size("seq")
    offset = lax.axis_index("seq") * local_len
    ends = jnp.cumsum(lengths, axis=1)
    places = jnp.arange(full_len, dtype=jnp.int32)
    seg_full = jnp.sum((ends[:, None, :] <= places[None, :, None]).astype(jnp.int32), axis=2)
    seg_here = lax.dynamic_slice_in_dim(seg_full, offset, local_len, 1)
    here = offset + jnp.arange(local_len, dtype=jnp.int32)
    same = seg_here[:, :, None] == seg_full[:, None, :]
    causal = same & (places[None, None, :] <= here[None, :, None])
    onehot = (groups[:, :, None] == jnp.arange(LANGS, dtype=jnp.int32)[None, None, :]).astype(
        jnp.float32
    )
    local_counts = jnp.sum(onehot * lengths[:, :, None].astype(jnp.float32), axis=(0, 1))
    counts = lax.psum(local_counts, "dp")
    all_tokens = rows * lax.axis_size("dp") * full_len
    seg_weight = all_tokens / (LANGS * jnp.sum(onehot * counts[None, None, :], axis=2))
    seg_match = (seg_here[:, :, None] == jnp.arange(NSEG, dtype=jnp.int32)[None, None, :]).astype(
        jnp.float32
    )
    tok_weight = jnp.sum(seg_match * seg_weight[:, None, :], axis=2)
    fetched = (
        lax.all_gather(enc_gains, ("dp", "seq"), axis=1, tiled=True),
        lax.all_gather(enc_biases, ("dp", "seq"), axis=1, tiled=True),
        lax.all_gather(enc_qkv, ("dp", "seq"), axis=1, tiled=True),
        lax.all_gather(enc_out, ("dp", "seq"), axis=1, tiled=True),
        lax.all_gather(enc_up, ("dp", "seq"), axis=0, tiled=True),
        lax.all_gather(enc_down, ("dp", "seq"), axis=1, tiled=True),
        lax.all_gather(dec_gains, ("dp", "seq"), axis=1, tiled=True),
        lax.all_gather(dec_biases, ("dp", "seq"), axis=1, tiled=True),
        lax.all_gather(dec_self_qkv, ("dp", "seq"), axis=1, tiled=True),
        lax.all_gather(dec_cross_qkv, ("dp", "seq"), axis=1, tiled=True),
        lax.all_gather(dec_outs, ("dp", "seq"), axis=2, tiled=True),
        lax.all_gather(dec_up, ("dp", "seq"), axis=0, tiled=True),
        lax.all_gather(dec_down, ("dp", "seq"), axis=1, tiled=True),
    )
    e_gain, e_bias, d_gain, d_bias = norm_rows(fetched)
    enc_mid, saved_one = attn_forward(
        src.astype(jnp.float32), e_gain[0], e_bias[0], fetched[2], fetched[3], same, None
    )
    memory, saved_two = ffn_forward(enc_mid, e_gain[1], e_bias[1], fetched[4], fetched[5])
    dec_mid, saved_three = attn_forward(
        tgt.astype(jnp.float32), d_gain[0], d_bias[0], fetched[8], fetched[10][0], causal, None
    )
    dec_cross, saved_four = attn_forward(
        dec_mid, d_gain[1], d_bias[1], fetched[9], fetched[10][1], same, memory
    )
    decoded, saved_five = ffn_forward(dec_cross, d_gain[2], d_bias[2], fetched[11], fetched[12])
    fetched = (
        lax.all_gather(enc_gains, ("dp", "seq"), axis=1, tiled=True),
        lax.all_gather(enc_biases, ("dp", "seq"), axis=1, tiled=True),
        lax.all_gather(enc_qkv, ("dp", "seq"), axis=1, tiled=True),
        lax.all_gather(enc_out, ("dp", "seq"), axis=1, tiled=True),
        lax.all_gather(enc_up, ("dp", "seq"), axis=0, tiled=True),
        lax.all_gather(enc_down, ("dp", "seq"), axis=1, tiled=True),
        lax.all_gather(dec_gains, ("dp", "seq"), axis=1, tiled=True),
        lax.all_gather(dec_biases, ("dp", "seq"), axis=1, tiled=True),
        lax.all_gather(dec_self_qkv, ("dp", "seq"), axis=1, tiled=True),
        lax.all_gather(dec_cross_qkv, ("dp", "seq"), axis=1, tiled=True),
        lax.all_gather(dec_outs, ("dp", "seq"), axis=2, tiled=True),
        lax.all_gather(dec_up, ("dp", "seq"), axis=0, tiled=True),
        lax.all_gather(dec_down, ("dp", "seq"), axis=1, tiled=True),
    )
    e_gain, e_bias, d_gain, d_bias = norm_rows(fetched)
    out_grad = cotangent.astype(jnp.float32) * tok_weight[:, :, None]
    cross_in, fifth = ffn_backward(
        out_grad, saved_five, d_gain[2], d_bias[2], fetched[11], fetched[12]
    )
    mid_in, memory_grad, fourth = attn_backward(
        cross_in, saved_four, d_gain[1], d_bias[1], fetched[9], fetched[10][1], same, True
    )
    tgt_grad, unused_dec, third = attn_backward(
        mid_in, saved_three, d_gain[0], d_bias[0], fetched[8], fetched[10][0], causal, False
    )
    factor = 1.0 / all_tokens
    dec_gain_term = jnp.stack([third[0], fourth[0], fifth[0]]) * factor
    dec_bias_term = jnp.stack([third[1], fourth[1], fifth[1]]) * factor
    dec_self_term = third[2] * factor
    dec_cross_term = fourth[2] * factor
    dec_outs_term = jnp.stack([third[3], fourth[3]]) * factor
    dec_up_term = fifth[2] * factor
    dec_down_term = fifth[3] * factor
    mid_grad, second = ffn_backward(
        memory_grad, saved_two, e_gain[1], e_bias[1], fetched[4], fetched[5]
    )
    src_grad, unused_enc, first = attn_backward(
        mid_grad, saved_one, e_gain[0], e_bias[0], fetched[2], fetched[3], same, False
    )
    enc_gain_term = jnp.stack([first[0], second[0]]) * factor
    enc_bias_term = jnp.stack([first[1], second[1]]) * factor
    enc_qkv_term = first[2] * factor
    enc_out_term = first[3] * factor
    enc_up_term = second[2] * factor
    enc_down_term = second[3] * factor
    summed = (
        lax.psum_scatter(enc_gain_term, ("dp", "seq"), scatter_dimension=1, tiled=True),
        lax.psum_scatter(enc_bias_term, ("dp", "seq"), scatter_dimension=1, tiled=True),
        lax.psum_scatter(enc_qkv_term, ("dp", "seq"), scatter_dimension=1, tiled=True),
        lax.psum_scatter(enc_out_term, ("dp", "seq"), scatter_dimension=1, tiled=True),
        lax.psum_scatter(enc_up_term, ("dp", "seq"), scatter_dimension=0, tiled=True),
        lax.psum_scatter(enc_down_term, ("dp", "seq"), scatter_dimension=1, tiled=True),
        lax.psum_scatter(dec_gain_term, ("dp", "seq"), scatter_dimension=1, tiled=True),
        lax.psum_scatter(dec_bias_term, ("dp", "seq"), scatter_dimension=1, tiled=True),
        lax.psum_scatter(dec_self_term, ("dp", "seq"), scatter_dimension=1, tiled=True),
        lax.psum_scatter(dec_cross_term, ("dp", "seq"), scatter_dimension=1, tiled=True),
        lax.psum_scatter(dec_outs_term, ("dp", "seq"), scatter_dimension=2, tiled=True),
        lax.psum_scatter(dec_up_term, ("dp", "seq"), scatter_dimension=0, tiled=True),
        lax.psum_scatter(dec_down_term, ("dp", "seq"), scatter_dimension=1, tiled=True),
    )
    return (
        decoded.astype(jnp.bfloat16),
        src_grad,
        tgt_grad,
        memory_grad,
        summed[0],
        summed[1],
        summed[2],
        summed[3],
        summed[4],
        summed[5],
        summed[6],
        summed[7],
        summed[8],
        summed[9],
        summed[10],
        summed[11],
        summed[12],
    )


def solution(mesh):
    placed = (
        P("dp", "seq", None),
        P("dp", "seq", None),
        P("dp", "seq", None),
        P("dp", None),
        P("dp", None),
        P(None, ("dp", "seq")),
        P(None, ("dp", "seq")),
        P(None, ("dp", "seq"), "mp"),
        P("mp", ("dp", "seq")),
        P(("dp", "seq"), "mp"),
        P("mp", ("dp", "seq")),
        P(None, ("dp", "seq")),
        P(None, ("dp", "seq")),
        P(None, ("dp", "seq"), "mp"),
        P(None, ("dp", "seq"), "mp"),
        P(None, "mp", ("dp", "seq")),
        P(("dp", "seq"), "mp"),
        P("mp", ("dp", "seq")),
    )
    return jax.shard_map(
        per_device,
        mesh=mesh,
        in_specs=placed,
        out_specs=(
            P("dp", "seq", None),
            P("dp", "seq", None),
            P("dp", "seq", None),
            P("dp", "seq", None),
            P(None, ("dp", "seq")),
            P(None, ("dp", "seq")),
            P(None, ("dp", "seq"), "mp"),
            P("mp", ("dp", "seq")),
            P(("dp", "seq"), "mp"),
            P("mp", ("dp", "seq")),
            P(None, ("dp", "seq")),
            P(None, ("dp", "seq")),
            P(None, ("dp", "seq"), "mp"),
            P(None, ("dp", "seq"), "mp"),
            P(None, "mp", ("dp", "seq")),
            P(("dp", "seq"), "mp"),
            P("mp", ("dp", "seq")),
        ),
        check_vma=False,
    )
```

profile of v0, /device:TPU:0, one launch (start us, length us, event | category | flops | bytes accessed | tf_op | source)
XLA Modules:
  0.0 3420.1 jit_solution(13581515175454670830)
XLA Ops:
  11.9 42.4 %all-gather.2 = bf16[16,64,2]{1,2,0:T(2,128)(2,1)S(1)} all-gather(bf16[1,64,2]{1,2,0:T(2,128)(2,1)} %bitcast.586), channel_id=1, replica_groups=mesh['dp'=4,'seq'=4,'mp'=2] {'dp','seq'}, dimensions={0}, use_global_device_ids=true | all-gather | bytes 4352 | tf_op jit(solution)/shard_map/all_gather | solution.py:206
  54.4 35.8 %all-gather.3 = bf16[16,64,2]{1,2,0:T(2,128)(2,1)S(1)} all-gather(bf16[1,64,2]{1,2,0:T(2,128)(2,1)} %bitcast.587), channel_id=1, replica_groups=mesh['dp'=4,'seq'=4,'mp'=2] {'dp','seq'}, dimensions={0}, use_global_device_ids=true | all-gather | bytes 4352 | tf_op jit(solution)/shard_map/all_gather | solution.py:207
  102.1 37.6 %all-gather = bf16[16,64,3]{1,2,0:T(4,128)(2,1)S(1)} all-gather(bf16[1,64,3]{1,2,0:T(4,128)(2,1)S(1)} %bitcast.584), channel_id=1, replica_groups=mesh['dp'=4,'seq'=4,'mp'=2] {'dp','seq'}, dimensions={0}, use_global_device_ids=true | all-gather | bytes 6528 | tf_op jit(solution)/shard_map/all_gather | solution.py:212
  139.8 35.7 %all-gather.1 = bf16[16,64,3]{1,2,0:T(4,128)(2,1)S(1)} all-gather(bf16[1,64,3]{1,2,0:T(4,128)(2,1)S(1)} %bitcast.585), channel_id=1, replica_groups=mesh['dp'=4,'seq'=4,'mp'=2] {'dp','seq'}, dimensions={0}, use_global_device_ids=true | all-gather | bytes 6528 | tf_op jit(solution)/shard_map/all_gather | solution.py:213
  193.8 39.2 %all-gather.25.cloned.1.call-done = bf16[2,2,1024,8,64]{2,4,3,1,0:T(8,128)(2,1)} async-done(((bf16[2,2,256,8,64]{2,4,3,1,0:T(8,128)(2,1)}), bf16[2,2,1024,8,64]{2,4,3,1,0:T(8,128)(2,1)}) %all-gather.25.cloned.1.call-update) | async-done | bytes 4194320 | tf_op jit(solution)/shard_map/all_gather | solution.py:65
  251.4 37.8 %all-gather.27.cloned.1.call-done = bf16[512,1024]{0,1:T(8,128)(2,1)} async-done(((bf16[512,64]{0,1:T(8,128)(2,1)}), bf16[512,1024]{0,1:T(8,128)(2,1)}) %all-gather.27.cloned.1.call-update) | async-done | bytes 1048592 | tf_op jit(solution)/shard_map/all_gather | solution.py:209
  298.7 71.9 %all-gather.19.cloned.1.call-done = bf16[2,2,1024,8,64]{2,4,3,1,0:T(8,128)(2,1)} async-done(((bf16[2,2,256,8,64]{2,4,3,1,0:T(8,128)(2,1)}), bf16[2,2,1024,8,64]{2,4,3,1,0:T(8,128)(2,1)}) %all-gather.19.cloned.1.call-update) | async-done | bytes 4194320 | tf_op jit(solution)/shard_map/all_gather | solution.py:65
  389.2 42.9 %all-gather.21.cloned.1.call-done = bf16[2,512,1024]{1,2,0:T(8,128)(2,1)} async-done(((bf16[2,512,64]{1,2,0:T(8,128)(2,1)}), bf16[2,512,1024]{1,2,0:T(8,128)(2,1)}) %all-gather.21.cloned.1.call-update) | async-done | bytes 2097168 | tf_op jit(solution)/shard_map/all_gather | solution.py:216
  435.4 19.4 all-reduce.16.cloned.1.call-done
  458.8 76.3 %all-gather.29.cloned.1.call-done = bf16[1024,2048]{1,0:T(8,128)(2,1)} async-done(((bf16[64,2048]{1,0:T(8,128)(2,1)}), bf16[1024,2048]{1,0:T(8,128)(2,1)}) %all-gather.29.cloned.1.call-update) | async-done | bytes 4194320 | tf_op jit(solution)/shard_map/all_gather | solution.py:210
  535.1 15.4 multiply_convert_fusion.7
  550.5 62.2 %all-gather.31.cloned.1.call-done = bf16[2048,1024]{0,1:T(8,128)(2,1)} async-done(((bf16[2048,64]{0,1:T(8,128)(2,1)}), bf16[2048,1024]{0,1:T(8,128)(2,1)}) %all-gather.31.cloned.1.call-update) | async-done | bytes 4194320 | tf_op jit(solution)/shard_map/all_gather | solution.py:211
  620.1 26.5 all-reduce.30.cloned.1.call-done
  649.5 68.9 %all-gather.33.cloned.1.call-done = bf16[3,1024,512]{2,1,0:T(8,128)(2,1)} async-done(((bf16[3,64,512]{2,1,0:T(8,128)(2,1)}), bf16[3,1024,512]{2,1,0:T(8,128)(2,1)}) %all-gather.33.cloned.1.call-update) | async-done | bytes 3145744 | tf_op jit(solution)/shard_map/all_gather | solution.py:215
  736.2 70.8 %all-gather.35.cloned.1.call-done = bf16[2,2,1024,8,64]{2,4,3,1,0:T(8,128)(2,1)} async-done(((bf16[2,2,256,8,64]{2,4,3,1,0:T(8,128)(2,1)}), bf16[2,2,1024,8,64]{2,4,3,1,0:T(8,128)(2,1)}) %all-gather.35.cloned.1.call-update) | async-done | bytes 4194320 | tf_op jit(solution)/shard_map/all_gather | solution.py:65
  829.3 10.0 psum.82
  852.2 75.5 %all-gather.37.cloned.1.call-done = bf16[1024,2048]{1,0:T(8,128)(2,1)} async-done(((bf16[64,2048]{1,0:T(8,128)(2,1)}), bf16[1024,2048]{1,0:T(8,128)(2,1)}) %all-gather.37.cloned.1.call-update) | async-done | bytes 4194320 | tf_op jit(solution)/shard_map/all_gather | solution.py:217
  934.5 70.7 %all-gather.39.cloned.1.call-done = bf16[2048,1024]{0,1:T(8,128)(2,1)} async-done(((bf16[2048,64]{0,1:T(8,128)(2,1)}), bf16[2048,1024]{0,1:T(8,128)(2,1)}) %all-gather.39.cloned.1.call-update) | async-done | bytes 4194320 | tf_op jit(solution)/shard_map/all_gather | solution.py:218
  1005.1 15.5 add_convert_fusion.1
  1025.9 19.7 all-reduce.20.cloned.1.call-done
  1059.4 8.8 convert_bitcast_fusion.2
  1068.2 11.1 multiply_reduce_fusion.2
  1079.4 11.8 multiply_convert_fusion.2
  1108.8 66.2 %reduce-scatter.21.cloned.1.call-done = bf16[2,2,256,8,64]{2,4,3,1,0:T(8,128)(2,1)} async-done(((bf16[2,2,1024,8,64]{2,4,3,1,0:T(8,128)(2,1)}), bf16[2,2,256,8,64]{2,4,3,1,0:T(8,128)(2,1)}) %reduce-scatter.21.cloned.1.call-update) | async-done | bytes 1048592 | tf_op jit(solution)/shard_map/reduce_scatter | solution.py:101
  1186.6 29.0 all-reduce.22.cloned.1.call-done
  1215.7 8.8 add_convert_fusion
  1235.7 16.4 all-reduce.24.cloned.1.call-done
  1266.9 7.9 convert_bitcast_fusion
  1274.8 11.2 multiply_reduce_fusion
  1286.0 11.8 multiply_convert_fusion
  1307.0 12.5 multiply_reduce_fusion.1
  1319.5 15.9 multiply_convert_fusion.1
  1367.6 14.2 reduce-scatter.25.cloned.1.call-done
  1384.9 76.4 %reduce-scatter.23.cloned.1.call-done = bf16[2,2,256,8,64]{2,4,3,1,0:T(8,128)(2,1)} async-done(((bf16[2,2,1024,8,64]{2,4,3,1,0:T(8,128)(2,1)}), bf16[2,2,256,8,64]{2,4,3,1,0:T(8,128)(2,1)}) %reduce-scatter.23.cloned.1.call-update) | async-done | bytes 1048592 | tf_op jit(solution)/shard_map/reduce_scatter | solution.py:101
  1486.1 10.0 copy.254
  1500.6 8.0 copy.255
  1538.4 9.4 copy.252
  1547.8 9.5 copy.250
  1578.6 8.0 convolution_multiply_fusion.2
  1608.5 72.9 %reduce-scatter.39.cloned.1.call-done = f32[64,2]{1,0:T(8,128)} async-done(((f32[1024,2]{1,0:T(8,128)}), f32[64,2]{1,0:T(8,128)}) %reduce-scatter.39.cloned.1.call-update) | async-done | bytes 528
  1682.8 74.2 %reduce-scatter.41.cloned.1.call-done = f32[64,3]{1,0:T(8,128)} async-done(((f32[1024,3]{1,0:T(8,128)}), f32[64,3]{1,0:T(8,128)}) %reduce-scatter.41.cloned.1.call-update) | async-done | bytes 784
  1758.4 74.2 %reduce-scatter.43.cloned.1.call-done = f32[64,3]{1,0:T(8,128)} async-done(((f32[1024,3]{1,0:T(8,128)}), f32[64,3]{1,0:T(8,128)}) %reduce-scatter.43.cloned.1.call-update) | async-done | bytes 784
  1834.1 762.8 %all-reduce.26.cloned.1.call-done = (f32[3,1024,512]{2,0,1:T(4,128)}, f32[3,1024,512]{2,0,1:T(4,128)}, f32[3,1024,512]{2,0,1:T(4,128)}, f32[2,512,1024]{1,0,2:T(2,128)}) async-done(((f32[3,1024,512]{2,0,1:T(4,128)}, f32[3,1024,512]{2,0,1:T(4,128)}, f32[3,1024,512]{2,0,1:T(4,128)}, f32[2,512,1024]{1,0,2:T(2,128)}), (f32[3,1024,512]{2,0,1:T(4,128)}, f32[3,1024,512]{2,0,1:T(4,128)}, f32[3,1024,512]{2,0,1:T(4,128)}, ...) | async-done | bytes 23068688
  2603.7 177.4 %reduce-scatter.35.cloned.1.call-done = f32[2048,64]{0,1:T(8,128)} async-done(((f32[2048,1024]{0,1:T(8,128)}), f32[2048,64]{0,1:T(8,128)}) %reduce-scatter.35.cloned.1.call-update) | async-done | bytes 524304 | tf_op jit(solution)/shard_map/reduce_scatter | solution.py:291
  2781.2 182.7 %reduce-scatter.33.cloned.1.call-done = f32[64,2048]{1,0:T(8,128)} async-done(((f32[1024,2048]{1,0:T(8,128)}), f32[64,2048]{1,0:T(8,128)}) %reduce-scatter.33.cloned.1.call-update) | async-done | bytes 524304 | tf_op jit(solution)/shard_map/reduce_scatter | solution.py:290
  2963.9 84.7 %reduce-scatter.27.cloned.1.call-done = f32[512,64]{0,1:T(8,128)} async-done(((f32[512,1024]{0,1:T(8,128)}), f32[512,64]{0,1:T(8,128)}) %reduce-scatter.27.cloned.1.call-update) | async-done | bytes 131088 | tf_op jit(solution)/shard_map/reduce_scatter | solution.py:282
  3048.6 181.7 %reduce-scatter.31.cloned.1.call-done = f32[2048,64]{0,1:T(8,128)} async-done(((f32[2048,1024]{0,1:T(8,128)}), f32[2048,64]{0,1:T(8,128)}) %reduce-scatter.31.cloned.1.call-update) | async-done | bytes 524304 | tf_op jit(solution)/shard_map/reduce_scatter | solution.py:284
  3230.3 182.7 %reduce-scatter.29.cloned.1.call-done = f32[64,2048]{1,0:T(8,128)} async-done(((f32[1024,2048]{1,0:T(8,128)}), f32[64,2048]{1,0:T(8,128)}) %reduce-scatter.29.cloned.1.call-update) | async-done | bytes 524304 | tf_op jit(solution)/shard_map/reduce_scatter | solution.py:283
  (554 shorter events, 388.3 us)
Async XLA Ops:
  7.2 84.8 %all-gather.23.cloned.1.call-start = ((), (), s32[]{:S(2)}) async-start(), calls=%async_computation.15 | async-start | bytes 3342336 | tf_op jit(solution)/shard_map/all_gather | solution.py:208
  7.9 169.3 %all-gather.17.cloned.1.call-start = ((), (), s32[]{:S(2)}) async-start(), calls=%async_computation.12 | async-start | bytes 3342336 | tf_op jit(solution)/shard_map/all_gather | solution.py:214
  8.7 224.3 %all-gather.25.cloned.1.call-start = ((), (), s32[]{:S(2)}) async-start(), calls=%async_computation.16 | async-start | bytes 5242880 | tf_op jit(solution)/shard_map/all_gather | solution.py:65
  10.2 85.7 %copy-start.93 = (f32[1,2,2,128]{3,1,2,0:T(2,128)}, f32[1,2,2,128]{3,1,2,0:T(2,128)S(1)}, u32[]{:S(2)}) copy-start(f32[1,2,2,128]{3,1,2,0:T(2,128)S(1)} %copy.294) | copy-start | bytes 6148
  11.9 84.0 %copy-start.101 = (f32[512]{0:T(512)}, f32[512]{0:T(512)S(1)}, u32[]{:S(2)}) copy-start(f32[512]{0:T(512)S(1)} %rsqrt.67) | copy-start | bytes 6148
  90.2 96.3 %copy-start.78 = (f32[1,1024]{1,0:T(1,128)}, f32[1,1024]{1,0:T(1,128)S(1)}, u32[]{:S(2)}) copy-start(f32[1,1024]{1,0:T(1,128)S(1)} %get-tuple-element.159) | copy-start | bytes 12292
  90.2 367.2 %copy-start.86 = (f32[1,1024]{1,0:T(1,128)}, f32[1,1024]{1,0:T(1,128)S(1)}, u32[]{:S(2)}) copy-start(f32[1,1024]{1,0:T(1,128)S(1)} %get-tuple-element.158) | copy-start | bytes 12292
  100.7 188.5 %all-gather.27.cloned.1.call-start = ((), (), s32[]{:S(2)}) async-start(), calls=%async_computation.17 | async-start | bytes 1114112 | tf_op jit(solution)/shard_map/all_gather | solution.py:209
  101.3 269.3 %all-gather.19.cloned.1.call-start = ((), (), s32[]{:S(2)}) async-start(), calls=%async_computation.13 | async-start | bytes 5242880 | tf_op jit(solution)/shard_map/all_gather | solution.py:65
  101.6 78.5 %copy-start.95 = (f32[1,2,2,128]{3,1,2,0:T(2,128)}, f32[1,2,2,128]{3,1,2,0:T(2,128)S(1)}, u32[]{:S(2)}) copy-start(f32[1,2,2,128]{3,1,2,0:T(2,128)S(1)} %copy.291) | copy-start | bytes 6148
  102.1 78.0 %copy-start.103 = (f32[512]{0:T(512)}, f32[512]{0:T(512)S(1)}, u32[]{:S(2)}) copy-start(f32[512]{0:T(512)S(1)} %rsqrt.65) | copy-start | bytes 6148
  176.1 117.9 %copy-start.80 = (f32[1,1024]{1,0:T(1,128)}, f32[1,1024]{1,0:T(1,128)S(1)}, u32[]{:S(2)}) copy-start(f32[1,1024]{1,0:T(1,128)S(1)} %get-tuple-element.152) | copy-start | bytes 12292
  185.2 246.9 %all-gather.21.cloned.1.call-start = ((), (), s32[]{:S(2)}) async-start(), calls=%async_computation.14 | async-start | bytes 2228224 | tf_op jit(solution)/shard_map/all_gather | solution.py:216
  185.8 269.1 %all-reduce.16.cloned.1.call-start = ((), (), s32[]{:S(2)}) async-start(), calls=%async_computation.18 | async-start | bytes 4194304 | tf_op jit(solution)/shard_map/psum | solution.py:38
  292.5 242.6 %all-gather.29.cloned.1.call-start = ((), (), s32[]{:S(2)}) async-start(), calls=%async_computation.19 | async-start | bytes 4456448 | tf_op jit(solution)/shard_map/all_gather | solution.py:210
  293.3 319.5 %all-gather.31.cloned.1.call-start = ((), (), s32[]{:S(2)}) async-start(), calls=%async_computation.20 | async-start | bytes 4456448 | tf_op jit(solution)/shard_map/all_gather | solution.py:211
  294.0 352.6 %all-reduce.30.cloned.1.call-start = ((), (), s32[]{:S(2)}) async-start(), calls=%async_computation.43 | async-start | bytes 8388608 | tf_op jit(solution)/shard_map/psum | solution.py:38
  298.7 76.6 %copy-start.38 = (bf16[2,256,8,64]{1,3,2,0:T(8,128)(2,1)}, bf16[2,256,8,64]{1,3,2,0:T(8,128)(2,1)S(1)}, u32[]{:S(2)}) copy-start(bf16[2,256,8,64]{1,3,2,0:T(8,128)(2,1)S(1)} %copy.214) | copy-start | bytes 1572868
  457.0 189.6 %copy-start.8 = (f32[2,256,1024]{2,1,0:T(8,128)}, f32[2,256,1024]{2,1,0:T(8,128)S(1)}, u32[]{:S(2)}) copy-start(f32[2,256,1024]{2,1,0:T(8,128)S(1)} %get-tuple-element.144) | copy-start | bytes 6291460
  457.0 93.5 %copy-start.97 = (f32[1,2,2,128]{3,1,2,0:T(2,128)}, f32[1,2,2,128]{3,1,2,0:T(2,128)S(1)}, u32[]{:S(2)}) copy-start(f32[1,2,2,128]{3,1,2,0:T(2,128)S(1)} %copy.297) | copy-start | bytes 6148
  457.4 93.1 %copy-start.111 = (f32[1,2,2,128]{3,1,2,0:T(2,128)}, f32[1,2,2,128]{3,1,2,0:T(2,128)S(1)}, u32[]{:S(2)}) copy-start(f32[1,2,2,128]{3,1,2,0:T(2,128)S(1)} %copy.298) | copy-start | bytes 6148
  457.4 93.1 %copy-start.99 = (f32[512]{0:T(512)}, f32[512]{0:T(512)S(1)}, u32[]{:S(2)}) copy-start(f32[512]{0:T(512)S(1)} %rsqrt.69) | copy-start | bytes 6148
  619.3 99.0 %all-gather.33.cloned.1.call-start = ((), (), s32[]{:S(2)}) async-start(), calls=%async_computation.21 | async-start | bytes 3342336 | tf_op jit(solution)/shard_map/all_gather | solution.py:215
  620.0 187.0 %all-gather.35.cloned.1.call-start = ((), (), s32[]{:S(2)}) async-start(), calls=%async_computation.22 | async-start | bytes 5242880 | tf_op jit(solution)/shard_map/all_gather | solution.py:65
  727.2 120.3 %all-reduce.18.cloned.1.call-start = ((), (), s32[]{:S(2)}) async-start(), calls=%async_computation.23 | async-start | bytes 4194304 | tf_op jit(solution)/shard_map/psum | solution.py:38
  729.5 77.5 %copy-start.44 = (pred[2,256,1024]{2,1,0:T(8,128)(4,1)S(1)}, pred[2,256,1024]{2,1,0:T(8,128)(4,1)}, u32[]{:S(2)}) copy-start(pred[2,256,1024]{2,1,0:T(8,128)(4,1)} %copy-done.43) | copy-start | bytes 1572868
  828.0 99.6 %all-gather.37.cloned.1.call-start = ((), (), s32[]{:S(2)}) async-start(), calls=%async_computation.24 | async-start | bytes 4456448 | tf_op jit(solution)/shard_map/all_gather | solution.py:217
  828.6 176.6 %all-gather.39.cloned.1.call-start = ((), (), s32[]{:S(2)}) async-start(), calls=%async_computation.25 | async-start | bytes 4456448 | tf_op jit(solution)/shard_map/all_gather | solution.py:218
  829.2 216.5 %all-reduce.20.cloned.1.call-start = ((), (), s32[]{:S(2)}) async-start(), calls=%async_computation.26 | async-start | bytes 4194304 | tf_op jit(solution)/shard_map/psum | solution.py:42
  1025.7 149.4 %reduce-scatter.21.cloned.1.call-start = ((), (), s32[]{:S(2)}) async-start(), calls=%async_computation.27 | async-start | bytes 5242880 | tf_op jit(solution)/shard_map/reduce_scatter | solution.py:101
  1096.9 118.7 %all-reduce.22.cloned.1.call-start = ((), (), s32[]{:S(2)}) async-start(), calls=%async_computation.28 | async-start | bytes 8388608 | tf_op jit(solution)/shard_map/psum | solution.py:42
  1186.6 65.5 %all-reduce.24.cloned.1.call-start = ((), (), s32[]{:S(2)}) async-start(), calls=%async_computation.29 | async-start | bytes 4194304 | tf_op jit(solution)/shard_map/psum | solution.py:42
  1229.5 152.2 %reduce-scatter.25.cloned.1.call-start = ((), (), s32[]{:S(2)}) async-start(), calls=%async_computation.31 | async-start | bytes 5242880 | tf_op jit(solution)/shard_map/reduce_scatter | solution.py:101
  1303.6 157.7 %reduce-scatter.23.cloned.1.call-start = ((), (), s32[]{:S(2)}) async-start(), calls=%async_computation.30 | async-start | bytes 5242880 | tf_op jit(solution)/shard_map/reduce_scatter | solution.py:101
  1346.6 173.5 %all-reduce.28.cloned.1.call-start = ((), (), s32[]{:S(2)}) async-start(), calls=%async_computation.42 | async-start | bytes 12582912 | tf_op jit(solution)/shard_map/psum | solution.py:38
  1364.2 105.3 %copy-start.53 = (bf16[64,8,2,256]{3,1,2,0:T(8,128)(2,1)}, bf16[64,8,2,256]{3,1,2,0:T(8,128)(2,1)S(1)}, u32[]{:S(2)}) copy-start(bf16[64,8,2,256]{3,1,2,0:T(8,128)(2,1)S(1)} %copy.307) | copy-start | bytes 1572868
  1367.5 105.4 %copy-start.55 = (bf16[64,8,2,256]{3,1,2,0:T(8,128)(2,1)}, bf16[64,8,2,256]{3,1,2,0:T(8,128)(2,1)S(1)}, u32[]{:S(2)}) copy-start(bf16[64,8,2,256]{3,1,2,0:T(8,128)(2,1)S(1)} %copy.303) | copy-start | bytes 1572868
  1384.9 83.3 %copy-start.63 = (bf16[2,512,512]{1,2,0:T(8,128)(2,1)}, bf16[2,512,512]{1,2,0:T(8,128)(2,1)S(1)}, u32[]{:S(2)}) copy-start(bf16[2,512,512]{1,2,0:T(8,128)(2,1)S(1)} %reshape.723) | copy-start | bytes 3145732
  1475.0 132.1 %reduce-scatter.37.cloned.1.call-start = ((), (), s32[]{:S(2)}) async-start(), calls=%async_computation.37 | async-start | bytes 557056
  1527.9 153.5 %reduce-scatter.39.cloned.1.call-start = ((), (), s32[]{:S(2)}) async-start(), calls=%async_computation.38 | async-start | bytes 557056
  1529.1 228.0 %reduce-scatter.41.cloned.1.call-start = ((), (), s32[]{:S(2)}) async-start(), calls=%async_computation.39 | async-start | bytes 557056
  1530.2 302.5 %reduce-scatter.43.cloned.1.call-start = ((), (), s32[]{:S(2)}) async-start(), calls=%async_computation.40 | async-start | bytes 557056
  1531.4 1065.5 %all-reduce.26.cloned.1.call-start = ((), (), s32[]{:S(2)}) async-start(), calls=%async_computation.41 | async-start | bytes 58720256
  1557.3 1223.9 %reduce-scatter.35.cloned.1.call-start = ((), (), s32[]{:S(2)}) async-start(), calls=%async_computation.36 | async-start | bytes 8912896 | tf_op jit(solution)/shard_map/reduce_scatter | solution.py:291
  1565.8 1398.1 %reduce-scatter.33.cloned.1.call-start = ((), (), s32[]{:S(2)}) async-start(), calls=%async_computation.35 | async-start | bytes 8912896 | tf_op jit(solution)/shard_map/reduce_scatter | solution.py:290
  1574.2 1474.4 %reduce-scatter.27.cloned.1.call-start = ((), (), s32[]{:S(2)}) async-start(), calls=%async_computation.32 | async-start | bytes 2228224 | tf_op jit(solution)/shard_map/reduce_scatter | solution.py:282
  1578.6 1651.8 %reduce-scatter.31.cloned.1.call-start = ((), (), s32[]{:S(2)}) async-start(), calls=%async_computation.34 | async-start | bytes 8912896 | tf_op jit(solution)/shard_map/reduce_scatter | solution.py:284
  1586.6 1826.5 %reduce-scatter.29.cloned.1.call-start = ((), (), s32[]{:S(2)}) async-start(), calls=%async_computation.33 | async-start | bytes 8912896 | tf_op jit(solution)/shard_map/reduce_scatter | solution.py:283
  (117 other events, 1189.9 us)
Sparse Core Ops, SparseCore 0:
  10.8 70.4 all-gather.22
  84.1 67.5 all-gather.16
  153.8 79.1 all-gather.24
  235.6 53.5 all-gather.26
  291.2 79.3 all-gather.18
  373.2 58.8 all-gather.20
  435.0 19.7 all-reduce.15
  458.0 77.0 all-gather.28
  538.2 74.4 all-gather.30
  619.4 27.1 all-reduce.29
  649.4 68.8 all-gather.32
  727.3 79.6 all-gather.34
  828.1 19.3 all-reduce.17
  850.5 77.0 all-gather.36
  930.6 74.4 all-gather.38
  1025.8 19.8 all-reduce.19
  1097.1 77.9 reduce-scatter.20
  1186.7 28.9 all-reduce.21
  1229.6 22.3 all-reduce.23
  1303.7 77.9 reduce-scatter.24
  1384.0 77.2 reduce-scatter.22
  1475.1 32.7 all-reduce.27
  1528.1 77.6 reduce-scatter.36
  1608.0 73.3 reduce-scatter.38
  1683.6 73.3 reduce-scatter.40
  1759.2 73.4 reduce-scatter.42
  1839.0 757.8 all-reduce.25
  2599.8 181.3 reduce-scatter.34
  2784.0 179.8 reduce-scatter.32
  2966.6 81.9 reduce-scatter.26
  3051.5 178.8 reduce-scatter.30
  3233.2 179.8 reduce-scatter.28
where the time goes:
time: 3430 us; the launch traced here: 3420 us
  waiting for transfers between devices  2690 us (78%)
  matrix products  266 us (8%)
  blocking collectives  161 us (5%)
  other arithmetic  141 us (4%)
  local copies, waits for them, and re-layouts  141 us (4%)
    unnamed x37, waiting for transfers between devices  990 us
    reduce_scatter x1, waiting for transfers between devices, per_device(): lax.psum_scatter(enc_up_term, ('dp', 'seq'), scatter_dimension=0, tiled=T...  183 us
    reduce_scatter x1, waiting for transfers between devices, per_device(): lax.psum_scatter(dec_up_term, ('dp', 'seq'), scatter_dimension=0, tiled=T...  183 us
    all_gather x3, waiting for transfers between devices, attn_forward(): gathered = lax.all_gather(pair, 'seq', axis=2, tiled=True)  182 us
    reduce_scatter x1, waiting for transfers between devices, per_device(): lax.psum_scatter(enc_down_term, ('dp', 'seq'), scatter_dimension=1, tiled...  182 us
    reduce_scatter x1, waiting for transfers between devices, per_device(): lax.psum_scatter(dec_down_term, ('dp', 'seq'), scatter_dimension=1, tiled...  177 us
    reduce_scatter x3, waiting for transfers between devices, attn_backward(): lax.psum_scatter(jnp.stack([key_part, value_part]).astype(jnp.bfloat16),...  157 us
    reduce_scatter x1, waiting for transfers between devices, per_device(): lax.psum_scatter(enc_out_term, ('dp', 'seq'), scatter_dimension=1, tiled=...  84.7 us
  transfers between devices with their start and end apart: 32, of which 28 were waited for; matrix products, arithmetic and copies ran while one was open for 9% of the time, Pallas kernels for 0%

commit v1 on v0

v1 whole, which is shorter than its diff:
```python
import jax
import jax.numpy as jnp
from jax import lax
from jax.experimental import pallas as pl
from jax.experimental.pallas import tpu as pltpu
from jax.sharding import PartitionSpec as P

HEAD = 64
NSEG = 8
LANGS = 4
LANES = 128
F32 = jnp.float32
LOW = jnp.bfloat16


def matmul(left, right):
    return jnp.dot(left, right, preferred_element_type=F32)


def inner_rows(left, right):
    return lax.dot_general(left, right, (((0,), (0,)), ((), ())), preferred_element_type=F32)


def outer_cols(left, right):
    return lax.dot_general(left, right, (((1,), (1,)), ((), ())), preferred_element_type=F32)


def xor_perm(size, bits):
    return [(i, i ^ bits) for i in range(size)]


def swap(value, axis, bits):
    return lax.ppermute(value, axis, xor_perm(lax.axis_size(axis), bits))


def pick(value, index, axis=0):
    return lax.dynamic_index_in_dim(value, index, axis, keepdims=False)


def place(blocks, order):
    count, (rows, cols) = len(blocks), blocks[0].shape
    each = len(order) // count
    size = rows // each

    def body(order_ref, *refs):
        sources, out = refs[:count], refs[count]
        held, in_sems, out_sems = refs[count + 1 :]
        loads = [pltpu.make_async_copy(sources[j], held.at[j], in_sems.at[j]) for j in range(count)]
        stores = []
        for load in loads:
            load.start()
        for j in range(count):
            loads[j].wait()
            for i in range(each):
                spot = order_ref[j * each + i]
                start = pl.multiple_of(spot * size, size)
                stores.append(
                    pltpu.make_async_copy(
                        held.at[j, pl.ds(i * size, size)],
                        out.at[pl.ds(start, size)],
                        out_sems.at[j * each + i],
                    )
                )
                stores[-1].start()
        for store in stores:
            store.wait()

    return pl.pallas_call(
        body,
        out_shape=jax.ShapeDtypeStruct((count * rows, cols), blocks[0].dtype),
        in_specs=[pl.BlockSpec(memory_space=pltpu.SMEM)]
        + [pl.BlockSpec(memory_space=pl.ANY)] * count,
        out_specs=pl.BlockSpec(memory_space=pl.ANY),
        scratch_shapes=[
            pltpu.VMEM((count, rows, cols), blocks[0].dtype),
            pltpu.SemaphoreType.DMA((count,)),
            pltpu.SemaphoreType.DMA((len(order),)),
        ],
        compiler_params=pltpu.CompilerParams(vmem_limit_bytes=16 << 20),
        cost_estimate=pl.CostEstimate(
            flops=0, bytes_accessed=4 * count * rows * cols, transcendentals=0
        ),
    )(jnp.stack(order).astype(jnp.int32), *blocks)


def gather_weight(shard, first):
    here, spot = lax.axis_index("seq"), lax.axis_index("dp")
    n_dp, n_seq = lax.axis_size("dp"), lax.axis_size("seq")
    column = jnp.concatenate([shard] + [swap(shard, "seq", k) for k in range(1, n_seq)], axis=0)
    order = [here ^ k for k in range(n_seq)]
    if n_dp != 4:
        column = place([column], order)
        return lax.all_gather(column, "dp", axis=0, tiled=True)
    second = 3 - first
    near = swap(column, "dp", first)
    side = swap(column, "dp", second)
    far = swap(near, "dp", second)
    order = [(spot ^ j) * n_seq + i for j in (0, first, second, 3) for i in order]
    return place([column, near, side, far], order)


def scatter_grad(grad, first):
    here, spot = lax.axis_index("seq"), lax.axis_index("dp")
    n_dp, n_seq = lax.axis_size("dp"), lax.axis_size("seq")
    total, cols = grad.shape
    if n_dp != 4:
        column = lax.psum_scatter(grad, "dp", scatter_dimension=0, tiled=True).astype(F32)
        column = column.reshape(n_seq, -1, cols)
    else:
        axis = 0 if first == 2 else 1
        mine, other = (spot // 2, spot % 2) if first == 2 else (spot % 2, spot // 2)
        four = grad.reshape(2, 2, total // 4, cols)
        came = swap(pick(four, 1 - mine, axis), "dp", first)
        half = pick(four, mine, axis).astype(F32) + came.astype(F32)
        came = swap(pick(half, 1 - other).astype(LOW), "dp", 3 - first)
        column = pick(half, other) + came.astype(F32)
        column = column.reshape(n_seq, -1, cols)
    result = pick(column, here)
    for k in range(1, n_seq):
        result = result + swap(pick(column, here ^ k).astype(LOW), "seq", k).astype(F32)
    return result


def trade_half(value):
    core = lax.axis_index("mp")
    size = value.shape[0] // 2
    part = lax.dynamic_slice_in_dim(value, core * size, size, 0)
    part = swap(part, "seq", 2)
    rest = swap(part, "mp", 1)
    return jnp.where(
        core == 0, jnp.concatenate([part, rest], axis=0), jnp.concatenate([rest, part], axis=0)
    )


def to_pair(value):
    row = lax.axis_index("seq") // 2
    return jnp.concatenate([pick(value, row), trade_half(pick(value, 1 - row))], axis=0)


def from_pair(value):
    size = value.shape[0] // 2
    kept = value[:size]
    came = trade_half(value[size:].astype(LOW)).astype(value.dtype)
    row = lax.axis_index("seq") // 2
    return jnp.where(row == 0, jnp.stack([kept, came]), jnp.stack([came, kept]))


def core_total(part):
    low = lax.optimization_barrier(part.astype(LOW))
    return low.astype(F32) + swap(low, "mp", 1).astype(F32)


def norm_parts(values):
    center = values - jnp.mean(values, axis=-1, keepdims=True)
    scale = lax.rsqrt(jnp.mean(center * center, axis=-1, keepdims=True) + 1e-05)
    return center * scale, scale


def layer_norm(values, gain, bias):
    return (norm_parts(values)[0] * gain + bias).astype(LOW)


def norm_backward(values, gain, grad):
    unit, scale = norm_parts(values)
    gain_grad = jnp.sum(grad * unit, axis=0)
    bias_grad = jnp.sum(grad, axis=0)
    inner = grad * gain
    inner = inner - jnp.mean(inner, axis=-1, keepdims=True) - unit * jnp.mean(
        inner * unit, axis=-1, keepdims=True
    )
    return inner * scale, gain_grad, bias_grad


def heads(value):
    return value.reshape(value.shape[0], -1, HEAD)


def score_table(query, keys, mask):
    scores = jnp.einsum("qhe,khe->hqk", heads(query), heads(keys), preferred_element_type=F32)
    return jnp.where(mask[None], scores * HEAD ** (-0.5), -1e30)


def attn_forward(inputs, gain, bias, weights, mask, source):
    wkv, wq, wo = weights
    normed = layer_norm(inputs, gain, bias)
    if source is None:
        source = normed
    pair = matmul(source, wkv).astype(LOW)
    peer = swap(pair, "seq", 1)
    query = matmul(normed, wq).astype(LOW)
    full = jnp.concatenate([pair, peer], axis=0)
    width = full.shape[1] // 2
    keys, values = full[:, :width], full[:, width:]
    scores = score_table(query, keys, mask)
    top = jnp.max(scores, axis=-1, keepdims=True)
    expd = jnp.exp(scores - top)
    total = jnp.sum(expd, axis=-1, keepdims=True)
    probs = (expd / total).astype(LOW)
    context = jnp.einsum("hqk,khe->qhe", probs, heads(values), preferred_element_type=F32)
    context = context.astype(LOW).reshape(query.shape)
    branch = core_total(outer_cols(context, wo))
    saved = (inputs, normed, source, query, keys, values, top + jnp.log(total), context)
    return inputs + branch, saved


def attn_backward(grad, saved, gain, weights, mask, cross):
    wkv, wq, wo = weights
    inputs, normed, source, query, keys, values, logsum, context = saved
    size = grad.shape[0]
    low = grad.astype(LOW)
    out_grad = inner_rows(low, context).astype(LOW)
    ctx_grad = matmul(low, wo).astype(LOW)
    probs = jnp.exp(score_table(query, keys, mask) - logsum)
    value_part = jnp.einsum(
        "hqk,qhe->khe", probs.astype(LOW), heads(ctx_grad), preferred_element_type=F32
    )
    prob_grad = jnp.einsum("qhe,khe->hqk", heads(ctx_grad), heads(values), preferred_element_type=F32)
    delta = jnp.sum(prob_grad * probs, axis=-1, keepdims=True)
    score_grad = (probs * (prob_grad - delta)).astype(LOW)
    key_part = jnp.einsum("hqk,qhe->khe", score_grad, heads(query), preferred_element_type=F32)
    key_part = key_part * HEAD ** (-0.5)
    parts = jnp.concatenate(
        [key_part.reshape(keys.shape), value_part.reshape(values.shape)], axis=1
    )
    came = swap(parts[size:].astype(LOW), "seq", 1)
    query_low = jnp.einsum("hqk,khe->qhe", score_grad, heads(keys), preferred_element_type=F32)
    query_low = (query_low * HEAD ** (-0.5)).astype(LOW).reshape(query.shape)
    query_w_grad = inner_rows(normed, query_low).astype(LOW)
    pair_low = (parts[:size] + came.astype(F32)).astype(LOW)
    pair_w_grad = inner_rows(source, pair_low).astype(LOW)
    normed_part = outer_cols(query_low, wq)
    source_part = outer_cols(pair_low, wkv)
    if cross:
        normed_grad = core_total(normed_part)
        source_grad = core_total(source_part)
    else:
        normed_grad = core_total(normed_part + source_part)
        source_grad = None
    flat_grad, gain_grad, bias_grad = norm_backward(inputs, gain, normed_grad)
    side = jnp.concatenate([query_w_grad, out_grad], axis=1)
    return grad + flat_grad, source_grad, (gain_grad, bias_grad, pair_w_grad, side)


def ffn_forward(inputs, gain, bias, weights):
    up, down = weights
    normed = layer_norm(inputs, gain, bias)
    pre = matmul(normed, up)
    act = jax.nn.gelu(pre, approximate=False).astype(LOW)
    branch = core_total(outer_cols(act, down))
    return inputs + branch, (inputs, normed, pre, act)


def ffn_backward(grad, saved, gain, weights):
    up, down = weights
    inputs, normed, pre, act = saved
    low = grad.astype(LOW)
    _, pull = jax.vjp(lambda v: jax.nn.gelu(v, approximate=False), pre)
    (pre_grad,) = pull(matmul(low, down))
    pre_low = pre_grad.astype(LOW)
    normed_grad = core_total(outer_cols(pre_low, up))
    down_grad = inner_rows(low, act).astype(LOW)
    up_grad = inner_rows(normed, pre_low).astype(LOW)
    flat_grad, gain_grad, bias_grad = norm_backward(inputs, gain, normed_grad)
    return grad + flat_grad, (gain_grad, bias_grad, up_grad, down_grad)


def token_tables(lengths, groups, full_len, quarter):
    here, row = lax.axis_index("seq"), lax.axis_index("seq") // 2
    rows = lengths.shape[0]
    onehot = (groups[:, :, None] == jnp.arange(LANGS, dtype=jnp.int32)).astype(F32)
    counts = lax.psum(jnp.sum(onehot * lengths[:, :, None].astype(F32), axis=(0, 1)), "dp")
    all_tokens = rows * lax.axis_size("dp") * full_len
    seg_weight = all_tokens / (LANGS * jnp.sum(onehot * counts, axis=2))
    ends = pick(jnp.cumsum(lengths, axis=1), row)
    steps = jnp.arange(quarter, dtype=jnp.int32)
    places = jnp.concatenate([(here ^ k) * quarter + steps for k in (0, 2, 1, 3)])
    segs = jnp.sum((ends[None, :] <= places[:, None]).astype(jnp.int32), axis=1)
    mine = 2 * quarter
    same = segs[:mine, None] == segs[None, :]
    causal = same & (places[None, :] <= places[:mine, None])
    match = (segs[:mine, None] == jnp.arange(NSEG, dtype=jnp.int32)).astype(F32)
    tok_weight = jnp.sum(match * pick(seg_weight, row)[None, :], axis=1)
    return same, causal, tok_weight, all_tokens


def attn_shards(qkv, out):
    d, width = qkv.shape[1:]
    pair = jnp.concatenate([qkv[1], qkv[2]], axis=1)
    side = jnp.concatenate([qkv[0], out.T], axis=1)
    return pair, side


def split_side(side):
    width = side.shape[1] // 2
    return side[:, :width], side[:, width:]


def qkv_out(pair, side):
    width = side.shape[1] // 2
    qkv = jnp.stack([side[:, :width], pair[:, :width], pair[:, width : 2 * width]])
    return qkv, side[:, width:].T


def per_device(
    src,
    tgt,
    cotangent,
    lengths,
    groups,
    enc_gains,
    enc_biases,
    enc_qkv,
    enc_out,
    enc_up,
    enc_down,
    dec_gains,
    dec_biases,
    dec_self_qkv,
    dec_cross_qkv,
    dec_outs,
    dec_up,
    dec_down,
):
    rows, quarter, width = src.shape
    full_len = quarter * lax.axis_size("seq")
    n_enc, n_dec = enc_gains.shape[0], dec_gains.shape[0]

    norms = jnp.concatenate([enc_gains, enc_biases, dec_gains, dec_biases], axis=0)
    norm_cols = jnp.pad(norms.T, ((0, 0), (0, LANES - norms.shape[0])))
    pair, side = attn_shards(enc_qkv, enc_out)
    pair = jnp.concatenate([pair, norm_cols], axis=1)
    wide = pair.shape[1] - LANES
    e_pair_all = gather_weight(pair, 1)
    e_side = gather_weight(side, 2)
    e_pair = e_pair_all[:, :wide]
    table = e_pair_all[:, wide : wide + norms.shape[0]].T.astype(F32)
    e_gain, e_bias = table[:n_enc], table[n_enc : 2 * n_enc]
    d_gain, d_bias = table[2 * n_enc : 2 * n_enc + n_dec], table[2 * n_enc + n_dec :]
    pair, side = attn_shards(dec_self_qkv, dec_outs[0])
    s_pair, s_side = gather_weight(pair, 1), gather_weight(side, 2)
    e_up, e_down = gather_weight(enc_up, 1), gather_weight(enc_down.T, 2)
    pair, side = attn_shards(dec_cross_qkv, dec_outs[1])
    c_pair, c_side = gather_weight(pair, 1), gather_weight(side, 2)
    d_up, d_down = gather_weight(dec_up, 1), gather_weight(dec_down.T, 2)
    enc_w = (e_pair, *split_side(e_side))
    self_w = (s_pair, *split_side(s_side))
    cross_w = (c_pair, *split_side(c_side))

    same, causal, tok_weight, all_tokens = token_tables(lengths, groups, full_len, quarter)

    x_src = to_pair(src).astype(F32)
    x_tgt = to_pair(tgt).astype(F32)
    out_grad = to_pair(cotangent).astype(F32) * tok_weight[:, None]
    enc_mid, saved_one = attn_forward(x_src, e_gain[0], e_bias[0], enc_w, same, None)
    dec_mid, saved_three = attn_forward(x_tgt, d_gain[0], d_bias[0], self_w, causal, None)
    memory, saved_two = ffn_forward(enc_mid, e_gain[1], e_bias[1], (e_up, e_down))
    dec_cross, saved_four = attn_forward(
        dec_mid, d_gain[1], d_bias[1], cross_w, same, memory.astype(LOW)
    )
    decoded, saved_five = ffn_forward(dec_cross, d_gain[2], d_bias[2], (d_up, d_down))
    decoded = from_pair(decoded.astype(LOW))

    cross_in, fifth = ffn_backward(out_grad, saved_five, d_gain[2], (d_up, d_down))
    d_up_g, d_down_g = scatter_grad(fifth[2], 2), scatter_grad(fifth[3], 1)
    mid_in, memory_grad, fourth = attn_backward(
        cross_in, saved_four, d_gain[1], cross_w, same, True
    )
    c_pair_g, c_side_g = scatter_grad(fourth[2], 2), scatter_grad(fourth[3], 1)
    mid_grad, second = ffn_backward(memory_grad, saved_two, e_gain[1], (e_up, e_down))
    e_up_g, e_down_g = scatter_grad(second[2], 2), scatter_grad(second[3], 1)
    tgt_grad, _, third = attn_backward(mid_in, saved_three, d_gain[0], self_w, causal, False)
    s_pair_g, s_side_g = scatter_grad(third[2], 2), scatter_grad(third[3], 1)
    src_grad, _, first = attn_backward(mid_grad, saved_one, e_gain[0], enc_w, same, False)
    norm_grads = jnp.stack(
        [first[0], second[0], first[1], second[1]]
        + [third[0], fourth[0], fifth[0], third[1], fourth[1], fifth[1]]
    ).astype(LOW)
    norm_grads = jnp.pad(norm_grads.T, ((0, 0), (0, LANES - norm_grads.shape[0])))
    pair = jnp.concatenate([first[2], norm_grads], axis=1)
    e_pair_g, e_side_g = scatter_grad(pair, 2), scatter_grad(first[3], 1)

    factor = 1.0 / all_tokens
    norm_out = e_pair_g[:, wide : wide + norms.shape[0]].T * factor
    enc_qkv_g, enc_out_g = qkv_out(e_pair_g * factor, e_side_g * factor)
    self_qkv_g, self_out_g = qkv_out(s_pair_g * factor, s_side_g * factor)
    cross_qkv_g, cross_out_g = qkv_out(c_pair_g * factor, c_side_g * factor)
    return (
        decoded,
        from_pair(src_grad),
        from_pair(tgt_grad),
        from_pair(memory_grad),
        norm_out[:n_enc],
        norm_out[n_enc : 2 * n_enc],
        enc_qkv_g,
        enc_out_g,
        e_up_g * factor,
        (e_down_g * factor).T,
        norm_out[2 * n_enc : 2 * n_enc + n_dec],
        norm_out[2 * n_enc + n_dec :],
        self_qkv_g,
        cross_qkv_g,
        jnp.stack([self_out_g, cross_out_g]),
        d_up_g * factor,
        (d_down_g * factor).T,
    )


def solution(mesh):
    placed = (
        P("dp", "seq", None),
        P("dp", "seq", None),
        P("dp", "seq", None),
        P("dp", None),
        P("dp", None),
        P(None, ("dp", "seq")),
        P(None, ("dp", "seq")),
        P(None, ("dp", "seq"), "mp"),
        P("mp", ("dp", "seq")),
        P(("dp", "seq"), "mp"),
        P("mp", ("dp", "seq")),
        P(None, ("dp", "seq")),
        P(None, ("dp", "seq")),
        P(None, ("dp", "seq"), "mp"),
        P(None, ("dp", "seq"), "mp"),
        P(None, "mp", ("dp", "seq")),
        P(("dp", "seq"), "mp"),
        P("mp", ("dp", "seq")),
    )
    return jax.shard_map(
        per_device,
        mesh=mesh,
        in_specs=placed,
        out_specs=(
            P("dp", "seq", None),
            P("dp", "seq", None),
            P("dp", "seq", None),
            P("dp", "seq", None),
            P(None, ("dp", "seq")),
            P(None, ("dp", "seq")),
            P(None, ("dp", "seq"), "mp"),
            P("mp", ("dp", "seq")),
            P(("dp", "seq"), "mp"),
            P("mp", ("dp", "seq")),
            P(None, ("dp", "seq")),
            P(None, ("dp", "seq")),
            P(None, ("dp", "seq"), "mp"),
            P(None, ("dp", "seq"), "mp"),
            P(None, "mp", ("dp", "seq")),
            P(("dp", "seq"), "mp"),
            P("mp", ("dp", "seq")),
        ),
        check_vma=False,
    )
```

time: 3430 us -> 1220 us (0.36)
  waiting for transfers between devices: 2690 us -> 457 us
  starting transfers between devices: 3.13 us -> 168 us
  blocking collectives: 161 us -> 9.88 us
  matrix products: 266 us -> 195 us
    unnamed x37 -> x0, waiting for transfers between devices: 990 us -> none
    reduce_scatter x8 -> x0, waiting for transfers between devices: 966 us -> none  [the longest x1 183 us: per_device(): lax.psum_scatter(enc_up_term, ('dp', 'seq'), scatter_dimension=0, tiled=T...]
    all_gather x12 -> x0, waiting for transfers between devices: 616 us -> none  [the longest x3 182 us: attn_forward(): gathered = lax.all_gather(pair, 'seq', axis=2, tiled=True)]
    ppermute x0 -> x141, waiting for transfers between devices: none -> 457 us  [swap(): return lax.ppermute(value, axis, xor_perm(lax.axis_size(axis), bits))]
    ppermute x0 -> x141, starting transfers between devices: none -> 168 us  [swap(): return lax.ppermute(value, axis, xor_perm(lax.axis_size(axis), bits))]
    all_gather x4 -> x0, blocking collectives: 151 us -> none  [the longest x1 42.4 us: per_device(): lax.all_gather(enc_gains, ('dp', 'seq'), axis=1, tiled=True)]
    psum x7 -> x0, waiting for transfers between devices: 118 us -> none  [the longest x3 65.1 us: feature_total(): return lax.psum(partial_value, 'mp')]
    mul x4 -> x1, local copies, waits for them, and re-layouts: 36.9 us -> 0.01 us  [token_tables(): tok_weight = jnp.sum(match * pick(seg_weight, row)[None, :], axis=1)]
  transfers between devices with their start and end apart: 32 -> 141, of which waited for: 28 -> 49; matrix products, arithmetic and copies ran while one was open for 9% -> 39% of each run, Pallas kernels for 0% -> 3%
where the time goes in v1:
time: 1220 us; the launch traced here: 1200 us
  waiting for transfers between devices  457 us (37%)
  matrix products  195 us (16%)
  local copies, waits for them, and re-layouts  170 us (14%)
  starting transfers between devices  168 us (14%)
  other arithmetic  164 us (13%)
  Pallas kernels  32.8 us (3%)
    ppermute x141, waiting for transfers between devices, swap(): return lax.ppermute(value, axis, xor_perm(lax.axis_size(axis), bits))  457 us
    ppermute x141, starting transfers between devices, swap(): return lax.ppermute(value, axis, xor_perm(lax.axis_size(axis), bits))  168 us
    unnamed x441, local copies, waits for them, and re-layouts  71.5 us
    dot_general x13, matrix products, matmul(): return jnp.dot(left, right, preferred_element_type=F32)  49.5 us
    convert_element_type x3, other arithmetic, attn_backward(): score_grad = (probs * (prob_grad - delta)).astype(LOW)  39.7 us
    dot_general x3, matrix products, attn_backward(): jnp.einsum('qhe,khe->hqk', heads(ctx_grad), heads(values), preferred_elem...  35 us
    pallas_call x10, Pallas kernels, place(): pl.pallas_call(body, out_shape=jax.ShapeDtypeStruct((count * rows, cols),...  32.8 us
    dynamic_slice x4, local copies, waits for them, and re-layouts, pick(): return lax.dynamic_index_in_dim(value, index, axis, keepdims=False)  25.7 us
  transfers between devices with their start and end apart: 141, of which 49 were waited for; matrix products, arithmetic and copies ran while one was open for 39% of the time, Pallas kernels for 3%

profile of v1, /device:TPU:0, one launch (start us, length us, event | category | flops | bytes accessed | tf_op | source)
XLA Modules:
  0.0 1201.5 jit_solution(15427216835245547761)
XLA Ops:
  18.2 9.9 psum.7
  50.7 8.4 collective-permute-done.16
  75.6 5.9 collective-permute-done.53
  81.5 7.0 collective-permute-start.40
  89.2 9.3 collective-permute-done.3
  103.0 33.3 %collective-permute-done.39 = bf16[64,2048]{1,0:T(8,128)(2,1)S(1)} collective-permute-done((bf16[64,2048]{1,0:T(8,128)(2,1)S(1)}, bf16[64,2048]{1,0:T(8,128)(2,1)S(1)}, u32[]{:S(2)}, u32[]{:S(2)}) %collective-permute-start.39) | collective-permute-done | bytes 262176 | tf_op jit(solution)/shard_map/ppermute | solution.py:33
  139.6 19.3 %collective-permute-done.22 = bf16[128,1024]{1,0:T(8,128)(2,1)S(1)} collective-permute-done((bf16[128,1024]{1,0:T(8,128)(2,1)S(1)}, bf16[128,1024]{1,0:T(8,128)(2,1)S(1)}, u32[]{:S(2)}, u32[]{:S(2)}) %collective-permute-start.22) | collective-permute-done | bytes 262176 | tf_op jit(solution)/shard_map/ppermute | solution.py:33
  165.5 10.3 collective-permute-done.5.refs_1_
  177.1 9.6 collective-permute-done.11.refs_1_
  190.6 18.0 %collective-permute-done.13.refs_3_ = bf16[256,1024]{1,0:T(8,128)(2,1)S(1)} collective-permute-done((bf16[256,1024]{1,0:T(8,128)(2,1)S(1)}, bf16[256,1024]{1,0:T(8,128)(2,1)S(1)}, u32[]{:S(2)}, u32[]{:S(2)}) %collective-permute-start.13) | collective-permute-done | bytes 524320 | tf_op jit(solution)/shard_map/ppermute | solution.py:33
  224.2 6.9 collective-permute-done.28.refs_1_
  234.8 21.3 %collective-permute-done.20.refs_3_ = bf16[256,1024]{1,0:T(8,128)(2,1)S(1)} collective-permute-done((bf16[256,1024]{1,0:T(8,128)(2,1)S(1)}, bf16[256,1024]{1,0:T(8,128)(2,1)S(1)}, u32[]{:S(2)}, u32[]{:S(2)}) %collective-permute-start.20) | collective-permute-done | bytes 524320 | tf_op jit(solution)/shard_map/ppermute | solution.py:33
  258.6 17.4 %collective-permute-done.41.refs_1_ = bf16[256,2048]{1,0:T(8,128)(2,1)S(1)} collective-permute-done((bf16[256,2048]{1,0:T(8,128)(2,1)S(1)}, bf16[256,2048]{1,0:T(8,128)(2,1)S(1)}, u32[]{:S(2)}, u32[]{:S(2)}) %collective-permute-start.41) | collective-permute-done | bytes 1048608 | tf_op jit(solution)/shard_map/ppermute | solution.py:33
  301.1 6.8 collective-permute-done.43.refs_3_
  317.0 18.9 %collective-permute-done.24 = bf16[512,1024]{1,0:T(8,128)(2,1)} collective-permute-done((bf16[512,1024]{1,0:T(8,128)(2,1)}, bf16[512,1024]{1,0:T(8,128)(2,1)}, u32[]{:S(2)}, u32[]{:S(2)}) %collective-permute-start.24) | collective-permute-done | bytes 1048608 | tf_op jit(solution)/shard_map/ppermute | solution.py:33
  359.9 7.6 fusion.225
  368.8 7.9 fusion
  380.3 12.9 %multiply_convert_fusion.4 = (bf16[512,2048]{1,0:T(8,128)(2,1)S(1)}, f32[512,2048]{1,0:T(8,128)}, f32[512,2048]{1,0:T(8,128)}) fusion(bf16[1024,2048]{1,0:T(8,128)(2,1)S(1)} %copy-done.8, f32[512,1024]{1,0:T(8,128)S(1)} %get-tuple-element.126, f32[1024]{0:T(1024)S(1)} %get-tuple-element.109, f32[1024]{0:T(1024)S(1)} %get-tuple-element.110, ...), kind=kOutput, calls=%fused_computation.64 | convolution fusion | flops 2218262528 | bytes 16789504 | tf_op jit(solution)/shard_map/dot_general | solution.py:17
  404.1 7.3 collective-permute-done.55.refs_1_
  415.7 8.2 collective-permute-done.57.refs_3_
  447.9 12.4 %collective-permute-done.62.refs_1_ = bf16[256,2048]{1,0:T(8,128)(2,1)} collective-permute-done((bf16[256,2048]{1,0:T(8,128)(2,1)}, bf16[256,2048]{1,0:T(8,128)(2,1)}, u32[]{:S(2)}, u32[]{:S(2)}) %collective-permute-start.62) | collective-permute-done | bytes 1048608 | tf_op jit(solution)/shard_map/ppermute | solution.py:33
  460.3 17.9 %collective-permute-done.68.refs_1_ = bf16[256,2048]{1,0:T(8,128)(2,1)} collective-permute-done((bf16[256,2048]{1,0:T(8,128)(2,1)S(1)}, bf16[256,2048]{1,0:T(8,128)(2,1)}, u32[]{:S(2)}, u32[]{:S(2)}) %collective-permute-start.68) | collective-permute-done | bytes 1048608 | tf_op jit(solution)/shard_map/ppermute | solution.py:33
  515.3 11.0 multiply_convert_fusion.3
  559.8 11.0 multiply_reduce_fusion.2
  570.9 11.8 multiply_convert_fusion.2
  594.5 7.8 collective-permute-done.72
  614.8 5.9 collective-permute-done.77
  634.7 11.1 multiply_reduce_fusion
  645.8 12.1 %multiply_convert_fusion = bf16[8,512,1024]{2,1,0:T(8,128)(2,1)S(1)} fusion(f32[8,512,1024]{2,1,0:T(8,128)} %get-tuple-element.219, f32[8,512,1024]{2,1,0:T(8,128)} %get-tuple-element.207, f32[8,512]{1,0:T(8,128)S(1)} %get-tuple-element.218, f32[8,512]{1,0:T(8,128)S(1)} %log_add_fusion), kind=kLoop, calls=%fused_computation | loop fusion | flops 16777216 | bytes 41975808 | tf_op jit(solution)/shard_map/convert_element_type | solution.py:219
  668.0 7.5 fusion.6
  684.6 9.8 constant_dynamic-slice_fusion.1
  694.4 5.8 copy.124
  711.9 6.2 copy.122
  739.3 8.4 add_convert_fusion
  774.8 14.6 %collective-permute-done.132 = bf16[256,2048]{1,0:T(8,128)(2,1)S(1)} collective-permute-done((bf16[256,2048]{1,0:T(8,128)(2,1)S(1)}, bf16[256,2048]{1,0:T(8,128)(2,1)S(1)}, u32[]{:S(2)}, u32[]{:S(2)}) %collective-permute-start.132) | collective-permute-done | bytes 1048608 | tf_op jit(solution)/shard_map/ppermute | solution.py:33
  798.9 8.8 collective-permute-done.135
  807.7 16.9 %collective-permute-done.134 = bf16[64,2048]{1,0:T(8,128)(2,1)S(1)} collective-permute-done((bf16[64,2048]{1,0:T(8,128)(2,1)S(1)}, bf16[64,2048]{1,0:T(8,128)(2,1)S(1)}, u32[]{:S(2)}, u32[]{:S(2)}) %collective-permute-start.134) | collective-permute-done | bytes 262176 | tf_op jit(solution)/shard_map/ppermute | solution.py:33
  828.4 18.6 %collective-permute-done.139 = bf16[64,2048]{1,0:T(8,128)(2,1)S(1)} collective-permute-done((bf16[64,2048]{1,0:T(8,128)(2,1)S(1)}, bf16[64,2048]{1,0:T(8,128)(2,1)S(1)}, u32[]{:S(2)}, u32[]{:S(2)}) %collective-permute-start.139) | collective-permute-done | bytes 262176 | tf_op jit(solution)/shard_map/ppermute | solution.py:33
  858.8 15.9 %collective-permute-done.122 = bf16[256,1024]{1,0:T(8,128)(2,1)S(1)} collective-permute-done((bf16[256,1024]{1,0:T(8,128)(2,1)S(1)}, bf16[256,1024]{1,0:T(8,128)(2,1)S(1)}, u32[]{:S(2)}, u32[]{:S(2)}) %collective-permute-start.122) | collective-permute-done | bytes 524320 | tf_op jit(solution)/shard_map/ppermute | solution.py:33
  897.0 6.1 collective-permute-start.130
  910.2 12.9 %multiply_reduce_fusion.1 = (f32[8,512]{1,0:T(8,128)S(1)}, f32[8,512,1024]{2,1,0:T(8,128)}) fusion(f32[8,512,1024]{2,1,0:T(8,128)} %copy-done.23, f32[8,512]{1,0:T(8,128)S(1)} %copy-done.137, bf16[512,8,64]{0,2,1:T(8,128)(2,1)S(1)} %bitcast.522, bf16[1024,8,64]{0,2,1:T(8,128)(2,1)S(1)} %bitcast.527), kind=kOutput, calls=%fused_computation.4 | convolution fusion | flops 549449728 | bytes 35160064 | tf_op jit(solution)/shard_map/qhe,khe->hqk/dot_general | solution.py:217
  923.2 15.7 %multiply_convert_fusion.1 = bf16[8,512,1024]{2,1,0:T(8,128)(2,1)} fusion(f32[8,512,1024]{2,1,0:T(8,128)} %get-tuple-element.217, f32[8,512,1024]{2,1,0:T(8,128)} %copy-done.23, f32[8,512]{1,0:T(8,128)S(1)} %get-tuple-element.216, f32[8,512]{1,0:T(8,128)S(1)} %copy-done.137), kind=kLoop, calls=%fused_computation.3 | loop fusion | flops 16777216 | bytes 41975808 | tf_op jit(solution)/shard_map/convert_element_type | solution.py:219
  970.5 8.7 constant_dynamic-slice_fusion.5
  987.9 5.9 copy.120
  1011.7 55.7 %collective-permute-done.96 = bf16[2,256,1024]{2,1,0:T(8,128)(2,1)S(1)} collective-permute-done((bf16[2,256,1024]{2,1,0:T(8,128)(2,1)}, bf16[2,256,1024]{2,1,0:T(8,128)(2,1)S(1)}, u32[]{:S(2)}, u32[]{:S(2)}) %collective-permute-start.96) | collective-permute-done | bytes 1048608 | tf_op jit(solution)/shard_map/ppermute | solution.py:33
  1075.7 7.2 collective-permute-done.97
  1133.4 10.2 collective-permute-done.108
  1144.4 13.7 %collective-permute-start.103 = (bf16[64,2048]{1,0:T(8,128)(2,1)S(1)}, bf16[64,2048]{1,0:T(8,128)(2,1)S(1)}, u32[]{:S(2)}, u32[]{:S(2)}) collective-permute-start(bf16[64,2048]{1,0:T(8,128)(2,1)S(1)} %get-tuple-element.142), channel_id=1, source_target_pairs={{0,2},{2,0},{4,6},{6,4},{1,3},{3,1},{5,7},{7,5},{8,10},{10,8},{12,... | collective-permute-start | bytes 786440 | tf_op jit(solution)/shard_map/ppermute | solution.py:33
  (974 shorter events, 600.8 us)
Async XLA Ops:
  88.5 47.9 %collective-permute-start.39 = (bf16[64,2048]{1,0:T(8,128)(2,1)S(1)}, bf16[64,2048]{1,0:T(8,128)(2,1)S(1)}, u32[]{:S(2)}, u32[]{:S(2)}) collective-permute-start(bf16[64,2048]{1,0:T(8,128)(2,1)S(1)} %bitcast.587), channel_id=1, source_target_pairs={{0,4},{2,6},{4,0},{6,2},{1,5},{3,7},{5,1},{7,3},{8,12},{10,14},{12... | collective-permute-start | bytes 786440 | tf_op jit(solution)/shard_map/ppermute | solution.py:33
  88.5 47.9 %collective-permute-start.38 = (bf16[64,2048]{1,0:T(8,128)(2,1)S(1)}, bf16[64,2048]{1,0:T(8,128)(2,1)S(1)}, u32[]{:S(2)}, u32[]{:S(2)}) collective-permute-start(bf16[64,2048]{1,0:T(8,128)(2,1)S(1)} %bitcast.588), channel_id=1, source_target_pairs={{0,2},{2,0},{4,6},{6,4},{1,3},{3,1},{5,7},{7,5},{8,10},{10,8},{12,... | collective-permute-start | bytes 786440 | tf_op jit(solution)/shard_map/ppermute | solution.py:33
  98.5 61.1 %collective-permute-start.33 = (bf16[64,2048]{1,0:T(8,128)(2,1)S(1)}, bf16[64,2048]{1,0:T(8,128)(2,1)S(1)}, u32[]{:S(2)}, u32[]{:S(2)}) collective-permute-start(bf16[64,2048]{1,0:T(8,128)(2,1)S(1)} %copy-done.138), channel_id=1, source_target_pairs={{0,4},{2,6},{4,0},{6,2},{1,5},{3,7},{5,1},{7,3},{8,12},{10,14},{12... | collective-permute-start | bytes 786440 | tf_op jit(solution)/shard_map/ppermute | solution.py:33
  98.5 40.9 %collective-permute-start.32 = (bf16[64,2048]{1,0:T(8,128)(2,1)S(1)}, bf16[64,2048]{1,0:T(8,128)(2,1)S(1)}, u32[]{:S(2)}, u32[]{:S(2)}) collective-permute-start(bf16[64,2048]{1,0:T(8,128)(2,1)S(1)} %copy-done.138), channel_id=1, source_target_pairs={{0,2},{2,0},{4,6},{6,4},{1,3},{3,1},{5,7},{7,5},{8,10},{10,8},{12,... | collective-permute-start | bytes 786440 | tf_op jit(solution)/shard_map/ppermute | solution.py:33
  102.0 57.6 %collective-permute-start.34 = (bf16[64,2048]{1,0:T(8,128)(2,1)S(1)}, bf16[64,2048]{1,0:T(8,128)(2,1)S(1)}, u32[]{:S(2)}, u32[]{:S(2)}) collective-permute-start(bf16[64,2048]{1,0:T(8,128)(2,1)S(1)} %copy-done.138), channel_id=1, source_target_pairs={{0,6},{2,4},{4,2},{6,0},{1,7},{3,5},{5,3},{7,1},{8,14},{10,12},{12... | collective-permute-start | bytes 786440 | tf_op jit(solution)/shard_map/ppermute | solution.py:33
  136.4 51.9 %collective-permute-start.60 = (bf16[64,2048]{1,0:T(8,128)(2,1)}, bf16[64,2048]{1,0:T(8,128)(2,1)S(1)}, u32[]{:S(2)}, u32[]{:S(2)}) collective-permute-start(bf16[64,2048]{1,0:T(8,128)(2,1)} %param.34), channel_id=1, source_target_pairs={{0,4},{2,6},{4,0},{6,2},{1,5},{3,7},{5,1},{7,3},{8,12},{10,14},{12... | collective-permute-start | bytes 786440 | tf_op jit(solution)/shard_map/ppermute | solution.py:33
  217.1 58.9 %collective-permute-start.36 = (bf16[256,2048]{1,0:T(8,128)(2,1)S(1)}, bf16[256,2048]{1,0:T(8,128)(2,1)S(1)}, u32[]{:S(2)}, u32[]{:S(2)}) collective-permute-start(bf16[256,2048]{1,0:T(8,128)(2,1)S(1)} %constant_dynamic-update-slice_fusion.refs_0_), channel_id=1, source_target_pairs={{0,16},{8,24},{16,0},{24,8},{1,17},{9,25},{17,1},{25,9},{2,18},{10... | collective-permute-start | bytes 3145736 | tf_op jit(solution)/shard_map/ppermute | solution.py:33
  218.8 39.4 %collective-permute-start.35 = (bf16[256,2048]{1,0:T(8,128)(2,1)S(1)}, bf16[256,2048]{1,0:T(8,128)(2,1)S(1)}, u32[]{:S(2)}, u32[]{:S(2)}) collective-permute-start(bf16[256,2048]{1,0:T(8,128)(2,1)S(1)} %constant_dynamic-update-slice_fusion.refs_0_), channel_id=1, source_target_pairs={{0,8},{8,0},{16,24},{24,16},{1,9},{9,1},{17,25},{25,17},{2,10},{10... | collective-permute-start | bytes 3145736 | tf_op jit(solution)/shard_map/ppermute | solution.py:33
  220.8 55.2 %collective-permute-start.41 = (bf16[256,2048]{1,0:T(8,128)(2,1)S(1)}, bf16[256,2048]{1,0:T(8,128)(2,1)S(1)}, u32[]{:S(2)}, u32[]{:S(2)}) collective-permute-start(bf16[256,2048]{1,0:T(8,128)(2,1)S(1)} %pad_maximum_fusion.11.refs_0_), channel_id=1, source_target_pairs={{0,16},{8,24},{16,0},{24,8},{1,17},{9,25},{17,1},{25,9},{2,18},{10... | collective-permute-start | bytes 3145736 | tf_op jit(solution)/shard_map/ppermute | solution.py:33
  231.1 44.9 %collective-permute-start.30 = (bf16[256,1024]{1,0:T(8,128)(2,1)S(1)}, bf16[256,1024]{1,0:T(8,128)(2,1)S(1)}, u32[]{:S(2)}, u32[]{:S(2)}) collective-permute-start(bf16[256,1024]{1,0:T(8,128)(2,1)S(1)} %collective-permute-done.28.refs_1_), channel_id=1, source_target_pairs={{0,8},{8,0},{16,24},{24,16},{1,9},{9,1},{17,25},{25,17},{2,10},{10... | collective-permute-start | bytes 1572872 | tf_op jit(solution)/shard_map/ppermute | solution.py:33
  256.1 45.0 %collective-permute-start.42 = (bf16[256,2048]{1,0:T(8,128)(2,1)S(1)}, bf16[256,2048]{1,0:T(8,128)(2,1)S(1)}, u32[]{:S(2)}, u32[]{:S(2)}) collective-permute-start(bf16[256,2048]{1,0:T(8,128)(2,1)S(1)} %pad_maximum_fusion.11.refs_0_), channel_id=1, source_target_pairs={{0,8},{8,0},{16,24},{24,16},{1,9},{9,1},{17,25},{25,17},{2,10},{10... | collective-permute-start | bytes 3145736 | tf_op jit(solution)/shard_map/ppermute | solution.py:33
  258.1 37.9 %collective-permute-start.37 = (bf16[256,2048]{1,0:T(8,128)(2,1)S(1)}, bf16[256,2048]{1,0:T(8,128)(2,1)S(1)}, u32[]{:S(2)}, u32[]{:S(2)}) collective-permute-start(bf16[256,2048]{1,0:T(8,128)(2,1)S(1)} %collective-permute-done.35.refs_1_), channel_id=1, source_target_pairs={{0,16},{8,24},{16,0},{24,8},{1,17},{9,25},{17,1},{25,9},{2,18},{10... | collective-permute-start | bytes 3145736 | tf_op jit(solution)/shard_map/ppermute | solution.py:33
  276.0 59.9 %collective-permute-start.24 = (bf16[512,1024]{1,0:T(8,128)(2,1)}, bf16[512,1024]{1,0:T(8,128)(2,1)}, u32[]{:S(2)}, u32[]{:S(2)}) collective-permute-start(bf16[512,1024]{1,0:T(8,128)(2,1)} %fusion.92), channel_id=1, source_target_pairs={{0,2},{2,0},{4,6},{6,4},{1,3},{3,1},{5,7},{7,5},{8,10},{10,8},{12,... | collective-permute-start | bytes 3145736 | tf_op jit(solution)/shard_map/ppermute | solution.py:33
  296.1 100.5 %collective-permute-start.67 = (bf16[64,2048]{1,0:T(8,128)(2,1)}, bf16[64,2048]{1,0:T(8,128)(2,1)}, u32[]{:S(2)}, u32[]{:S(2)}) collective-permute-start(bf16[64,2048]{1,0:T(8,128)(2,1)} %bitcast.53), channel_id=1, source_target_pairs={{0,6},{2,4},{4,2},{6,0},{1,7},{3,5},{5,3},{7,1},{8,14},{10,12},{12... | collective-permute-start | bytes 786440 | tf_op jit(solution)/shard_map/ppermute | solution.py:33
  301.1 95.6 %collective-permute-start.66 = (bf16[64,2048]{1,0:T(8,128)(2,1)}, bf16[64,2048]{1,0:T(8,128)(2,1)}, u32[]{:S(2)}, u32[]{:S(2)}) collective-permute-start(bf16[64,2048]{1,0:T(8,128)(2,1)} %bitcast.53), channel_id=1, source_target_pairs={{0,4},{2,6},{4,0},{6,2},{1,5},{3,7},{5,1},{7,3},{8,12},{10,14},{12... | collective-permute-start | bytes 786440 | tf_op jit(solution)/shard_map/ppermute | solution.py:33
  307.9 90.3 %collective-permute-start.65 = (bf16[64,2048]{1,0:T(8,128)(2,1)}, bf16[64,2048]{1,0:T(8,128)(2,1)}, u32[]{:S(2)}, u32[]{:S(2)}) collective-permute-start(bf16[64,2048]{1,0:T(8,128)(2,1)} %bitcast.53), channel_id=1, source_target_pairs={{0,2},{2,0},{4,6},{6,4},{1,3},{3,1},{5,7},{7,5},{8,10},{10,8},{12,... | collective-permute-start | bytes 786440 | tf_op jit(solution)/shard_map/ppermute | solution.py:33
  311.3 90.8 %collective-permute-start.61 = (bf16[64,2048]{1,0:T(8,128)(2,1)}, bf16[64,2048]{1,0:T(8,128)(2,1)S(1)}, u32[]{:S(2)}, u32[]{:S(2)}) collective-permute-start(bf16[64,2048]{1,0:T(8,128)(2,1)} %param.34), channel_id=1, source_target_pairs={{0,6},{2,4},{4,2},{6,0},{1,7},{3,5},{5,3},{7,1},{8,14},{10,12},{12... | collective-permute-start | bytes 786440 | tf_op jit(solution)/shard_map/ppermute | solution.py:33
  398.1 42.1 %collective-permute-start.44 = (bf16[512,1024]{1,0:T(8,128)(2,1)}, bf16[512,1024]{1,0:T(8,128)(2,1)}, u32[]{:S(2)}, u32[]{:S(2)}) collective-permute-start(bf16[512,1024]{1,0:T(8,128)(2,1)} %convolution_convert_fusion.23), channel_id=1, source_target_pairs={{0,1},{1,0},{2,3},{3,2},{4,5},{5,4},{6,7},{7,6},{8,9},{9,8},{10,11... | collective-permute-start | bytes 3145736 | tf_op jit(solution)/shard_map/ppermute | solution.py:33
  428.6 77.3 %collective-permute-start.63 = (bf16[256,2048]{1,0:T(8,128)(2,1)}, bf16[256,2048]{1,0:T(8,128)(2,1)}, u32[]{:S(2)}, u32[]{:S(2)}) collective-permute-start(bf16[256,2048]{1,0:T(8,128)(2,1)} %constant_dynamic-update-slice_fusion.4.refs_0_), channel_id=1, source_target_pairs={{0,16},{8,24},{16,0},{24,8},{1,17},{9,25},{17,1},{25,9},{2,18},{10... | collective-permute-start | bytes 3145736 | tf_op jit(solution)/shard_map/ppermute | solution.py:33
  440.2 38.0 %collective-permute-start.68 = (bf16[256,2048]{1,0:T(8,128)(2,1)S(1)}, bf16[256,2048]{1,0:T(8,128)(2,1)}, u32[]{:S(2)}, u32[]{:S(2)}) collective-permute-start(bf16[256,2048]{1,0:T(8,128)(2,1)S(1)} %pad_maximum_fusion.12.refs_0_), channel_id=1, source_target_pairs={{0,16},{8,24},{16,0},{24,8},{1,17},{9,25},{17,1},{25,9},{2,18},{10... | collective-permute-start | bytes 3145736 | tf_op jit(solution)/shard_map/ppermute | solution.py:33
  447.3 61.7 %collective-permute-start.69 = (bf16[256,2048]{1,0:T(8,128)(2,1)S(1)}, bf16[256,2048]{1,0:T(8,128)(2,1)}, u32[]{:S(2)}, u32[]{:S(2)}) collective-permute-start(bf16[256,2048]{1,0:T(8,128)(2,1)S(1)} %pad_maximum_fusion.12.refs_0_), channel_id=1, source_target_pairs={{0,8},{8,0},{16,24},{24,16},{1,9},{9,1},{17,25},{25,17},{2,10},{10... | collective-permute-start | bytes 3145736 | tf_op jit(solution)/shard_map/ppermute | solution.py:33
  460.3 42.9 %collective-permute-start.75 = (bf16[128,1024]{1,0:T(8,128)(2,1)S(1)}, bf16[128,1024]{1,0:T(8,128)(2,1)}, u32[]{:S(2)}, u32[]{:S(2)}) collective-permute-start(bf16[128,1024]{1,0:T(8,128)(2,1)S(1)} %collective-permute-done.74), channel_id=1, source_target_pairs={{0,1},{1,0},{2,3},{3,2},{4,5},{5,4},{6,7},{7,6},{8,9},{9,8},{10,11... | collective-permute-start | bytes 786440 | tf_op jit(solution)/shard_map/ppermute | solution.py:33
  541.4 181.3 %collective-permute-start.131 = (bf16[2,256,2048]{2,1,0:T(8,128)(2,1)}, bf16[2,256,2048]{2,1,0:T(8,128)(2,1)}, u32[]{:S(2)}, u32[]{:S(2)}) collective-permute-start(bf16[2,256,2048]{2,1,0:T(8,128)(2,1)} %dynamic-slice_bitcast_fusion.1), channel_id=1, source_target_pairs={{0,16},{8,24},{16,0},{24,8},{1,17},{9,25},{17,1},{25,9},{2,18},{10... | collective-permute-start | bytes 6291464 | tf_op jit(solution)/shard_map/ppermute | solution.py:33
  549.1 169.1 %collective-permute-start.136 = (bf16[2,256,2048]{2,1,0:T(8,128)(2,1)}, bf16[2,256,2048]{2,1,0:T(8,128)(2,1)}, u32[]{:S(2)}, u32[]{:S(2)}) collective-permute-start(bf16[2,256,2048]{2,1,0:T(8,128)(2,1)} %dynamic-slice_bitcast_fusion), channel_id=1, source_target_pairs={{0,8},{8,0},{16,24},{24,16},{1,9},{9,1},{17,25},{25,17},{2,10},{10... | collective-permute-start | bytes 6291464 | tf_op jit(solution)/shard_map/ppermute | solution.py:33
  633.2 93.2 %collective-permute-start.126 = (bf16[2,256,1024]{2,1,0:T(8,128)(2,1)}, bf16[2,256,1024]{2,1,0:T(8,128)(2,1)}, u32[]{:S(2)}, u32[]{:S(2)}) collective-permute-start(bf16[2,256,1024]{2,1,0:T(8,128)(2,1)} %dynamic-slice_bitcast_fusion.4), channel_id=1, source_target_pairs={{0,16},{8,24},{16,0},{24,8},{1,17},{9,25},{17,1},{25,9},{2,18},{10... | collective-permute-start | bytes 3145736 | tf_op jit(solution)/shard_map/ppermute | solution.py:33
  633.5 101.8 %collective-permute-start.78 = (bf16[512,1024]{1,0:T(8,128)(2,1)}, bf16[512,1024]{1,0:T(8,128)(2,1)}, u32[]{:S(2)}, u32[]{:S(2)}) collective-permute-start(bf16[512,1024]{1,0:T(8,128)(2,1)} %convolution_convert_fusion.7), channel_id=1, source_target_pairs={{0,1},{1,0},{2,3},{3,2},{4,5},{5,4},{6,7},{7,6},{8,9},{9,8},{10,11... | collective-permute-start | bytes 3145736 | tf_op jit(solution)/shard_map/ppermute | solution.py:33
  682.9 47.5 %collective-permute-start.85 = (bf16[512,1024]{0,1:T(8,128)(2,1)}, bf16[512,1024]{0,1:T(8,128)(2,1)}, u32[]{:S(2)}, u32[]{:S(2)}) collective-permute-start(bf16[512,1024]{0,1:T(8,128)(2,1)} %fusion.69), channel_id=1, source_target_pairs={{0,2},{2,0},{4,6},{6,4},{1,3},{3,1},{5,7},{7,5},{8,10},{10,8},{12,... | collective-permute-start | bytes 3145736 | tf_op jit(solution)/shard_map/ppermute | solution.py:33
  718.1 37.4 %collective-permute-start.111 = (bf16[2,256,1024]{2,1,0:T(8,128)(2,1)}, bf16[2,256,1024]{2,1,0:T(8,128)(2,1)}, u32[]{:S(2)}, u32[]{:S(2)}) collective-permute-start(bf16[2,256,1024]{2,1,0:T(8,128)(2,1)} %bitcast.569), channel_id=1, source_target_pairs={{0,8},{8,0},{16,24},{24,16},{1,9},{9,1},{17,25},{25,17},{2,10},{10... | collective-permute-start | bytes 3145736 | tf_op jit(solution)/shard_map/ppermute | solution.py:33
  722.8 44.1 %collective-permute-start.121 = (bf16[2,256,1024]{2,1,0:T(8,128)(2,1)S(1)}, bf16[2,256,1024]{2,1,0:T(8,128)(2,1)S(1)}, u32[]{:S(2)}, u32[]{:S(2)}) collective-permute-start(bf16[2,256,1024]{2,1,0:T(8,128)(2,1)S(1)} %bitcast.567), channel_id=1, source_target_pairs={{0,8},{8,0},{16,24},{24,16},{1,9},{9,1},{17,25},{25,17},{2,10},{10... | collective-permute-start | bytes 3145736 | tf_op jit(solution)/shard_map/ppermute | solution.py:33
  726.4 63.0 %collective-permute-start.132 = (bf16[256,2048]{1,0:T(8,128)(2,1)S(1)}, bf16[256,2048]{1,0:T(8,128)(2,1)S(1)}, u32[]{:S(2)}, u32[]{:S(2)}) collective-permute-start(bf16[256,2048]{1,0:T(8,128)(2,1)S(1)} %fusion.103), channel_id=1, source_target_pairs={{0,8},{8,0},{16,24},{24,16},{1,9},{9,1},{17,25},{25,17},{2,10},{10... | collective-permute-start | bytes 3145736 | tf_op jit(solution)/shard_map/ppermute | solution.py:33
  730.4 64.4 %collective-permute-start.137 = (bf16[256,2048]{1,0:T(8,128)(2,1)S(1)}, bf16[256,2048]{1,0:T(8,128)(2,1)S(1)}, u32[]{:S(2)}, u32[]{:S(2)}) collective-permute-start(bf16[256,2048]{1,0:T(8,128)(2,1)S(1)} %fusion.104), channel_id=1, source_target_pairs={{0,16},{8,24},{16,0},{24,8},{1,17},{9,25},{17,1},{25,9},{2,18},{10... | collective-permute-start | bytes 3145736 | tf_op jit(solution)/shard_map/ppermute | solution.py:33
  735.3 119.6 %collective-permute-start.127 = (bf16[256,1024]{1,0:T(8,128)(2,1)}, bf16[256,1024]{1,0:T(8,128)(2,1)}, u32[]{:S(2)}, u32[]{:S(2)}) collective-permute-start(bf16[256,1024]{1,0:T(8,128)(2,1)} %fusion.125), channel_id=1, source_target_pairs={{0,8},{8,0},{16,24},{24,16},{1,9},{9,1},{17,25},{25,17},{2,10},{10... | collective-permute-start | bytes 1572872 | tf_op jit(solution)/shard_map/ppermute | solution.py:33
  757.5 94.1 %collective-permute-start.112 = (bf16[256,1024]{1,0:T(8,128)(2,1)S(1)}, bf16[256,1024]{1,0:T(8,128)(2,1)S(1)}, u32[]{:S(2)}, u32[]{:S(2)}) collective-permute-start(bf16[256,1024]{1,0:T(8,128)(2,1)S(1)} %fusion.122), channel_id=1, source_target_pairs={{0,16},{8,24},{16,0},{24,8},{1,17},{9,25},{17,1},{25,9},{2,18},{10... | collective-permute-start | bytes 1572872 | tf_op jit(solution)/shard_map/ppermute | solution.py:33
  828.4 75.5 %collective-permute-start.79 = (bf16[512,1024]{1,0:T(8,128)(2,1)S(1)}, bf16[512,1024]{1,0:T(8,128)(2,1)S(1)}, u32[]{:S(2)}, u32[]{:S(2)}) collective-permute-start(bf16[512,1024]{1,0:T(8,128)(2,1)S(1)} %convolution_convert_fusion.20), channel_id=1, source_target_pairs={{0,1},{1,0},{2,3},{3,2},{4,5},{5,4},{6,7},{7,6},{8,9},{9,8},{10,11... | collective-permute-start | bytes 3145736 | tf_op jit(solution)/shard_map/ppermute | solution.py:33
  847.1 104.9 %collective-permute-start.116 = (bf16[2,256,1024]{2,1,0:T(8,128)(2,1)}, bf16[2,256,1024]{2,1,0:T(8,128)(2,1)}, u32[]{:S(2)}, u32[]{:S(2)}) collective-permute-start(bf16[2,256,1024]{2,1,0:T(8,128)(2,1)} %dynamic-slice_bitcast_fusion.5), channel_id=1, source_target_pairs={{0,16},{8,24},{16,0},{24,8},{1,17},{9,25},{17,1},{25,9},{2,18},{10... | collective-permute-start | bytes 3145736 | tf_op jit(solution)/shard_map/ppermute | solution.py:33
  889.2 71.2 %collective-permute-start.86 = (bf16[512,1024]{1,0:T(8,128)(2,1)S(1)}, bf16[512,1024]{1,0:T(8,128)(2,1)}, u32[]{:S(2)}, u32[]{:S(2)}) collective-permute-start(bf16[512,1024]{1,0:T(8,128)(2,1)S(1)} %add_convert_fusion.2), channel_id=1, source_target_pairs={{0,1},{1,0},{2,3},{3,2},{4,5},{5,4},{6,7},{7,6},{8,9},{9,8},{10,11... | collective-permute-start | bytes 3145736 | tf_op jit(solution)/shard_map/ppermute | solution.py:33
  891.9 91.2 %collective-permute-start.128 = (bf16[64,1024]{1,0:T(8,128)(2,1)}, bf16[64,1024]{1,0:T(8,128)(2,1)}, u32[]{:S(2)}, u32[]{:S(2)}) collective-permute-start(bf16[64,1024]{1,0:T(8,128)(2,1)} %get-tuple-element.163), channel_id=1, source_target_pairs={{0,2},{2,0},{4,6},{6,4},{1,3},{3,1},{5,7},{7,5},{8,10},{10,8},{12,... | collective-permute-start | bytes 393224 | tf_op jit(solution)/shard_map/ppermute | solution.py:33
  897.0 89.0 %collective-permute-start.130 = (bf16[64,1024]{1,0:T(8,128)(2,1)}, bf16[64,1024]{1,0:T(8,128)(2,1)}, u32[]{:S(2)}, u32[]{:S(2)}) collective-permute-start(bf16[64,1024]{1,0:T(8,128)(2,1)} %get-tuple-element.164), channel_id=1, source_target_pairs={{0,6},{2,4},{4,2},{6,0},{1,7},{3,5},{5,3},{7,1},{8,14},{10,12},{12... | collective-permute-start | bytes 393224 | tf_op jit(solution)/shard_map/ppermute | solution.py:33
  904.0 98.1 %collective-permute-start.129 = (bf16[64,1024]{1,0:T(8,128)(2,1)S(1)}, bf16[64,1024]{1,0:T(8,128)(2,1)}, u32[]{:S(2)}, u32[]{:S(2)}) collective-permute-start(bf16[64,1024]{1,0:T(8,128)(2,1)S(1)} %get-tuple-element.165), channel_id=1, source_target_pairs={{0,4},{2,6},{4,0},{6,2},{1,5},{3,7},{5,1},{7,3},{8,12},{10,14},{12... | collective-permute-start | bytes 393224 | tf_op jit(solution)/shard_map/ppermute | solution.py:33
  952.0 55.5 %collective-permute-start.80 = (bf16[512,1024]{0,1:T(8,128)(2,1)}, bf16[512,1024]{0,1:T(8,128)(2,1)}, u32[]{:S(2)}, u32[]{:S(2)}) collective-permute-start(bf16[512,1024]{0,1:T(8,128)(2,1)} %fusion.70), channel_id=1, source_target_pairs={{0,2},{2,0},{4,6},{6,4},{1,3},{3,1},{5,7},{7,5},{8,10},{10,8},{12,... | collective-permute-start | bytes 3145736 | tf_op jit(solution)/shard_map/ppermute | solution.py:33
  1002.0 68.9 %collective-permute-start.106 = (bf16[2,256,2048]{2,1,0:T(8,128)(2,1)}, bf16[2,256,2048]{2,1,0:T(8,128)(2,1)S(1)}, u32[]{:S(2)}, u32[]{:S(2)}) collective-permute-start(bf16[2,256,2048]{2,1,0:T(8,128)(2,1)} %dynamic-slice_bitcast_fusion.2), channel_id=1, source_target_pairs={{0,8},{8,0},{16,24},{24,16},{1,9},{9,1},{17,25},{25,17},{2,10},{10... | collective-permute-start | bytes 6291464 | tf_op jit(solution)/shard_map/ppermute | solution.py:33
  1004.0 70.8 %collective-permute-start.101 = (bf16[2,256,2048]{2,1,0:T(8,128)(2,1)}, bf16[2,256,2048]{2,1,0:T(8,128)(2,1)S(1)}, u32[]{:S(2)}, u32[]{:S(2)}) collective-permute-start(bf16[2,256,2048]{2,1,0:T(8,128)(2,1)} %dynamic-slice_bitcast_fusion.3), channel_id=1, source_target_pairs={{0,16},{8,24},{16,0},{24,8},{1,17},{9,25},{17,1},{25,9},{2,18},{10... | collective-permute-start | bytes 6291464 | tf_op jit(solution)/shard_map/ppermute | solution.py:33
  1004.2 63.2 %collective-permute-start.96 = (bf16[2,256,1024]{2,1,0:T(8,128)(2,1)}, bf16[2,256,1024]{2,1,0:T(8,128)(2,1)S(1)}, u32[]{:S(2)}, u32[]{:S(2)}) collective-permute-start(bf16[2,256,1024]{2,1,0:T(8,128)(2,1)} %bitcast.568), channel_id=1, source_target_pairs={{0,8},{8,0},{16,24},{24,16},{1,9},{9,1},{17,25},{25,17},{2,10},{10... | collective-permute-start | bytes 3145736 | tf_op jit(solution)/shard_map/ppermute | solution.py:33
  1011.7 83.6 %collective-permute-start.81 = (bf16[512,1024]{1,0:T(8,128)(2,1)S(1)}, bf16[512,1024]{1,0:T(8,128)(2,1)S(1)}, u32[]{:S(2)}, u32[]{:S(2)}) collective-permute-start(bf16[512,1024]{1,0:T(8,128)(2,1)S(1)} %add_convert_fusion.3), channel_id=1, source_target_pairs={{0,1},{1,0},{2,3},{3,2},{4,5},{5,4},{6,7},{7,6},{8,9},{9,8},{10,11... | collective-permute-start | bytes 3145736 | tf_op jit(solution)/shard_map/ppermute | solution.py:33
  1073.0 52.8 %collective-permute-start.107 = (bf16[256,2048]{1,0:T(8,128)(2,1)}, bf16[256,2048]{1,0:T(8,128)(2,1)}, u32[]{:S(2)}, u32[]{:S(2)}) collective-permute-start(bf16[256,2048]{1,0:T(8,128)(2,1)} %fusion.102), channel_id=1, source_target_pairs={{0,16},{8,24},{16,0},{24,8},{1,17},{9,25},{17,1},{25,9},{2,18},{10... | collective-permute-start | bytes 3145736 | tf_op jit(solution)/shard_map/ppermute | solution.py:33
  1088.2 43.5 %collective-permute-start.102 = (bf16[256,2048]{1,0:T(8,128)(2,1)}, bf16[256,2048]{1,0:T(8,128)(2,1)}, u32[]{:S(2)}, u32[]{:S(2)}) collective-permute-start(bf16[256,2048]{1,0:T(8,128)(2,1)} %fusion.101), channel_id=1, source_target_pairs={{0,8},{8,0},{16,24},{24,16},{1,9},{9,1},{17,25},{25,17},{2,10},{10... | collective-permute-start | bytes 3145736 | tf_op jit(solution)/shard_map/ppermute | solution.py:33
  1117.2 49.0 %collective-permute-start.82 = (bf16[128,1024]{1,0:T(8,128)(2,1)}, bf16[128,1024]{1,0:T(8,128)(2,1)}, u32[]{:S(2)}, u32[]{:S(2)}) collective-permute-start(bf16[128,1024]{1,0:T(8,128)(2,1)} %dynamic-slice_convert_fusion.11), channel_id=1, source_target_pairs={{0,4},{2,6},{4,0},{6,2},{1,5},{3,7},{5,1},{7,3},{8,12},{10,14},{12... | collective-permute-start | bytes 786440 | tf_op jit(solution)/shard_map/ppermute | solution.py:33
  1122.9 45.8 %collective-permute-start.91 = (bf16[2,256,1152]{2,1,0:T(8,128)(2,1)}, bf16[2,256,1152]{2,1,0:T(8,128)(2,1)S(1)}, u32[]{:S(2)}, u32[]{:S(2)}) collective-permute-start(bf16[2,256,1152]{2,1,0:T(8,128)(2,1)} %bitcast.566), channel_id=1, source_target_pairs={{0,16},{8,24},{16,0},{24,8},{1,17},{9,25},{17,1},{25,9},{2,18},{10... | collective-permute-start | bytes 3538952 | tf_op jit(solution)/shard_map/ppermute | solution.py:33
  (305 other events, 6054.9 us)

commit v2 on v1

v2 whole, which is shorter than its diff:
```python
import functools

import jax
import jax.numpy as jnp
from jax import lax
from jax.experimental import pallas as pl
from jax.experimental.pallas import tpu as pltpu
from jax.sharding import PartitionSpec as P

HEAD = 64
NSEG = 8
LANGS = 4
LANES = 128
TILE = 512
F32 = jnp.float32
LOW = jnp.bfloat16
EPS = 1e-05


def dot_nn(left, right):
    return jnp.dot(left, right, preferred_element_type=F32)


def dot_tn(left, right):
    return lax.dot_general(left, right, (((0,), (0,)), ((), ())), preferred_element_type=F32)


def dot_nt(left, right):
    return lax.dot_general(left, right, (((1,), (1,)), ((), ())), preferred_element_type=F32)


def xor_perm(size, bits):
    return [(i, i ^ bits) for i in range(size)]


def swap(value, axis, bits):
    return lax.ppermute(value, axis, xor_perm(lax.axis_size(axis), bits))


def pick(value, index, axis=0):
    return lax.dynamic_index_in_dim(value, index, axis, keepdims=False)


def params(mib):
    return pltpu.CompilerParams(vmem_limit_bytes=mib << 20)


def whole(shape):
    return pl.BlockSpec(shape, lambda *_: (0,) * len(shape))


def shaped(shape, dtype):
    return jax.ShapeDtypeStruct(shape, dtype)


def cost(flops, nbytes, exps=0):
    return pl.CostEstimate(flops=int(flops), bytes_accessed=int(nbytes), transcendentals=int(exps))


class Order:
    def __init__(self):
        self.last = []

    def __call__(self, step, *values):
        leaves, tree = jax.tree.flatten(values)
        spots = [i for i, leaf in enumerate(leaves) if isinstance(leaf, jax.Array)]
        for i, leaf in zip(spots, after([leaves[i] for i in spots], self.last), strict=True):
            leaves[i] = leaf
        out = step(*jax.tree.unflatten(tree, leaves))
        self.last = jax.tree.leaves(out)
        return out


def after(values, others):
    count = len(values)
    return list(lax.optimization_barrier((*values, *others))[:count])


def place(sources, order, cuts):
    flat, where_from = [], []
    for source in sources:
        if isinstance(source, tuple):
            where_from.append([(len(flat), None), (len(flat) + 1, None)])
            flat.extend(source)
        else:
            where_from.append([(len(flat), 0), (len(flat), 1)])
            flat.append(source)
    count = len(sources)
    rows, cols = flat[0].shape[-2:]
    each = order.shape[0] // count
    size = rows // each

    def body(order_ref, *refs):
        inputs = refs[: len(flat)]
        outs = refs[len(flat) : len(flat) + len(cuts)]
        held, in_sems, out_sems = refs[len(flat) + len(cuts) :]
        loads = []
        for j in range(count):
            for half in range(2):
                index, part = where_from[j][half]
                source = inputs[index] if part is None else inputs[index].at[part]
                loads.append(
                    pltpu.make_async_copy(source, held.at[half, j], in_sems.at[2 * j + half])
                )
                loads[-1].start()
        stores = []
        for j in range(count):
            for half in range(2):
                loads[2 * j + half].wait()
                for i in range(each):
                    spot = order_ref[j * each + i]
                    start = pl.multiple_of(spot * size, size)
                    for n, (side, first, width) in enumerate(cuts):
                        if side != half:
                            continue
                        stores.append(
                            pltpu.make_async_copy(
                                held.at[half, j, pl.ds(i * size, size), pl.ds(first, width)],
                                outs[n].at[pl.ds(start, size)],
                                out_sems.at[j * each + i, n],
                            )
                        )
                        stores[-1].start()
        for store in stores:
            store.wait()

    total = count * rows
    return pl.pallas_call(
        body,
        out_shape=[shaped((total, width), LOW) for _, _, width in cuts],
        in_specs=[pl.BlockSpec(memory_space=pltpu.SMEM)]
        + [pl.BlockSpec(memory_space=pl.ANY)] * len(flat),
        out_specs=[pl.BlockSpec(memory_space=pl.ANY)] * len(cuts),
        scratch_shapes=[
            pltpu.VMEM((2, count, rows, cols), LOW),
            pltpu.SemaphoreType.DMA((2 * count,)),
            pltpu.SemaphoreType.DMA((order.shape[0], len(cuts))),
        ],
        compiler_params=params(24),
        cost_estimate=cost(0, 8 * total * cols),
    )(order, *flat)


def seq_steps():
    steps, step = [], lax.axis_size("seq") // 2
    while step:
        steps.append(step)
        step //= 2
    return steps


def seq_order():
    spots = [0]
    for step in seq_steps():
        spots += [spot ^ step for spot in spots]
    return spots


class Gather:
    def __init__(self, shard):
        self.column = shard
        self.steps = seq_steps()

    def along(self, others=()):
        (ready,) = after([self.column], others)
        self.came = swap(ready, "seq", self.steps.pop(0))

    def join(self, order):
        self.column = order(
            lambda one, two: jnp.concatenate([one, two], axis=1), self.column, self.came
        )

    def across(self, others=()):
        self.plain = lax.axis_size("dp") != 4
        self.near = []
        if self.plain:
            return
        (ready,) = after([self.column], others)
        self.near = [swap(ready, "dp", 1), swap(ready, "dp", 2)]

    def far(self, order):
        if self.plain:
            return
        one, two = order(lambda x, y: (x[0], y[1]), *self.near)
        self.last = (swap(one, "dp", 2), swap(two, "dp", 1))

    def place(self, order, cuts):
        if self.plain:
            return order(place_weights, [self.column], cuts)
        return order(place_weights, [self.column, *self.near, self.last], cuts)


def place_weights(sources, cuts):
    here, spot = lax.axis_index("seq"), lax.axis_index("dp")
    spots = jnp.asarray(seq_order(), jnp.int32) ^ here.astype(jnp.int32)
    if lax.axis_size("dp") != 4:
        cols = sources[0].shape[2]
        halves = place(sources, spots, [(0, 0, cols), (1, 0, cols)])
        halves = [lax.all_gather(half, "dp", axis=0, tiled=True) for half in halves]
        return [halves[side][:, first : first + width] for side, first, width in cuts]
    blocks = jnp.arange(4, dtype=jnp.int32) ^ spot.astype(jnp.int32)
    spots = (blocks[:, None] * spots.shape[0] + spots[None, :]).reshape(-1)
    return place(sources, spots, cuts)


def block_order(first):
    if lax.axis_size("dp") != 4:
        return jnp.arange(4, dtype=jnp.int32)
    spot = lax.axis_index("dp").astype(jnp.int32)
    return jnp.asarray([first, 3, 0, 3 - first], jnp.int32) ^ spot


def row_order(first):
    away = jnp.arange(lax.axis_size("seq"), dtype=jnp.int32)
    away = away ^ lax.axis_index("seq").astype(jnp.int32)
    turn, bits = jnp.zeros_like(away), seq_steps()
    for one, two in zip(bits, reversed(bits), strict=True):
        turn = turn + jnp.where((away & one) != 0, two, 0)
    return jnp.concatenate([block_order(first), turn])


def weight_grad(pairs, order):
    tokens, width = pairs[0][0].shape
    size = width // 4
    cols = sum(right.shape[1] for _, right in pairs)
    n_seq = lax.axis_size("seq")
    near = lax.axis_size("dp") == 4
    unit = size // n_seq if near else size

    def body(order_ref, *refs):
        away, stay = refs[2 * len(pairs) :]
        step = pl.program_id(0)
        start = 0
        for j in range(len(pairs)):
            left, right = refs[2 * j], refs[2 * j + 1]
            part = dot_tn(left[...], right[...]).astype(LOW)
            stop = start + part.shape[1]

            def put(out):
                for k in range(size // unit):
                    spot = order_ref[4 + k] if near else k
                    rows = pl.ds(pl.multiple_of(spot * unit, unit), unit)
                    out[rows, start:stop] = part[k * unit : (k + 1) * unit]

            pl.when(step < 2)(functools.partial(put, away))
            pl.when(step >= 2)(functools.partial(put, stay))
            start = stop

    specs, values = [], []
    for left, right in pairs:
        specs.append(pl.BlockSpec((tokens, size), lambda i, order: (0, order[i])))
        specs.append(pl.BlockSpec(right.shape, lambda i, order: (0, 0)))
        values += [left, right]
    return pl.pallas_call(
        body,
        grid_spec=pltpu.PrefetchScalarGridSpec(
            num_scalar_prefetch=1,
            grid=(4,),
            in_specs=specs,
            out_specs=[
                pl.BlockSpec((size, cols), lambda i, order: (jnp.minimum(i, 1), 0)),
                pl.BlockSpec((size, cols), lambda i, order: (jnp.maximum(i - 2, 0), 0)),
            ],
        ),
        out_shape=[shaped((2 * size, cols), LOW)] * 2,
        compiler_params=params(32),
        cost_estimate=cost(2 * tokens * width * cols, 4 * width * cols),
    )(order, *values)


class Scatter:
    def __init__(self, pair, side, factor):
        self.halves, self.factor, self.stage = (pair, side), factor, 0
        self.bits = (2, 1)
        self.plain = lax.axis_size("dp") != 4

    def start(self, j):
        away, _ = self.halves[j]
        return None if self.plain else swap(away, "dp", self.bits[j])

    def begin(self):
        self.came = [self.start(0), self.start(1)]
        return self

    def add(self, order):
        self.stage += 1
        if self.plain:
            if self.stage == 4:
                self.out = self.plain_sum()
            return
        (getattr(self, "add%d" % self.stage))(order)

    def add1(self, order):
        stays = [stay for _, stay in self.halves]

        def step(stays, came):
            size = stays[0].shape[0] // 2
            onward = [
                (stay[size:].astype(F32) + new[size:].astype(F32)).astype(LOW)
                for stay, new in zip(stays, came, strict=True)
            ]
            return onward

        onward = order(step, stays, self.came)
        self.last = [swap(value, "dp", 3 - bit) for value, bit in zip(onward, self.bits, strict=True)]

    def add2(self, order):
        stays = [stay for _, stay in self.halves]

        def step(stays, came, last):
            size = stays[0].shape[0] // 2
            both = jnp.stack(
                [
                    stay[:size].astype(F32) + new[:size].astype(F32) + more.astype(F32)
                    for stay, new, more in zip(stays, came, last, strict=True)
                ]
            )
            size = size // 2
            return both[:, size:].astype(LOW), both[:, :size]

        away, self.kept = order(step, stays, self.came, self.last)
        self.came = swap(away, "seq", 1)

    def add3(self, order):
        def step(kept, came):
            both = kept + came.astype(F32)
            size = both.shape[1] // 2
            return both[:, size:].astype(LOW), both[:, :size]

        away, self.kept = order(step, self.kept, self.came)
        self.came = swap(away, "seq", 2)

    def add4(self, order):
        self.out = order(
            lambda kept, came: (kept + came.astype(F32)) * self.factor, self.kept, self.came
        )

    def plain_sum(self):
        here, n_seq = lax.axis_index("seq"), lax.axis_size("seq")
        columns = []
        for away, stay in self.halves:
            grad = jnp.concatenate([away, stay], axis=0)
            columns.append(
                lax.psum_scatter(grad, "dp", scatter_dimension=0, tiled=True).astype(F32)
            )
        both = jnp.stack(columns)
        both = both.reshape(2, n_seq, -1, both.shape[-1])
        result = pick(both, here, 1)
        for k in range(1, n_seq):
            result = result + swap(pick(both, here ^ k, 1).astype(LOW), "seq", k).astype(F32)
        return result * self.factor


def trade_start(value):
    size = value.shape[0] // 2
    part = lax.dynamic_slice_in_dim(value, lax.axis_index("mp") * size, size, 0)
    return swap(part, "seq", 2)


def trade_end(part):
    rest = swap(part, "mp", 1)
    return jnp.where(
        lax.axis_index("mp") == 0,
        jnp.concatenate([part, rest], axis=0),
        jnp.concatenate([rest, part], axis=0),
    )


def pair_start(value, others):
    row = lax.axis_index("seq") // 2
    (sent,) = after([pick(value, 1 - row)], others)
    return trade_start(sent)


def pair_end(value, part):
    row = lax.axis_index("seq") // 2
    return jnp.concatenate([pick(value, row), trade_end(part)], axis=0)


def back_start(value):
    return trade_start(value[value.shape[0] // 2 :].astype(LOW))


def back_end(value, part):
    kept = value[: value.shape[0] // 2]
    came = trade_end(part).astype(value.dtype)
    row = lax.axis_index("seq") // 2
    return jnp.where(row == 0, jnp.stack([kept, came]), jnp.stack([came, kept]))


def norm_parts(values):
    center = values - jnp.mean(values, axis=-1, keepdims=True)
    scale = lax.rsqrt(jnp.mean(center * center, axis=-1, keepdims=True) + EPS)
    return center * scale, scale


def enter(inputs, parts, norm, weight):
    tokens, width = inputs.shape
    blocks = weight.shape[1] // TILE
    rows = [inputs, *parts] + ([] if norm is None else list(norm))
    keep = len(parts) > 0 and norm is not None

    def body(*refs):
        x_ref, part_refs = refs[0], refs[1 : 1 + len(parts)]
        norm_refs = refs[1 + len(parts) : len(rows)]
        w_ref = refs[len(rows)]
        outs = refs[len(rows) + 1 :]
        low_ref, out_ref = outs[0], outs[1]

        @pl.when(pl.program_id(0) == 0)
        def _():
            x = x_ref[...].astype(F32)
            if part_refs:
                x = x + (part_refs[0][...].astype(F32) + part_refs[1][...].astype(F32))
            if keep:
                outs[2][...] = x
            if norm_refs:
                x = norm_parts(x)[0] * norm_refs[0][...] + norm_refs[1][...]
            low_ref[...] = x.astype(LOW)

        out_ref[0] = dot_nn(low_ref[...], w_ref[...]).astype(LOW)

    result = pl.pallas_call(
        body,
        grid=(blocks,),
        in_specs=[whole(v.shape) for v in rows] + [pl.BlockSpec((width, TILE), lambda j: (0, j))],
        out_specs=[
            whole((tokens, width)),
            pl.BlockSpec((1, tokens, TILE), lambda j: (j, 0, 0)),
        ]
        + ([whole((tokens, width))] if keep else []),
        out_shape=[shaped((tokens, width), LOW), shaped((blocks, tokens, TILE), LOW)]
        + ([shaped((tokens, width), F32)] if keep else []),
        compiler_params=params(32),
        cost_estimate=cost(2 * tokens * width * weight.shape[1], 14 * tokens * width),
    )(*rows, weight)
    return tuple(result)


def attend_body(rows, q_ref, ko_ref, kp_ref, vo_ref, vp_ref, bias_ref, ctx_ref, lse_ref):
    tokens = q_ref.shape[0]
    lane = lax.broadcasted_iota(jnp.int32, (rows, LANES), 1)
    ko, kp, vo, vp = ko_ref[0], kp_ref[0], vo_ref[0], vp_ref[0]
    for r in range(0, tokens, rows):
        q = q_ref[r : r + rows] * jnp.asarray(HEAD**-0.5, LOW)
        ctx = stat = None
        for h in range(LANES // HEAD):
            mine = (lane // HEAD) == h
            qh = jnp.where(mine, q, jnp.zeros_like(q))
            so = dot_nt(qh, ko) + bias_ref[r : r + rows, :tokens]
            sp = dot_nt(qh, kp) + bias_ref[r : r + rows, tokens:]
            top = jnp.maximum(
                jnp.max(so, axis=1, keepdims=True), jnp.max(sp, axis=1, keepdims=True)
            )
            eo, ep = jnp.exp(so - top), jnp.exp(sp - top)
            total = jnp.sum(eo, axis=1, keepdims=True) + jnp.sum(ep, axis=1, keepdims=True)
            acc = dot_nn(eo.astype(LOW), vo) + dot_nn(ep.astype(LOW), vp)
            acc = acc * (1.0 / total)
            lse = jnp.broadcast_to(top + jnp.log(total), (rows, LANES))
            ctx = acc if ctx is None else jnp.where(mine, acc, ctx)
            stat = lse if stat is None else jnp.where(mine, lse, stat)
        ctx_ref[r : r + rows] = ctx.astype(LOW)
        lse_ref[r : r + rows] = stat


def kv_spec(tokens, half):
    return pl.BlockSpec((1, tokens, LANES), lambda i: (half, 0, i))


def attend(query, own, peer, bias):
    tokens, width = query.shape
    spec = pl.BlockSpec((tokens, LANES), lambda i: (0, i))
    return pl.pallas_call(
        functools.partial(attend_body, 256),
        grid=(width // LANES,),
        in_specs=[spec]
        + [kv_spec(tokens, half) for half in (0, 0, 1, 1)]
        + [whole(bias.shape)],
        out_specs=[spec, spec],
        out_shape=[shaped((tokens, width), LOW), shaped((tokens, width), F32)],
        compiler_params=params(40),
        cost_estimate=cost(16 * tokens * tokens * width, 16 * tokens * width, 2 * tokens * tokens * 8),
    )(query, own, peer, own, peer, bias)


def attend_back_body(
    q_ref, ko_ref, kp_ref, vo_ref, vp_ref, g_ref, lse_ref, bias_ref, dq_ref, own_ref, peer_ref, acc
):
    tokens = q_ref.shape[0]
    lane = lax.broadcasted_iota(jnp.int32, (tokens, LANES), 1)
    q = q_ref[...] * jnp.asarray(HEAD**-0.5, LOW)
    g = g_ref[...]
    lse_t = lse_ref[...].T
    parts = ((kp_ref, vp_ref, peer_ref, tokens), (ko_ref, vo_ref, own_ref, 0))
    keys_t = [k_ref[0].T for k_ref, _, _, _ in parts]
    for h in range(LANES // HEAD):
        mine = (lane // HEAD) == h
        qh = jnp.where(mine, q, jnp.zeros_like(q))
        gh = jnp.where(mine, g, jnp.zeros_like(g))
        rows = slice(h * HEAD, (h + 1) * HEAD)
        lse = lse_t[h * HEAD : h * HEAD + 1]
        probs, inner = [], []
        for k_ref, v_ref, _, base in parts:
            scores = dot_nt(k_ref[0], qh) + bias_ref[base : base + tokens]
            probs.append(jnp.exp(scores - lse))
            inner.append(dot_nt(v_ref[0], gh))
        delta = sum(jnp.sum(p * d, axis=0, keepdims=True) for p, d in zip(probs, inner))
        total = None
        for j, (_, _, out_ref, _) in enumerate(parts):
            grads = (probs[j] * (inner[j] - delta)).astype(LOW)
            dv = dot_nn(probs[j].astype(LOW), gh).astype(LOW)
            dk = dot_nn(grads, qh).astype(LOW)
            part = dot_nn(keys_t[j][rows], grads)
            total = part if total is None else total + part
            if h == 0:
                out_ref[0], out_ref[1] = dk, dv
            else:
                out_ref[0] += dk
                out_ref[1] += dv
        acc[rows] = total
    dq_ref[...] = (acc[...].T * HEAD**-0.5).astype(LOW)


def attend_back(query, own, peer, grad, lse, bias_t):
    tokens, width = query.shape
    spec = pl.BlockSpec((tokens, LANES), lambda i: (0, i))
    both = pl.BlockSpec((2, tokens, LANES), lambda i: (0, 0, i))
    return pl.pallas_call(
        attend_back_body,
        grid=(width // LANES,),
        in_specs=[spec]
        + [kv_spec(tokens, half) for half in (0, 0, 1, 1)]
        + [spec, spec, whole(bias_t.shape)],
        out_specs=[spec, both, both],
        out_shape=[shaped((tokens, width), LOW)] + [shaped((2, tokens, width), LOW)] * 2,
        scratch_shapes=[pltpu.VMEM((LANES, tokens), F32)],
        compiler_params=params(40),
        cost_estimate=cost(40 * tokens * tokens * width, 24 * tokens * width, 2 * tokens * tokens * 8),
    )(query, own, peer, own, peer, grad, lse, bias_t)


def attend_leave(dq, own, came, wq, wkv, apart):
    tokens, width = dq.shape[0], wq.shape[0]
    size = tokens // 2

    def body(dq_ref, own_ref, came_ref, wq_ref, wkv_ref, pair_ref, *outs):
        low = [
            (own_ref[j].astype(F32) + came_ref[j].astype(F32)).astype(LOW) for j in range(2)
        ]
        cols = low[0].shape[1]
        for j in range(2):
            pair_ref[:, j * cols : (j + 1) * cols] = low[j]
        first = dot_nt(dq_ref[...], wq_ref[...])
        rest = dot_nt(pair_ref[...], wkv_ref[...])
        if apart:
            outs[0][0] = first.astype(LOW)
            outs[0][1] = rest.astype(LOW)
        else:
            outs[0][...] = (first + rest).astype(LOW)

    part_spec = (
        pl.BlockSpec((2, size, width), lambda i: (0, i, 0))
        if apart
        else pl.BlockSpec((size, width), lambda i: (i, 0))
    )
    cols = own.shape[2]
    return pl.pallas_call(
        body,
        grid=(2,),
        in_specs=[
            pl.BlockSpec((size, cols), lambda i: (i, 0)),
            pl.BlockSpec((2, size, cols), lambda i: (0, i, 0)),
            pl.BlockSpec((2, size, cols), lambda i: (0, i, 0)),
            whole(wq.shape),
            whole(wkv.shape),
        ],
        out_specs=[pl.BlockSpec((size, 2 * cols), lambda i: (i, 0)), part_spec],
        out_shape=[
            shaped((tokens, 2 * cols), LOW),
            shaped((2, tokens, width) if apart else (tokens, width), LOW),
        ],
        compiler_params=params(32),
        cost_estimate=cost(6 * tokens * width * cols, 14 * tokens * cols + 6 * width * cols),
    )(dq, own, came, wq, wkv)


def feed(inputs, parts, norm, up, down):
    tokens, width = inputs.shape
    hidden = up.shape[1]

    def body(x_ref, one_ref, two_ref, gain_ref, bias_ref, up_ref, down_ref, *rest):
        normed_ref, total_ref, act_ref, slope_ref, part_ref, acc = rest
        step = pl.program_id(0)

        @pl.when(step == 0)
        def _():
            x = x_ref[...].astype(F32) + (one_ref[...].astype(F32) + two_ref[...].astype(F32))
            total_ref[...] = x
            normed_ref[...] = (norm_parts(x)[0] * gain_ref[...] + bias_ref[...]).astype(LOW)

        pre = dot_nn(normed_ref[...], up_ref[...])
        below = 0.5 + 0.5 * lax.erf(pre * (0.5**0.5))
        act = (pre * below).astype(LOW)
        act_ref[...] = act
        slope = below + pre * (jnp.exp(pre * pre * -0.5) * 0.3989422804014327)
        slope_ref[...] = slope.astype(LOW)
        part = dot_nt(act, down_ref[...])

        @pl.when(step == 0)
        def _():
            acc[...] = part

        @pl.when(step > 0)
        def _():
            acc[...] += part

        @pl.when(step == pl.num_programs(0) - 1)
        def _():
            part_ref[...] = acc[...].astype(LOW)

    block = pl.BlockSpec((tokens, TILE), lambda j: (0, j))
    weight = pl.BlockSpec((width, TILE), lambda j: (0, j))
    same = whole((tokens, width))
    return pl.pallas_call(
        body,
        grid=(hidden // TILE,),
        in_specs=[same, same, same, whole((1, width)), whole((1, width)), weight, weight],
        out_specs=[same, same, block, block, same],
        out_shape=[
            shaped((tokens, width), LOW),
            shaped((tokens, width), F32),
            shaped((tokens, hidden), LOW),
            shaped((tokens, hidden), LOW),
            shaped((tokens, width), LOW),
        ],
        scratch_shapes=[pltpu.VMEM((tokens, width), F32)],
        compiler_params=params(48),
        cost_estimate=cost(4 * tokens * width * hidden, 8 * width * hidden, 2 * tokens * hidden),
    )(inputs, *parts, *norm, up, down)


def feed_back(low, slope, up, down):
    tokens, width = low.shape
    hidden = up.shape[1]

    def body(low_ref, slope_ref, up_ref, down_ref, pre_ref, part_ref, acc):
        step = pl.program_id(0)
        act_grad = dot_nn(low_ref[...], down_ref[...])
        pre = (act_grad * slope_ref[...].astype(F32)).astype(LOW)
        pre_ref[...] = pre
        part = dot_nt(pre, up_ref[...])

        @pl.when(step == 0)
        def _():
            acc[...] = part

        @pl.when(step > 0)
        def _():
            acc[...] += part

        @pl.when(step == pl.num_programs(0) - 1)
        def _():
            part_ref[...] = acc[...].astype(LOW)

    block = pl.BlockSpec((tokens, TILE), lambda j: (0, j))
    weight = pl.BlockSpec((width, TILE), lambda j: (0, j))
    same = whole((tokens, width))
    return pl.pallas_call(
        body,
        grid=(hidden // TILE,),
        in_specs=[same, block, weight, weight],
        out_specs=[block, same],
        out_shape=[shaped((tokens, hidden), LOW), shaped((tokens, width), LOW)],
        scratch_shapes=[pltpu.VMEM((tokens, width), F32)],
        compiler_params=params(48),
        cost_estimate=cost(4 * tokens * width * hidden, 6 * width * hidden),
    )(low, slope, up, down)


def norm_back(grad, values, parts, gain, weight):
    tokens, width = grad.shape
    size = tokens // 2

    def body(*refs):
        g_ref, x_ref, one_ref, two_ref, gain_ref = refs[:5]
        outs = refs[5:] if weight is None else refs[6:]
        step = pl.program_id(0)
        normed_grad = one_ref[...].astype(F32) + two_ref[...].astype(F32)
        unit, scale = norm_parts(x_ref[...].astype(F32))
        gains = jnp.sum(normed_grad * unit, axis=0, keepdims=True)
        biases = jnp.sum(normed_grad, axis=0, keepdims=True)
        inner = normed_grad * gain_ref[...]
        inner = inner - jnp.mean(inner, axis=-1, keepdims=True) - unit * jnp.mean(
            inner * unit, axis=-1, keepdims=True
        )
        total = g_ref[...] + inner * scale
        outs[0][...] = total

        @pl.when(step == 0)
        def _():
            outs[1][...] = jnp.concatenate([gains, biases], axis=0)

        @pl.when(step > 0)
        def _():
            outs[1][...] += jnp.concatenate([gains, biases], axis=0)

        if weight is not None:
            low = total.astype(LOW)
            outs[2][...] = low
            outs[3][...] = dot_nn(low, refs[5][...]).astype(LOW)

    row = pl.BlockSpec((size, width), lambda i: (i, 0))
    in_specs = [row] * 4 + [whole((1, width))]
    out_specs = [row, whole((2, width))]
    out_shape = [shaped((tokens, width), F32), shaped((2, width), F32)]
    extra = []
    if weight is not None:
        cols = weight.shape[1]
        extra = [weight]
        in_specs.append(whole(weight.shape))
        out_specs += [row, pl.BlockSpec((size, cols), lambda i: (i, 0))]
        out_shape += [shaped((tokens, width), LOW), shaped((tokens, cols), LOW)]
    return pl.pallas_call(
        body,
        grid=(tokens // size,),
        in_specs=in_specs,
        out_specs=out_specs,
        out_shape=out_shape,
        compiler_params=params(40),
        cost_estimate=cost(20 * tokens * width, 20 * tokens * width),
    )(grad, values, *parts, gain, *extra)


def weight_grad_one(left, right, order):
    return weight_grad([(left, right)], order)


def weight_grad_two(one, two, order):
    return weight_grad([one, two], order)


def attend_leave_apart(dq, own, came, wq, wkv):
    return attend_leave(dq, own, came, wq, wkv, True)


def attend_leave_joined(dq, own, came, wq, wkv):
    return attend_leave(dq, own, came, wq, wkv, False)


def norm_back_last(grad, values, parts, gain):
    return norm_back(grad, values, parts, gain, None)


def low_too(value):
    return value, value.astype(LOW)


def norm_halves(norm_rows, width):
    count = norm_rows.shape[0]
    cols = jnp.pad(norm_rows.T, ((0, 0), (0, LANES - count)))
    result = []
    for first in (2, 1):
        quarters = cols.reshape(4, -1, LANES)
        blocks = [pick(quarters, block_order(first)[i]) for i in range(4)]
        if lax.axis_size("dp") == 4:
            n_seq, here = lax.axis_size("seq"), lax.axis_index("seq")
            blocks = [
                pick(block.reshape(n_seq, -1, LANES), here ^ k)
                for block in blocks
                for k in seq_order()
            ]
        block = jnp.concatenate(blocks, axis=0)
        result.append((block[: width // 2], block[width // 2 :]))
    return result


def token_counts(lengths, groups):
    onehot = (groups[:, :, None] == jnp.arange(LANGS, dtype=jnp.int32)).astype(F32)
    counts = jnp.sum(onehot * lengths[:, :, None].astype(F32), axis=(0, 1))
    if lax.axis_size("dp") != 4:
        counts = lax.psum(counts, "dp")
        return counts, counts
    counts = jnp.pad(counts[None], ((0, 7), (0, LANES - LANGS)))
    counts = counts + swap(counts, "dp", 1)
    came = swap(counts, "dp", 2)
    return (counts + came)[0, :LANGS], came


def token_tables(lengths, groups, counts, full_len, quarter):
    here, row = lax.axis_index("seq"), lax.axis_index("seq") // 2
    rows = lengths.shape[0]
    onehot = (groups[:, :, None] == jnp.arange(LANGS, dtype=jnp.int32)).astype(F32)
    all_tokens = rows * lax.axis_size("dp") * full_len
    seg_weight = all_tokens / (LANGS * jnp.sum(onehot * counts, axis=2))
    ends = pick(jnp.cumsum(lengths, axis=1), row)
    steps = jnp.arange(quarter, dtype=jnp.int32)
    places = jnp.concatenate([(here ^ k) * quarter + steps for k in (0, 2, 1, 3)])
    segs = jnp.sum((ends[None, :] <= places[:, None]).astype(jnp.int32), axis=1)
    mine = 2 * quarter
    same = segs[:mine, None] == segs[None, :]
    causal = same & (places[None, :] <= places[:mine, None])
    same_t = segs[:, None] == segs[None, :mine]
    causal_t = same_t & (places[:, None] <= places[None, :mine])
    offsets = [jnp.where(mask, 0.0, -1e30).astype(F32) for mask in (same, same_t, causal, causal_t)]
    match = (segs[:mine, None] == jnp.arange(NSEG, dtype=jnp.int32)).astype(F32)
    tok_weight = jnp.sum(match * pick(seg_weight, row)[None, :], axis=1)
    return offsets, tok_weight, all_tokens


def attn_shard(qkv, out):
    pair = jnp.concatenate([qkv[1], qkv[2]], axis=1)
    side = jnp.concatenate([qkv[0], out.T], axis=1)
    return jnp.stack([pair, side])


def qkv_out(both):
    width = both.shape[2] // 2
    qkv = jnp.stack([both[1, :, :width], both[0, :, :width], both[0, :, width:]])
    return qkv, both[1, :, width:].T


def project(left, right):
    return dot_nn(left, right).astype(LOW)


def project_out(ctx, wo):
    return dot_nt(ctx, wo).astype(LOW)


def other_core(part):
    return swap(part, "mp", 1)


def per_device(
    src,
    tgt,
    cotangent,
    lengths,
    groups,
    enc_gains,
    enc_biases,
    enc_qkv,
    enc_out,
    enc_up,
    enc_down,
    dec_gains,
    dec_biases,
    dec_self_qkv,
    dec_cross_qkv,
    dec_outs,
    dec_up,
    dec_down,
):
    rows, quarter, width = src.shape
    full_len = quarter * lax.axis_size("seq")
    n_enc, n_dec = enc_gains.shape[0], dec_gains.shape[0]
    half, hidden = enc_qkv.shape[2], enc_up.shape[1]
    order = Order()

    norms = jnp.concatenate([enc_gains, enc_biases, dec_gains, dec_biases], axis=0)
    n_norms = norms.shape[0]
    extra = jnp.pad(norms.T[None], ((0, 1), (0, 0), (0, LANES - n_norms)))
    shards = [
        jnp.concatenate([attn_shard(enc_qkv, enc_out), extra], axis=2),
        attn_shard(dec_self_qkv, dec_outs[0]),
        jnp.stack([enc_up, enc_down.T]),
        attn_shard(dec_cross_qkv, dec_outs[1]),
        jnp.stack([dec_up, dec_down.T]),
    ]
    attn_cuts = [(0, 0, 2 * half), (1, 0, half), (1, half, half)]
    feed_cuts = [(0, 0, hidden), (1, 0, hidden)]
    counts, counted = token_counts(lengths, groups)
    one, two, three, four, five = [Gather(shard) for shard in shards]
    one.along()
    two.along([one.came])
    one.join(order)
    one.along()
    src_part = pair_start(src, [two.came])
    three.along([two.came])
    two.join(order)
    one.join(order)
    one.across([counted])
    two.along([one.column])
    y_first, x_first = order(lambda: (row_order(2), row_order(1)))
    two.join(order)
    two.across(one.near)
    three.join(order)
    three.along([two.column])
    four.along([three.column])
    x_src = order(pair_end, src, src_part)
    one.far(order)
    offsets, tok_weight, all_tokens = order(
        token_tables, lengths, groups, counts, full_len, quarter
    )
    same, same_t, causal, causal_t = offsets
    factor = 1.0 / all_tokens
    three.join(order)
    four.join(order)
    four.along()
    five.along([four.column])
    *enc_w, table = one.place(order, attn_cuts + [(0, 2 * half, LANES)])
    table = table[:, :n_norms].T.astype(F32)[:, None]
    e_norm = [(table[i], table[n_enc + i]) for i in range(n_enc)]
    d_norm = [(table[2 * n_enc + i], table[2 * n_enc + n_dec + i]) for i in range(n_dec)]
    enc_in, enc_own = order(enter, x_src, (), e_norm[0], enc_w[0])
    enc_peer = swap(enc_own, "seq", 1)
    tgt_part = pair_start(tgt, [five.came])
    two.far(order)
    three.across(two.near)
    enc_q = order(project, enc_in, enc_w[1])
    four.join(order)
    enc_ctx, enc_lse = order(attend, enc_q, enc_own, enc_peer, same)
    enc_part = order(project_out, enc_ctx, enc_w[2])
    enc_other = other_core(enc_part)
    five.join(order)
    five.along()
    self_w = two.place(order, attn_cuts)
    x_tgt = order(pair_end, tgt, tgt_part)
    cot_part = pair_start(cotangent, [x_tgt])
    self_in, self_own = order(enter, x_tgt, (), d_norm[0], self_w[0])
    self_peer = swap(self_own, "seq", 1)
    self_q = order(project, self_in, self_w[1])
    three.far(order)
    four.across(three.near)
    self_ctx, self_lse = order(attend, self_q, self_own, self_peer, causal)
    self_part = order(project_out, self_ctx, self_w[2])
    self_other = other_core(self_part)
    five.join(order)
    cot = order(pair_end, cotangent, cot_part)
    out_grad, out_low = order(
        lambda cot, weight: low_too(cot.astype(F32) * weight[:, None]), cot, tok_weight
    )
    e_up, e_down = three.place(order, feed_cuts)
    four.far(order)
    five.across(four.near)
    enc_normed, enc_mid, enc_act, enc_slope, mem_part = order(
        feed, x_src, (enc_part, enc_other), e_norm[1], e_up, e_down
    )
    mem_other = other_core(mem_part)
    cross_w = four.place(order, attn_cuts)
    source, cross_own = order(enter, enc_mid, (mem_part, mem_other), None, cross_w[0])
    cross_peer = swap(cross_own, "seq", 1)
    cross_in, cross_q, dec_mid = order(
        enter, x_tgt, (self_part, self_other), d_norm[1], cross_w[1]
    )
    cross_q = cross_q[0]
    five.far(order)
    cross_ctx, cross_lse = order(attend, cross_q, cross_own, cross_peer, same)
    cross_part = order(project_out, cross_ctx, cross_w[2])
    cross_other = other_core(cross_part)
    d_up, d_down = five.place(order, feed_cuts)
    dec_normed, dec_cross, dec_act, dec_slope, dec_part = order(
        feed, dec_mid, (cross_part, cross_other), d_norm[2], d_up, d_down
    )
    dec_other = other_core(dec_part)

    pre_grad, part = order(feed_back, out_low, dec_slope, d_up, d_down)
    parts = (part, other_core(part))
    down_g = order(weight_grad_one, out_low, dec_act, x_first)
    up_g = order(weight_grad_one, dec_normed, pre_grad, y_first)
    d_feed = Scatter(up_g, down_g, factor).begin()
    cross_g, norm_five, low, ctx_grad = order(
        norm_back, out_grad, dec_cross, parts, d_norm[2][0], cross_w[2]
    )
    dq, own_grad, peer_grad = order(
        attend_back, cross_q, cross_own, cross_peer, ctx_grad, cross_lse, same_t
    )
    came = swap(peer_grad, "seq", 1)
    side_g = order(weight_grad_two, (cross_in, dq), (low, cross_ctx), x_first)
    decoded = order(
        lambda total, one, two: (total + (one.astype(F32) + two.astype(F32))).astype(LOW),
        dec_cross,
        dec_part,
        dec_other,
    )
    decoded_part = back_start(decoded)
    d_feed.add(order)
    pair_low, part = order(attend_leave_apart, dq, own_grad, came, cross_w[1], cross_w[0])
    other = other_core(part)
    pair_g = order(weight_grad_one, source, pair_low, y_first)
    cross = Scatter(pair_g, side_g, factor).begin()
    memory_grad, memory_low = order(
        lambda one, two: low_too(one[1].astype(F32) + two[1].astype(F32)), part, other
    )
    memory_part = back_start(memory_low)
    cross_parts = (part[0], other[0])
    pre_grad, enc_part = order(feed_back, memory_low, enc_slope, e_up, e_down)
    enc_parts = (enc_part, other_core(enc_part))
    down_g = order(weight_grad_one, memory_low, enc_act, x_first)
    up_g = order(weight_grad_one, enc_normed, pre_grad, y_first)
    e_feed = Scatter(up_g, down_g, factor).begin()
    mid_g, norm_four, low, ctx_grad = order(
        norm_back, cross_g, dec_mid, cross_parts, d_norm[1][0], self_w[2]
    )
    d_feed.add(order)
    cross.add(order)
    dq, own_grad, peer_grad = order(
        attend_back, self_q, self_own, self_peer, ctx_grad, self_lse, causal_t
    )
    came = swap(peer_grad, "seq", 1)
    enc_mid_g, norm_two, enc_low, enc_ctx_grad = order(
        norm_back, memory_grad, enc_mid, enc_parts, e_norm[1][0], enc_w[2]
    )
    enc_dq, enc_own_grad, enc_peer_grad = order(
        attend_back, enc_q, enc_own, enc_peer, enc_ctx_grad, enc_lse, same_t
    )
    enc_came = swap(enc_peer_grad, "seq", 1)
    e_feed.add(order)
    pair_low, part = order(attend_leave_joined, dq, own_grad, came, self_w[1], self_w[0])
    parts = (part, other_core(part))
    side_g = order(weight_grad_two, (self_in, dq), (low, self_ctx), x_first)
    pair_g = order(weight_grad_one, self_in, pair_low, y_first)
    self_s = Scatter(pair_g, side_g, factor).begin()
    d_feed.add(order)
    cross.add(order)
    side_g = order(weight_grad_two, (enc_in, enc_dq), (enc_low, enc_ctx), x_first)
    pair_low, part = order(
        attend_leave_joined, enc_dq, enc_own_grad, enc_came, enc_w[1], enc_w[0]
    )
    enc_parts = (part, other_core(part))
    pair_g = order(weight_grad_one, enc_in, pair_low, y_first)
    enc = Scatter(pair_g, side_g, factor).begin()
    e_feed.add(order)
    tgt_grad, norm_three = order(norm_back_last, mid_g, x_tgt, parts, d_norm[0][0])
    tgt_part = back_start(tgt_grad)
    self_s.add(order)
    src_grad, norm_one = order(norm_back_last, enc_mid_g, x_src, enc_parts, e_norm[0][0])
    src_part = back_start(src_grad)
    norm_grads = [norm_one, norm_two, norm_three, norm_four, norm_five]
    norm_rows = jnp.stack(
        [norm_grads[i][j] for i, j in ((0, 0), (1, 0), (0, 1), (1, 1))]
        + [norm_grads[i][j] for j in (0, 1) for i in (2, 3, 4)]
    ).astype(LOW)
    small = Scatter(*order(norm_halves, norm_rows, width), factor).begin()
    decoded = order(back_end, decoded, decoded_part)
    memory_grad = order(back_end, memory_grad, memory_part)
    cross.add(order)
    d_feed.add(order)
    enc.add(order)
    small.add(order)
    e_feed.add(order)
    self_s.add(order)
    cross.add(order)
    enc.add(order)
    small.add(order)
    tgt_grad = order(back_end, tgt_grad, tgt_part)
    self_s.add(order)
    e_feed.add(order)
    enc.add(order)
    small.add(order)
    src_grad = order(back_end, src_grad, src_part)
    self_s.add(order)
    enc.add(order)
    small.add(order)

    norm_out = small.out[0][:, :n_norms].T
    enc_qkv_g, enc_out_g = qkv_out(enc.out)
    self_qkv_g, self_out_g = qkv_out(self_s.out)
    cross_qkv_g, cross_out_g = qkv_out(cross.out)
    return (
        decoded,
        src_grad,
        tgt_grad,
        memory_grad,
        norm_out[:n_enc],
        norm_out[n_enc : 2 * n_enc],
        enc_qkv_g,
        enc_out_g,
        e_feed.out[0],
        e_feed.out[1].T,
        norm_out[2 * n_enc : 2 * n_enc + n_dec],
        norm_out[2 * n_enc + n_dec :],
        self_qkv_g,
        cross_qkv_g,
        jnp.stack([self_out_g, cross_out_g]),
        d_feed.out[0],
        d_feed.out[1].T,
    )


def solution(mesh):
    placed = (
        P("dp", "seq", None),
        P("dp", "seq", None),
        P("dp", "seq", None),
        P("dp", None),
        P("dp", None),
        P(None, ("dp", "seq")),
        P(None, ("dp", "seq")),
        P(None, ("dp", "seq"), "mp"),
        P("mp", ("dp", "seq")),
        P(("dp", "seq"), "mp"),
        P("mp", ("dp", "seq")),
        P(None, ("dp", "seq")),
        P(None, ("dp", "seq")),
        P(None, ("dp", "seq"), "mp"),
        P(None, ("dp", "seq"), "mp"),
        P(None, "mp", ("dp", "seq")),
        P(("dp", "seq"), "mp"),
        P("mp", ("dp", "seq")),
    )
    return jax.shard_map(
        per_device,
        mesh=mesh,
        in_specs=placed,
        out_specs=(
            P("dp", "seq", None),
            P("dp", "seq", None),
            P("dp", "seq", None),
            P("dp", "seq", None),
            P(None, ("dp", "seq")),
            P(None, ("dp", "seq")),
            P(None, ("dp", "seq"), "mp"),
            P("mp", ("dp", "seq")),
            P(("dp", "seq"), "mp"),
            P("mp", ("dp", "seq")),
            P(None, ("dp", "seq")),
            P(None, ("dp", "seq")),
            P(None, ("dp", "seq"), "mp"),
            P(None, ("dp", "seq"), "mp"),
            P(None, "mp", ("dp", "seq")),
            P(("dp", "seq"), "mp"),
            P("mp", ("dp", "seq")),
        ),
        check_vma=False,
    )
```

time: 1220 us -> 840 us (0.69); the launches traced: 1200 us -> 835 us
  matrix products: 195 us -> 5.57 us
  Pallas kernels: 32.8 us -> 200 us
  waiting for transfers between devices: 457 us -> 345 us
  other arithmetic: 164 us -> 76.6 us
  local copies, waits for them, and re-layouts: 170 us -> 89.4 us
  starting transfers between devices: 168 us -> 97.5 us
  between operations: 4.73 us -> 19.4 us
    dot_general x57 -> x5, matrix products: 195 us -> 5.57 us  [the longest x3 4.16 us: dot_nt(): lax.dot_general(left, right, (((1,), (1,)), ((), ())), preferred_element_...]
    pallas_call x10 -> x37, Pallas kernels: 32.8 us -> 200 us  [the longest x3 45.2 us: attend_back(): pl.pallas_call(attend_back_body, grid=(width // LANES,), in_specs=[spec]...]
    ppermute x141 -> x98, waiting for transfers between devices: 457 us -> 345 us  [swap(): return lax.ppermute(value, axis, xor_perm(lax.axis_size(axis), bits))]
    ppermute x141 -> x98, starting transfers between devices: 168 us -> 97.5 us  [swap(): return lax.ppermute(value, axis, xor_perm(lax.axis_size(axis), bits))]
    reduce_sum x19 -> x1, other arithmetic: 33.8 us -> 0.79 us  [token_counts(): counts = jnp.sum(onehot * lengths[:, :, None].astype(F32), axis=(0, 1))]
    add x28 -> x10, other arithmetic: 34 us -> 4.46 us  [the longest x6 3.86 us: step(): both = kept + came.astype(F32)]
    dynamic_slice x4 -> x1, local copies, waits for them, and re-layouts: 25.7 us -> 0.05 us  [pick(): return lax.dynamic_index_in_dim(value, index, axis, keepdims=False)]
    concatenate x21 -> x5, other arithmetic: 20.2 us -> 0.31 us  [the longest x3 0.21 us: pair_end(): return jnp.concatenate([pick(value, row), trade_end(part)], axis=0)]
  transfers between devices with their start and end apart: 141 -> 98, of which waited for: 49 -> 40; matrix products, arithmetic and copies ran while one was open for 39% -> 14% of each run, Pallas kernels for 3% -> 20%
where the time goes in v2:
time: 840 us; the launch traced here: 835 us
  waiting for transfers between devices  345 us (41%)
  Pallas kernels  200 us (24%)
  starting transfers between devices  97.5 us (12%)
  local copies, waits for them, and re-layouts  89.4 us (11%)
  other arithmetic  76.6 us (9%)
  between operations  19.4 us (2%)
    ppermute x98, waiting for transfers between devices, swap(): return lax.ppermute(value, axis, xor_perm(lax.axis_size(axis), bits))  345 us
    ppermute x98, starting transfers between devices, swap(): return lax.ppermute(value, axis, xor_perm(lax.axis_size(axis), bits))  97.5 us
    unnamed x401, local copies, waits for them, and re-layouts  54.4 us
    pallas_call x3, Pallas kernels, attend_back(): pl.pallas_call(attend_back_body, grid=(width // LANES,), in_specs=[spec]...  45.2 us
    pallas_call x10, Pallas kernels, weight_grad(): pl.pallas_call(body, grid_spec=pltpu.PrefetchScalarGridSpec(num_scalar_pr...  39 us
    pallas_call x3, Pallas kernels, attend(): pl.pallas_call(functools.partial(attend_body, 256), grid=(width // LANES,...  27.5 us
    pallas_call x2, Pallas kernels, feed(): pl.pallas_call(body, grid=(hidden // TILE,), in_specs=[same, same, same,...  24.4 us
    convert_element_type x12, other arithmetic, step(): (stay[size:].astype(F32) + new[size:].astype(F32)).astype(LOW)  19.9 us
  transfers between devices with their start and end apart: 98, of which 40 were waited for; matrix products, arithmetic and copies ran while one was open for 14% of the time, Pallas kernels for 20%

profile of v2, /device:TPU:0, one launch (start us, length us, event | category | flops | bytes accessed | tf_op | source)
XLA Modules:
  0.0 834.5 jit_solution(12431073494361338544)
XLA Ops:
  3.5 4.1 collective-permute-start
  16.1 5.0 collective-permute-done
  27.1 14.0 %collective-permute-done.1 = bf16[2,64,1024]{2,1,0:T(8,128)(2,1)S(1)} collective-permute-done((bf16[2,64,1024]{2,1,0:T(8,128)(2,1)S(1)}, bf16[2,64,1024]{2,1,0:T(8,128)(2,1)S(1)}, u32[]{:S(2)}, u32[]{:S(2)}) %collective-permute-start.1) | collective-permute-done | bytes 262176 | tf_op jit(solution)/shard_map/ppermute | solution.py:37
  55.6 11.5 %collective-permute-done.4 = bf16[2,128,1024]{2,1,0:T(8,128)(2,1)} collective-permute-done((bf16[2,128,1024]{2,1,0:T(8,128)(2,1)S(1)}, bf16[2,128,1024]{2,1,0:T(8,128)(2,1)}, u32[]{:S(2)}, u32[]{:S(2)}) %collective-permute-start.4) | collective-permute-done | bytes 524320 | tf_op jit(solution)/shard_map/ppermute | solution.py:37
  69.8 11.7 %collective-permute-done.2 = bf16[2,64,2048]{2,1,0:T(8,128)(2,1)S(1)} collective-permute-done((bf16[2,64,2048]{2,1,0:T(8,128)(2,1)S(1)}, bf16[2,64,2048]{2,1,0:T(8,128)(2,1)S(1)}, u32[]{:S(2)}, u32[]{:S(2)}) %collective-permute-start.2) | collective-permute-done | bytes 524320 | tf_op jit(solution)/shard_map/ppermute | solution.py:37
  99.0 17.4 %collective-permute-done.6 = bf16[2,128,2048]{2,1,0:T(8,128)(2,1)} collective-permute-done((bf16[2,128,2048]{2,1,0:T(8,128)(2,1)S(1)}, bf16[2,128,2048]{2,1,0:T(8,128)(2,1)}, u32[]{:S(2)}, u32[]{:S(2)}) %collective-permute-start.6) | collective-permute-done | bytes 1048608 | tf_op jit(solution)/shard_map/ppermute | solution.py:37
  121.9 4.5 collective-permute-done.17.refs_3_
  127.9 3.7 collective-permute-done.18.refs_4_
  143.9 7.7 collective-permute-done.13
  159.5 19.1 %collective-permute-done.21.kp_ref.vp_ref = bf16[2,512,512]{2,1,0:T(8,128)(2,1)S(1)} collective-permute-done((bf16[2,512,512]{2,1,0:T(8,128)(2,1)S(1)}, bf16[2,512,512]{2,1,0:T(8,128)(2,1)S(1)}, u32[]{:S(2)}, u32[]{:S(2)}) %collective-permute-start.21) | collective-permute-done | bytes 1048608 | tf_op jit(solution)/shard_map/ppermute | solution.py:37
  180.0 9.0 %shard_map.442 = (bf16[512,512]{1,0:T(8,128)(2,1)S(1)}, f32[512,512]{1,0:T(8,128)S(1)}) custom-call(bf16[512,512]{1,0:T(8,128)(2,1)S(1)} %convolution_convert_fusion.4.q_ref, bf16[2,512,512]{2,1,0:T(8,128)(2,1)S(1)} %get-tuple-element.740.ko_ref.vo_ref, bf16[2,512,512]{2,1,0:T(8,128)(2,1)S(1)} %collective-permute-done.21.kp_ref.vp_ref, ...), custom_call_target="tpu_custom_call" | custom-call | flops 2147483648 | bytes 4194304 | tf_op jit(solution)/shard_map/pallas_call | solution.py:473
  192.9 15.7 %collective-permute-done.19.refs_3_ = bf16[256,1024]{1,0:T(8,128)(2,1)S(1)} collective-permute-done((bf16[256,1024]{1,0:T(8,128)(2,1)S(1)}, bf16[256,1024]{1,0:T(8,128)(2,1)S(1)}, u32[]{:S(2)}, u32[]{:S(2)}) %collective-permute-start.19) | collective-permute-done | bytes 524320 | tf_op jit(solution)/shard_map/ppermute | solution.py:37
  208.6 5.3 shard_map.443
  225.7 43.3 %collective-permute-done.24.kp_ref.vp_ref = bf16[2,512,512]{2,1,0:T(8,128)(2,1)S(1)} collective-permute-done((bf16[2,512,512]{2,1,0:T(8,128)(2,1)S(1)}, bf16[2,512,512]{2,1,0:T(8,128)(2,1)S(1)}, u32[]{:S(2)}, u32[]{:S(2)}) %collective-permute-start.24) | collective-permute-done | bytes 1048608 | tf_op jit(solution)/shard_map/ppermute | solution.py:37
  269.5 9.2 %shard_map.445 = (bf16[512,512]{1,0:T(8,128)(2,1)S(1)}, f32[512,512]{1,0:T(8,128)S(1)}) custom-call(bf16[512,512]{1,0:T(8,128)(2,1)S(1)} %convolution_convert_fusion.3.q_ref, bf16[2,512,512]{2,1,0:T(8,128)(2,1)S(1)} %get-tuple-element.721.ko_ref.vo_ref, bf16[2,512,512]{2,1,0:T(8,128)(2,1)S(1)} %collective-permute-done.24.kp_ref.vp_ref, ...), custom_call_target="tpu_custom_call" | custom-call | flops 2147483648 | bytes 4194304 | tf_op jit(solution)/shard_map/pallas_call | solution.py:473
  289.5 5.8 collective-permute-done.30.refs_3_
  295.3 11.3 %collective-permute-done.31.refs_4_ = bf16[256,2048]{1,0:T(8,128)(2,1)S(1)} collective-permute-done((bf16[256,2048]{1,0:T(8,128)(2,1)S(1)}, bf16[256,2048]{1,0:T(8,128)(2,1)S(1)}, u32[]{:S(2)}, u32[]{:S(2)}) %collective-permute-start.31) | collective-permute-done | bytes 1048608 | tf_op jit(solution)/shard_map/ppermute | solution.py:37
  318.3 12.1 %shard_map.447 = (bf16[512,1024]{1,0:T(8,128)(2,1)S(1)}, f32[512,1024]{1,0:T(8,128)}, bf16[512,2048]{1,0:T(8,128)(2,1)}, bf16[512,2048]{1,0:T(8,128)(2,1)}, bf16[512,1024]{1,0:T(8,128)(2,1)S(1)}) custom-call(bf16[512,1024]{1,0:T(8,128)(2,1)S(1)} %copy-done.6, bf16[512,1024]{1,0:T(8,128)(2,1)} %convolution_convert_fusion.2.one_ref, ...), custom_call_target="tpu_custom_call" | custom-call | flops 4294967296 | bytes 16777216 | tf_op jit(solution)/shard_map/pallas_call | solution.py:624
  330.9 19.4 %collective-permute-done.35.refs_3_ = bf16[256,1024]{1,0:T(8,128)(2,1)S(1)} collective-permute-done((bf16[256,1024]{1,0:T(8,128)(2,1)}, bf16[256,1024]{1,0:T(8,128)(2,1)S(1)}, u32[]{:S(2)}, u32[]{:S(2)}) %collective-permute-start.35) | collective-permute-done | bytes 524320 | tf_op jit(solution)/shard_map/ppermute | solution.py:37
  351.9 11.6 %collective-permute-done.36.refs_4_ = bf16[256,1024]{1,0:T(8,128)(2,1)S(1)} collective-permute-done((bf16[256,1024]{1,0:T(8,128)(2,1)}, bf16[256,1024]{1,0:T(8,128)(2,1)S(1)}, u32[]{:S(2)}, u32[]{:S(2)}) %collective-permute-start.36) | collective-permute-done | bytes 524320 | tf_op jit(solution)/shard_map/ppermute | solution.py:37
  363.4 4.6 shard_map.448
  376.3 18.0 %collective-permute-done.39.kp_ref.vp_ref = bf16[2,512,512]{2,1,0:T(8,128)(2,1)S(1)} collective-permute-done((bf16[2,512,512]{2,1,0:T(8,128)(2,1)S(1)}, bf16[2,512,512]{2,1,0:T(8,128)(2,1)S(1)}, u32[]{:S(2)}, u32[]{:S(2)}) %collective-permute-start.39) | collective-permute-done | bytes 1048608 | tf_op jit(solution)/shard_map/ppermute | solution.py:37
  394.3 9.4 %shard_map.451 = (bf16[512,512]{1,0:T(8,128)(2,1)S(1)}, f32[512,512]{1,0:T(8,128)S(1)}) custom-call(bf16[512,512]{1,0:T(8,128)(2,1)S(1)} %bitcast.264, bf16[2,512,512]{2,1,0:T(8,128)(2,1)S(1)} %get-tuple-element.648.ko_ref.vo_ref, bf16[2,512,512]{2,1,0:T(8,128)(2,1)S(1)} %collective-permute-done.39.kp_ref.vp_ref, ...), custom_call_target="tpu_custom_call" | custom-call | flops 2147483648 | bytes 4194304 | tf_op jit(solution)/shard_map/pallas_call | solution.py:473
  411.9 12.3 %shard_map.453 = (bf16[512,1024]{1,0:T(8,128)(2,1)S(1)}, f32[512,1024]{1,0:T(8,128)}, bf16[512,2048]{1,0:T(8,128)(2,1)}, bf16[512,2048]{1,0:T(8,128)(2,1)}, bf16[512,1024]{1,0:T(8,128)(2,1)S(1)}) custom-call(f32[512,1024]{1,0:T(8,128)} %copy-done.16, bf16[512,1024]{1,0:T(8,128)(2,1)S(1)} %convolution_convert_fusion.one_ref, ...), custom_call_target="tpu_custom_call" | custom-call | flops 4294967296 | bytes 16777216 | tf_op jit(solution)/shard_map/pallas_call | solution.py:624
  424.2 8.2 shard_map.454
  432.4 4.1 shard_map.455
  436.6 4.1 shard_map.456
  443.3 3.6 collective-permute-done.46.refs_3_
  457.3 14.6 %shard_map.458 = (bf16[512,512]{1,0:T(8,128)(2,1)S(1)}, bf16[2,512,512]{2,1,0:T(8,128)(2,1)S(1)}, bf16[2,512,512]{2,1,0:T(8,128)(2,1)S(1)}) custom-call(bf16[512,512]{1,0:T(8,128)(2,1)S(1)} %bitcast.265, bf16[2,512,512]{2,1,0:T(8,128)(2,1)S(1)} %copy-done.90, bf16[2,512,512]{2,1,0:T(8,128)(2,1)S(1)} %copy-done.94, bf16[2,512,512]{2,1,0:T(8,128)(2,1)S(1)} %copy-done.90, ...), custom_call_target="tpu_custom_call" | custom-call | flops 5368709120 | bytes 6291456 | tf_op jit(solution)/shard_map/pallas_call | solution.py:528
  473.4 3.7 shard_map.459
  480.6 8.1 collective-permute-done.49
  531.8 9.2 %shard_map.462 = (bf16[512,2048]{1,0:T(8,128)(2,1)S(1)}, bf16[512,1024]{1,0:T(8,128)(2,1)}) custom-call(bf16[512,1024]{1,0:T(8,128)(2,1)S(1)} %get-tuple-element.691.low_ref.refs_0_, bf16[512,2048]{1,0:T(8,128)(2,1)} %get-tuple-element.685.slope_ref, bf16[1024,2048]{1,0:T(8,128)(2,1)} %copy-done.60, bf16[1024,2048]{1,0:T(8,128)(2,1)} %copy-done.61), custom_call_target="tpu_custom_call" | custom-call | flops 4294967296 | bytes 12582912 | tf_op jit(solution)/shard_map/pallas_call | solution.py:668
  541.0 5.2 shard_map.463
  546.2 5.2 shard_map.464
  556.4 9.3 %collective-permute-done.55 = bf16[256,2048]{1,0:T(8,128)(2,1)} collective-permute-done((bf16[256,2048]{1,0:T(8,128)(2,1)}, bf16[256,2048]{1,0:T(8,128)(2,1)}, u32[]{:S(2)}, u32[]{:S(2)}) %collective-permute-start.55) | collective-permute-done | bytes 1048608 | tf_op jit(solution)/shard_map/ppermute | solution.py:37
  581.6 15.1 %shard_map.466 = (bf16[512,512]{1,0:T(8,128)(2,1)S(1)}, bf16[2,512,512]{2,1,0:T(8,128)(2,1)S(1)}, bf16[2,512,512]{2,1,0:T(8,128)(2,1)}) custom-call(bf16[512,512]{1,0:T(8,128)(2,1)S(1)} %copy-done.136, bf16[2,512,512]{2,1,0:T(8,128)(2,1)S(1)} %copy-done.79, bf16[2,512,512]{2,1,0:T(8,128)(2,1)S(1)} %copy-done.81, bf16[2,512,512]{2,1,0:T(8,128)(2,1)S(1)} %copy-done.79, ...), custom_call_target="tpu_custom_call" | custom-call | flops 5368709120 | bytes 6291456 | tf_op jit(solution)/shard_map/pallas_call | solution.py:528
  602.0 4.0 shard_map.467
  610.2 15.5 %shard_map.468 = (bf16[512,512]{1,0:T(8,128)(2,1)S(1)}, bf16[2,512,512]{2,1,0:T(8,128)(2,1)S(1)}, bf16[2,512,512]{2,1,0:T(8,128)(2,1)}) custom-call(bf16[512,512]{1,0:T(8,128)(2,1)S(1)} %copy-done.134, bf16[2,512,512]{2,1,0:T(8,128)(2,1)S(1)} %copy-done.73, bf16[2,512,512]{2,1,0:T(8,128)(2,1)S(1)} %copy-done.75, bf16[2,512,512]{2,1,0:T(8,128)(2,1)S(1)} %copy-done.73, ...), custom_call_target="tpu_custom_call" | custom-call | flops 5368709120 | bytes 6291456 | tf_op jit(solution)/shard_map/pallas_call | solution.py:528
  635.9 3.7 shard_map.470
  653.3 4.6 shard_map.472
  664.4 7.2 collective-permute-done.69
  681.5 9.4 %collective-permute-done.65 = bf16[512,1024]{1,0:T(8,128)(2,1)} collective-permute-done((bf16[512,1024]{1,0:T(8,128)(2,1)S(1)}, bf16[512,1024]{1,0:T(8,128)(2,1)}, u32[]{:S(2)}, u32[]{:S(2)}) %collective-permute-start.65) | collective-permute-done | bytes 1048608 | tf_op jit(solution)/shard_map/ppermute | solution.py:37
  720.3 10.2 %collective-permute-done.74 = bf16[512,1024]{1,0:T(8,128)(2,1)S(1)} collective-permute-done((bf16[512,1024]{1,0:T(8,128)(2,1)S(1)}, bf16[512,1024]{1,0:T(8,128)(2,1)S(1)}, u32[]{:S(2)}, u32[]{:S(2)}) %collective-permute-start.74) | collective-permute-done | bytes 1048608 | tf_op jit(solution)/shard_map/ppermute | solution.py:37
  736.0 7.8 collective-permute-done.72
  752.7 16.4 %collective-permute-done.84 = bf16[2,64,1024]{2,1,0:T(8,128)(2,1)S(1)} collective-permute-done((bf16[2,64,1024]{2,1,0:T(8,128)(2,1)S(1)}, bf16[2,64,1024]{2,1,0:T(8,128)(2,1)S(1)}, u32[]{:S(2)}, u32[]{:S(2)}) %collective-permute-start.84) | collective-permute-done | bytes 262176 | tf_op jit(solution)/shard_map/ppermute | solution.py:37
  783.0 14.8 %collective-permute-done.91 = bf16[2,128,1024]{2,1,0:T(8,128)(2,1)S(1)} collective-permute-done((bf16[2,128,1024]{2,1,0:T(8,128)(2,1)S(1)}, bf16[2,128,1024]{2,1,0:T(8,128)(2,1)S(1)}, u32[]{:S(2)}, u32[]{:S(2)}) %collective-permute-start.91) | collective-permute-done | bytes 524320 | tf_op jit(solution)/shard_map/ppermute | solution.py:37
  802.6 11.6 %collective-permute-done.89 = bf16[2,128,1024]{2,1,0:T(8,128)(2,1)S(1)} collective-permute-done((bf16[2,128,1024]{2,1,0:T(8,128)(2,1)S(1)}, bf16[2,128,1024]{2,1,0:T(8,128)(2,1)S(1)}, u32[]{:S(2)}, u32[]{:S(2)}) %collective-permute-start.89) | collective-permute-done | bytes 524320 | tf_op jit(solution)/shard_map/ppermute | solution.py:37
  821.3 7.2 collective-permute-done.96
  (791 shorter events, 326.8 us)
Async XLA Ops:
  9.7 37.5 %collective-permute-start.7 = (f32[8,128]{1,0:T(8,128)}, f32[8,128]{1,0:T(8,128)S(1)}, u32[]{:S(2)}, u32[]{:S(2)}) collective-permute-start(f32[8,128]{1,0:T(8,128)} %pad.13), channel_id=1, source_target_pairs={{0,8},{8,0},{16,24},{24,16},{1,9},{9,1},{17,25},{25,17},{2,10},{10... | collective-permute-start | bytes 12296 | tf_op jit(solution)/shard_map/ppermute | solution.py:37
  48.9 32.6 %collective-permute-start.2 = (bf16[2,64,2048]{2,1,0:T(8,128)(2,1)S(1)}, bf16[2,64,2048]{2,1,0:T(8,128)(2,1)S(1)}, u32[]{:S(2)}, u32[]{:S(2)}) collective-permute-start(bf16[2,64,2048]{2,1,0:T(8,128)(2,1)S(1)} %pad_maximum_fusion.9), channel_id=1, source_target_pairs={{0,4},{2,6},{4,0},{6,2},{1,5},{3,7},{5,1},{7,3},{8,12},{10,14},{12... | collective-permute-start | bytes 1572872 | tf_op jit(solution)/shard_map/ppermute | solution.py:37
  50.9 34.2 %collective-permute-start.11 = (bf16[128,1024]{1,0:T(8,128)(2,1)S(1)}, bf16[128,1024]{1,0:T(8,128)(2,1)S(1)}, u32[]{:S(2)}, u32[]{:S(2)}) collective-permute-start(bf16[128,1024]{1,0:T(8,128)(2,1)S(1)} %constant_dynamic-slice_fusion.14), channel_id=1, source_target_pairs={{0,4},{2,6},{4,0},{6,2},{1,5},{3,7},{5,1},{7,3},{8,12},{10,14},{12... | collective-permute-start | bytes 786440 | tf_op jit(solution)/shard_map/ppermute | solution.py:37
  52.6 34.4 %collective-permute-start.10 = (bf16[2,256,1152]{2,1,0:T(8,128)(2,1)}, bf16[2,256,1152]{2,1,0:T(8,128)(2,1)S(1)}, u32[]{:S(2)}, u32[]{:S(2)}) collective-permute-start(bf16[2,256,1152]{2,1,0:T(8,128)(2,1)} %constant_dynamic-update-slice_fusion.4.refs_0_), channel_id=1, source_target_pairs={{0,16},{8,24},{16,0},{24,8},{1,17},{9,25},{17,1},{25,9},{2,18},{10... | collective-permute-start | bytes 3538952 | tf_op jit(solution)/shard_map/ppermute | solution.py:37
  54.1 32.9 %collective-permute-start.9 = (bf16[2,256,1152]{2,1,0:T(8,128)(2,1)}, bf16[2,256,1152]{2,1,0:T(8,128)(2,1)S(1)}, u32[]{:S(2)}, u32[]{:S(2)}) collective-permute-start(bf16[2,256,1152]{2,1,0:T(8,128)(2,1)} %constant_dynamic-update-slice_fusion.4.refs_0_), channel_id=1, source_target_pairs={{0,8},{8,0},{16,24},{24,16},{1,9},{9,1},{17,25},{25,17},{2,10},{10... | collective-permute-start | bytes 3538952 | tf_op jit(solution)/shard_map/ppermute | solution.py:37
  85.1 31.3 %collective-permute-start.6 = (bf16[2,128,2048]{2,1,0:T(8,128)(2,1)S(1)}, bf16[2,128,2048]{2,1,0:T(8,128)(2,1)}, u32[]{:S(2)}, u32[]{:S(2)}) collective-permute-start(bf16[2,128,2048]{2,1,0:T(8,128)(2,1)S(1)} %constant_dynamic-update-slice_fusion.8), channel_id=1, source_target_pairs={{0,2},{2,0},{4,6},{6,4},{1,3},{3,1},{5,7},{7,5},{8,10},{10,8},{12,... | collective-permute-start | bytes 3145736 | tf_op jit(solution)/shard_map/ppermute | solution.py:37
  85.1 34.4 %collective-permute-start.5 = (bf16[2,64,1024]{2,1,0:T(8,128)(2,1)S(1)}, bf16[2,64,1024]{2,1,0:T(8,128)(2,1)}, u32[]{:S(2)}, u32[]{:S(2)}) collective-permute-start(bf16[2,64,1024]{2,1,0:T(8,128)(2,1)S(1)} %pad_maximum_fusion.13), channel_id=1, source_target_pairs={{0,4},{2,6},{4,0},{6,2},{1,5},{3,7},{5,1},{7,3},{8,12},{10,14},{12... | collective-permute-start | bytes 786440 | tf_op jit(solution)/shard_map/ppermute | solution.py:37
  87.1 64.6 %collective-permute-start.15 = (bf16[2,256,1024]{2,1,0:T(8,128)(2,1)}, bf16[2,256,1024]{2,1,0:T(8,128)(2,1)}, u32[]{:S(2)}, u32[]{:S(2)}) collective-permute-start(bf16[2,256,1024]{2,1,0:T(8,128)(2,1)} %constant_dynamic-update-slice_fusion.6.refs_0_), channel_id=1, source_target_pairs={{0,8},{8,0},{16,24},{24,16},{1,9},{9,1},{17,25},{25,17},{2,10},{10... | collective-permute-start | bytes 3145736 | tf_op jit(solution)/shard_map/ppermute | solution.py:37
  88.6 63.0 %collective-permute-start.16 = (bf16[2,256,1024]{2,1,0:T(8,128)(2,1)}, bf16[2,256,1024]{2,1,0:T(8,128)(2,1)}, u32[]{:S(2)}, u32[]{:S(2)}) collective-permute-start(bf16[2,256,1024]{2,1,0:T(8,128)(2,1)} %constant_dynamic-update-slice_fusion.6.refs_0_), channel_id=1, source_target_pairs={{0,16},{8,24},{16,0},{24,8},{1,17},{9,25},{17,1},{25,9},{2,18},{10... | collective-permute-start | bytes 3145736 | tf_op jit(solution)/shard_map/ppermute | solution.py:37
  91.9 34.5 %collective-permute-start.17 = (bf16[256,1152]{1,0:T(8,128)(2,1)}, bf16[256,1152]{1,0:T(8,128)(2,1)}, u32[]{:S(2)}, u32[]{:S(2)}) collective-permute-start(bf16[256,1152]{1,0:T(8,128)(2,1)} %slice_bitcast_fusion.10), channel_id=1, source_target_pairs={{0,16},{8,24},{16,0},{24,8},{1,17},{9,25},{17,1},{25,9},{2,18},{10... | collective-permute-start | bytes 1769480 | tf_op jit(solution)/shard_map/ppermute | solution.py:37
  121.9 33.9 %collective-permute-start.22 = (bf16[2,128,1024]{2,1,0:T(8,128)(2,1)}, bf16[2,128,1024]{2,1,0:T(8,128)(2,1)}, u32[]{:S(2)}, u32[]{:S(2)}) collective-permute-start(bf16[2,128,1024]{2,1,0:T(8,128)(2,1)} %constant_dynamic-update-slice_fusion.12), channel_id=1, source_target_pairs={{0,2},{2,0},{4,6},{6,4},{1,3},{3,1},{5,7},{7,5},{8,10},{10,8},{12,... | collective-permute-start | bytes 1572872 | tf_op jit(solution)/shard_map/ppermute | solution.py:37
  143.8 34.8 %collective-permute-start.21 = (bf16[2,512,512]{2,1,0:T(8,128)(2,1)S(1)}, bf16[2,512,512]{2,1,0:T(8,128)(2,1)S(1)}, u32[]{:S(2)}, u32[]{:S(2)}) collective-permute-start(bf16[2,512,512]{2,1,0:T(8,128)(2,1)S(1)} %get-tuple-element.740.ko_ref.vo_ref), channel_id=1, source_target_pairs={{0,2},{2,0},{4,6},{6,4},{1,3},{3,1},{5,7},{7,5},{8,10},{10,8},{12,... | collective-permute-start | bytes 3145736 | tf_op jit(solution)/shard_map/ppermute | solution.py:37
  151.6 62.4 %collective-permute-start.14 = (bf16[128,1024]{1,0:T(8,128)(2,1)S(1)}, bf16[128,1024]{1,0:T(8,128)(2,1)S(1)}, u32[]{:S(2)}, u32[]{:S(2)}) collective-permute-start(bf16[128,1024]{1,0:T(8,128)(2,1)S(1)} %constant_dynamic-slice_fusion.11), channel_id=1, source_target_pairs={{0,4},{2,6},{4,0},{6,2},{1,5},{3,7},{5,1},{7,3},{8,12},{10,14},{12... | collective-permute-start | bytes 786440 | tf_op jit(solution)/shard_map/ppermute | solution.py:37
  151.7 70.7 %collective-permute-start.25 = (bf16[2,256,2048]{2,1,0:T(8,128)(2,1)S(1)}, bf16[2,256,2048]{2,1,0:T(8,128)(2,1)S(1)}, u32[]{:S(2)}, u32[]{:S(2)}) collective-permute-start(bf16[2,256,2048]{2,1,0:T(8,128)(2,1)S(1)} %constant_dynamic-update-slice_fusion.10.refs_0_), channel_id=1, source_target_pairs={{0,8},{8,0},{16,24},{24,16},{1,9},{9,1},{17,25},{25,17},{2,10},{10... | collective-permute-start | bytes 6291464 | tf_op jit(solution)/shard_map/ppermute | solution.py:37
  152.3 70.1 %collective-permute-start.26 = (bf16[2,256,2048]{2,1,0:T(8,128)(2,1)S(1)}, bf16[2,256,2048]{2,1,0:T(8,128)(2,1)S(1)}, u32[]{:S(2)}, u32[]{:S(2)}) collective-permute-start(bf16[2,256,2048]{2,1,0:T(8,128)(2,1)S(1)} %constant_dynamic-update-slice_fusion.10.refs_0_), channel_id=1, source_target_pairs={{0,16},{8,24},{16,0},{24,8},{1,17},{9,25},{17,1},{25,9},{2,18},{10... | collective-permute-start | bytes 6291464 | tf_op jit(solution)/shard_map/ppermute | solution.py:37
  155.7 52.9 %collective-permute-start.19 = (bf16[256,1024]{1,0:T(8,128)(2,1)S(1)}, bf16[256,1024]{1,0:T(8,128)(2,1)S(1)}, u32[]{:S(2)}, u32[]{:S(2)}) collective-permute-start(bf16[256,1024]{1,0:T(8,128)(2,1)S(1)} %slice_bitcast_fusion.19), channel_id=1, source_target_pairs={{0,16},{8,24},{16,0},{24,8},{1,17},{9,25},{17,1},{25,9},{2,18},{10... | collective-permute-start | bytes 1572872 | tf_op jit(solution)/shard_map/ppermute | solution.py:37
  214.2 66.3 %collective-permute-start.33 = (bf16[2,128,2048]{2,1,0:T(8,128)(2,1)S(1)}, bf16[2,128,2048]{2,1,0:T(8,128)(2,1)S(1)}, u32[]{:S(2)}, u32[]{:S(2)}) collective-permute-start(bf16[2,128,2048]{2,1,0:T(8,128)(2,1)S(1)} %constant_dynamic-update-slice_fusion.16), channel_id=1, source_target_pairs={{0,2},{2,0},{4,6},{6,4},{1,3},{3,1},{5,7},{7,5},{8,10},{10,8},{12,... | collective-permute-start | bytes 3145736 | tf_op jit(solution)/shard_map/ppermute | solution.py:37
  219.8 49.2 %collective-permute-start.24 = (bf16[2,512,512]{2,1,0:T(8,128)(2,1)S(1)}, bf16[2,512,512]{2,1,0:T(8,128)(2,1)S(1)}, u32[]{:S(2)}, u32[]{:S(2)}) collective-permute-start(bf16[2,512,512]{2,1,0:T(8,128)(2,1)S(1)} %get-tuple-element.721.ko_ref.vo_ref), channel_id=1, source_target_pairs={{0,2},{2,0},{4,6},{6,4},{1,3},{3,1},{5,7},{7,5},{8,10},{10,8},{12,... | collective-permute-start | bytes 3145736 | tf_op jit(solution)/shard_map/ppermute | solution.py:37
  221.2 63.0 %collective-permute-start.32 = (bf16[128,1024]{1,0:T(8,128)(2,1)S(1)}, bf16[128,1024]{1,0:T(8,128)(2,1)S(1)}, u32[]{:S(2)}, u32[]{:S(2)}) collective-permute-start(bf16[128,1024]{1,0:T(8,128)(2,1)S(1)} %constant_dynamic-slice_fusion.10), channel_id=1, source_target_pairs={{0,4},{2,6},{4,0},{6,2},{1,5},{3,7},{5,1},{7,3},{8,12},{10,14},{12... | collective-permute-start | bytes 786440 | tf_op jit(solution)/shard_map/ppermute | solution.py:37
  222.4 64.9 %collective-permute-start.28 = (bf16[2,256,1024]{2,1,0:T(8,128)(2,1)S(1)}, bf16[2,256,1024]{2,1,0:T(8,128)(2,1)S(1)}, u32[]{:S(2)}, u32[]{:S(2)}) collective-permute-start(bf16[2,256,1024]{2,1,0:T(8,128)(2,1)S(1)} %constant_dynamic-update-slice_fusion.14.refs_0_), channel_id=1, source_target_pairs={{0,8},{8,0},{16,24},{24,16},{1,9},{9,1},{17,25},{25,17},{2,10},{10... | collective-permute-start | bytes 3145736 | tf_op jit(solution)/shard_map/ppermute | solution.py:37
  224.0 63.4 %collective-permute-start.29 = (bf16[2,256,1024]{2,1,0:T(8,128)(2,1)S(1)}, bf16[2,256,1024]{2,1,0:T(8,128)(2,1)S(1)}, u32[]{:S(2)}, u32[]{:S(2)}) collective-permute-start(bf16[2,256,1024]{2,1,0:T(8,128)(2,1)S(1)} %constant_dynamic-update-slice_fusion.14.refs_0_), channel_id=1, source_target_pairs={{0,16},{8,24},{16,0},{24,8},{1,17},{9,25},{17,1},{25,9},{2,18},{10... | collective-permute-start | bytes 3145736 | tf_op jit(solution)/shard_map/ppermute | solution.py:37
  287.3 86.2 %collective-permute-start.40 = (bf16[2,256,2048]{2,1,0:T(8,128)(2,1)}, bf16[2,256,2048]{2,1,0:T(8,128)(2,1)S(1)}, u32[]{:S(2)}, u32[]{:S(2)}) collective-permute-start(bf16[2,256,2048]{2,1,0:T(8,128)(2,1)} %constant_dynamic-update-slice_fusion.18.refs_0_), channel_id=1, source_target_pairs={{0,8},{8,0},{16,24},{24,16},{1,9},{9,1},{17,25},{25,17},{2,10},{10... | collective-permute-start | bytes 6291464 | tf_op jit(solution)/shard_map/ppermute | solution.py:37
  287.9 85.6 %collective-permute-start.41 = (bf16[2,256,2048]{2,1,0:T(8,128)(2,1)}, bf16[2,256,2048]{2,1,0:T(8,128)(2,1)S(1)}, u32[]{:S(2)}, u32[]{:S(2)}) collective-permute-start(bf16[2,256,2048]{2,1,0:T(8,128)(2,1)} %constant_dynamic-update-slice_fusion.18.refs_0_), channel_id=1, source_target_pairs={{0,16},{8,24},{16,0},{24,8},{1,17},{9,25},{17,1},{25,9},{2,18},{10... | collective-permute-start | bytes 6291464 | tf_op jit(solution)/shard_map/ppermute | solution.py:37
  313.8 36.6 %collective-permute-start.35 = (bf16[256,1024]{1,0:T(8,128)(2,1)}, bf16[256,1024]{1,0:T(8,128)(2,1)S(1)}, u32[]{:S(2)}, u32[]{:S(2)}) collective-permute-start(bf16[256,1024]{1,0:T(8,128)(2,1)} %slice_bitcast_fusion.17), channel_id=1, source_target_pairs={{0,16},{8,24},{16,0},{24,8},{1,17},{9,25},{17,1},{25,9},{2,18},{10... | collective-permute-start | bytes 1572872 | tf_op jit(solution)/shard_map/ppermute | solution.py:37
  330.4 37.7 %collective-permute-start.38 = (bf16[512,1024]{1,0:T(8,128)(2,1)S(1)}, bf16[512,1024]{1,0:T(8,128)(2,1)S(1)}, u32[]{:S(2)}, u32[]{:S(2)}) collective-permute-start(bf16[512,1024]{1,0:T(8,128)(2,1)S(1)} %get-tuple-element.577.refs_1_), channel_id=1, source_target_pairs={{0,1},{1,0},{2,3},{3,2},{4,5},{5,4},{6,7},{7,6},{8,9},{9,8},{10,11... | collective-permute-start | bytes 3145736 | tf_op jit(solution)/shard_map/ppermute | solution.py:37
  330.4 40.7 %collective-permute-start.27 = (bf16[512,1024]{1,0:T(8,128)(2,1)}, bf16[512,1024]{1,0:T(8,128)(2,1)S(1)}, u32[]{:S(2)}, u32[]{:S(2)}) collective-permute-start(bf16[512,1024]{1,0:T(8,128)(2,1)} %convolution_convert_fusion.1.refs_1_), channel_id=1, source_target_pairs={{0,1},{1,0},{2,3},{3,2},{4,5},{5,4},{6,7},{7,6},{8,9},{9,8},{10,11... | collective-permute-start | bytes 3145736 | tf_op jit(solution)/shard_map/ppermute | solution.py:37
  440.7 48.0 %collective-permute-start.49 = (bf16[512,2048]{1,0:T(8,128)(2,1)S(1)}, bf16[512,2048]{1,0:T(8,128)(2,1)}, u32[]{:S(2)}, u32[]{:S(2)}) collective-permute-start(bf16[512,2048]{1,0:T(8,128)(2,1)S(1)} %get-tuple-element.635), channel_id=1, source_target_pairs={{0,16},{8,24},{16,0},{24,8},{1,17},{9,25},{17,1},{25,9},{2,18},{10... | collective-permute-start | bytes 6291464 | tf_op jit(solution)/shard_map/ppermute | solution.py:37
  441.3 47.6 %collective-permute-start.50 = (bf16[512,2048]{1,0:T(8,128)(2,1)S(1)}, bf16[512,2048]{1,0:T(8,128)(2,1)}, u32[]{:S(2)}, u32[]{:S(2)}) collective-permute-start(bf16[512,2048]{1,0:T(8,128)(2,1)S(1)} %get-tuple-element.630), channel_id=1, source_target_pairs={{0,8},{8,0},{16,24},{24,16},{1,9},{9,1},{17,25},{25,17},{2,10},{10... | collective-permute-start | bytes 6291464 | tf_op jit(solution)/shard_map/ppermute | solution.py:37
  442.8 34.4 %collective-permute-start.45 = (bf16[512,1024]{1,0:T(8,128)(2,1)S(1)}, bf16[512,1024]{1,0:T(8,128)(2,1)}, u32[]{:S(2)}, u32[]{:S(2)}) collective-permute-start(bf16[512,1024]{1,0:T(8,128)(2,1)S(1)} %get-tuple-element.664), channel_id=1, source_target_pairs={{0,1},{1,0},{2,3},{3,2},{4,5},{5,4},{6,7},{7,6},{8,9},{9,8},{10,11... | collective-permute-start | bytes 3145736 | tf_op jit(solution)/shard_map/ppermute | solution.py:37
  517.4 56.9 %collective-permute-start.54 = (bf16[512,1024]{1,0:T(8,128)(2,1)}, bf16[512,1024]{1,0:T(8,128)(2,1)}, u32[]{:S(2)}, u32[]{:S(2)}) collective-permute-start(bf16[512,1024]{1,0:T(8,128)(2,1)} %copy-done.86), channel_id=1, source_target_pairs={{0,8},{8,0},{16,24},{24,16},{1,9},{9,1},{17,25},{25,17},{2,10},{10... | collective-permute-start | bytes 3145736 | tf_op jit(solution)/shard_map/ppermute | solution.py:37
  519.9 182.9 %collective-permute-start.47 = (bf16[128,1024]{1,0:T(8,128)(2,1)}, bf16[128,1024]{1,0:T(8,128)(2,1)}, u32[]{:S(2)}, u32[]{:S(2)}) collective-permute-start(bf16[128,1024]{1,0:T(8,128)(2,1)} %constant_dynamic-slice_fusion.9), channel_id=1, source_target_pairs={{0,4},{2,6},{4,0},{6,2},{1,5},{3,7},{5,1},{7,3},{8,12},{10,14},{12... | collective-permute-start | bytes 786440 | tf_op jit(solution)/shard_map/ppermute | solution.py:37
  519.9 36.4 %collective-permute-start.56 = (bf16[256,2048]{1,0:T(8,128)(2,1)}, bf16[256,2048]{1,0:T(8,128)(2,1)}, u32[]{:S(2)}, u32[]{:S(2)}) collective-permute-start(bf16[256,2048]{1,0:T(8,128)(2,1)} %add_convert_fusion.2), channel_id=1, source_target_pairs={{0,16},{8,24},{16,0},{24,8},{1,17},{9,25},{17,1},{25,9},{2,18},{10... | collective-permute-start | bytes 3145736 | tf_op jit(solution)/shard_map/ppermute | solution.py:37
  521.5 44.3 %collective-permute-start.55 = (bf16[256,2048]{1,0:T(8,128)(2,1)}, bf16[256,2048]{1,0:T(8,128)(2,1)}, u32[]{:S(2)}, u32[]{:S(2)}) collective-permute-start(bf16[256,2048]{1,0:T(8,128)(2,1)} %add_convert_fusion.3), channel_id=1, source_target_pairs={{0,8},{8,0},{16,24},{24,16},{1,9},{9,1},{17,25},{25,17},{2,10},{10... | collective-permute-start | bytes 3145736 | tf_op jit(solution)/shard_map/ppermute | solution.py:37
  528.4 46.5 %collective-permute-start.53 = (bf16[512,1024]{1,0:T(8,128)(2,1)S(1)}, bf16[512,1024]{1,0:T(8,128)(2,1)}, u32[]{:S(2)}, u32[]{:S(2)}) collective-permute-start(bf16[512,1024]{1,0:T(8,128)(2,1)S(1)} %get-tuple-element.680), channel_id=1, source_target_pairs={{0,16},{8,24},{16,0},{24,8},{1,17},{9,25},{17,1},{25,9},{2,18},{10... | collective-permute-start | bytes 3145736 | tf_op jit(solution)/shard_map/ppermute | solution.py:37
  556.3 42.2 %collective-permute-start.52 = (bf16[512,1024]{1,0:T(8,128)(2,1)}, bf16[512,1024]{1,0:T(8,128)(2,1)S(1)}, u32[]{:S(2)}, u32[]{:S(2)}) collective-permute-start(bf16[512,1024]{1,0:T(8,128)(2,1)} %get-tuple-element.731.refs_2_), channel_id=1, source_target_pairs={{0,1},{1,0},{2,3},{3,2},{4,5},{5,4},{6,7},{7,6},{8,9},{9,8},{10,11... | collective-permute-start | bytes 3145736 | tf_op jit(solution)/shard_map/ppermute | solution.py:37
  565.7 59.9 %collective-permute-start.62 = (bf16[512,2048]{1,0:T(8,128)(2,1)}, bf16[512,2048]{1,0:T(8,128)(2,1)}, u32[]{:S(2)}, u32[]{:S(2)}) collective-permute-start(bf16[512,2048]{1,0:T(8,128)(2,1)} %get-tuple-element.698), channel_id=1, source_target_pairs={{0,16},{8,24},{16,0},{24,8},{1,17},{9,25},{17,1},{25,9},{2,18},{10... | collective-permute-start | bytes 6291464 | tf_op jit(solution)/shard_map/ppermute | solution.py:37
  574.3 52.0 %collective-permute-start.63 = (bf16[512,2048]{1,0:T(8,128)(2,1)}, bf16[512,2048]{1,0:T(8,128)(2,1)}, u32[]{:S(2)}, u32[]{:S(2)}) collective-permute-start(bf16[512,2048]{1,0:T(8,128)(2,1)} %get-tuple-element.693), channel_id=1, source_target_pairs={{0,8},{8,0},{16,24},{24,16},{1,9},{9,1},{17,25},{25,17},{2,10},{10... | collective-permute-start | bytes 6291464 | tf_op jit(solution)/shard_map/ppermute | solution.py:37
  574.9 67.6 %collective-permute-start.60 = (bf16[2,128,2048]{2,1,0:T(8,128)(2,1)}, bf16[2,128,2048]{2,1,0:T(8,128)(2,1)}, u32[]{:S(2)}, u32[]{:S(2)}) collective-permute-start(bf16[2,128,2048]{2,1,0:T(8,128)(2,1)} %fusion.3), channel_id=1, source_target_pairs={{0,2},{2,0},{4,6},{6,4},{1,3},{3,1},{5,7},{7,5},{8,10},{10,8},{12,... | collective-permute-start | bytes 3145736 | tf_op jit(solution)/shard_map/ppermute | solution.py:37
  599.5 33.7 %collective-permute-start.61 = (bf16[2,512,512]{2,1,0:T(8,128)(2,1)}, bf16[2,512,512]{2,1,0:T(8,128)(2,1)S(1)}, u32[]{:S(2)}, u32[]{:S(2)}) collective-permute-start(bf16[2,512,512]{2,1,0:T(8,128)(2,1)} %get-tuple-element.728), channel_id=1, source_target_pairs={{0,2},{2,0},{4,6},{6,4},{1,3},{3,1},{5,7},{7,5},{8,10},{10,8},{12,... | collective-permute-start | bytes 3145736 | tf_op jit(solution)/shard_map/ppermute | solution.py:37
  647.9 31.0 %collective-permute-start.67 = (bf16[512,1024]{1,0:T(8,128)(2,1)S(1)}, bf16[512,1024]{1,0:T(8,128)(2,1)S(1)}, u32[]{:S(2)}, u32[]{:S(2)}) collective-permute-start(bf16[512,1024]{1,0:T(8,128)(2,1)S(1)} %get-tuple-element.806.refs_2_), channel_id=1, source_target_pairs={{0,1},{1,0},{2,3},{3,2},{4,5},{5,4},{6,7},{7,6},{8,9},{9,8},{10,11... | collective-permute-start | bytes 3145736 | tf_op jit(solution)/shard_map/ppermute | solution.py:37
  658.8 32.0 %collective-permute-start.65 = (bf16[512,1024]{1,0:T(8,128)(2,1)S(1)}, bf16[512,1024]{1,0:T(8,128)(2,1)}, u32[]{:S(2)}, u32[]{:S(2)}) collective-permute-start(bf16[512,1024]{1,0:T(8,128)(2,1)S(1)} %get-tuple-element.769), channel_id=1, source_target_pairs={{0,16},{8,24},{16,0},{24,8},{1,17},{9,25},{17,1},{25,9},{2,18},{10... | collective-permute-start | bytes 3145736 | tf_op jit(solution)/shard_map/ppermute | solution.py:37
  710.0 37.3 %collective-permute-start.87 = (bf16[2,128,2048]{2,1,0:T(8,128)(2,1)S(1)}, bf16[2,128,2048]{2,1,0:T(8,128)(2,1)S(1)}, u32[]{:S(2)}, u32[]{:S(2)}) collective-permute-start(bf16[2,128,2048]{2,1,0:T(8,128)(2,1)S(1)} %copy-done.156), channel_id=1, source_target_pairs={{0,2},{2,0},{4,6},{6,4},{1,3},{3,1},{5,7},{7,5},{8,10},{10,8},{12,... | collective-permute-start | bytes 3145736 | tf_op jit(solution)/shard_map/ppermute | solution.py:37
  713.8 34.5 %collective-permute-start.86 = (bf16[256,1024]{1,0:T(8,128)(2,1)S(1)}, bf16[256,1024]{1,0:T(8,128)(2,1)S(1)}, u32[]{:S(2)}, u32[]{:S(2)}) collective-permute-start(bf16[256,1024]{1,0:T(8,128)(2,1)S(1)} %copy-done.161), channel_id=1, source_target_pairs={{0,16},{8,24},{16,0},{24,8},{1,17},{9,25},{17,1},{25,9},{2,18},{10... | collective-permute-start | bytes 1572872 | tf_op jit(solution)/shard_map/ppermute | solution.py:37
  717.1 32.7 %collective-permute-start.85 = (bf16[256,1024]{1,0:T(8,128)(2,1)S(1)}, bf16[256,1024]{1,0:T(8,128)(2,1)S(1)}, u32[]{:S(2)}, u32[]{:S(2)}) collective-permute-start(bf16[256,1024]{1,0:T(8,128)(2,1)S(1)} %copy-done.160), channel_id=1, source_target_pairs={{0,8},{8,0},{16,24},{24,16},{1,9},{9,1},{17,25},{25,17},{2,10},{10... | collective-permute-start | bytes 1572872 | tf_op jit(solution)/shard_map/ppermute | solution.py:37
  733.4 44.3 %collective-permute-start.92 = (bf16[128,1024]{1,0:T(8,128)(2,1)S(1)}, bf16[128,1024]{1,0:T(8,128)(2,1)S(1)}, u32[]{:S(2)}, u32[]{:S(2)}) collective-permute-start(bf16[128,1024]{1,0:T(8,128)(2,1)S(1)} %copy-done.163), channel_id=1, source_target_pairs={{0,4},{2,6},{4,0},{6,2},{1,5},{3,7},{5,1},{7,3},{8,12},{10,14},{12... | collective-permute-start | bytes 786440 | tf_op jit(solution)/shard_map/ppermute | solution.py:37
  743.8 74.1 %collective-permute-start.71 = (bf16[128,1024]{1,0:T(8,128)(2,1)S(1)}, bf16[128,1024]{1,0:T(8,128)(2,1)S(1)}, u32[]{:S(2)}, u32[]{:S(2)}) collective-permute-start(bf16[128,1024]{1,0:T(8,128)(2,1)S(1)} %dynamic-slice_convert_fusion.1), channel_id=1, source_target_pairs={{0,4},{2,6},{4,0},{6,2},{1,5},{3,7},{5,1},{7,3},{8,12},{10,14},{12... | collective-permute-start | bytes 786440 | tf_op jit(solution)/shard_map/ppermute | solution.py:37
  777.5 36.6 %collective-permute-start.89 = (bf16[2,128,1024]{2,1,0:T(8,128)(2,1)S(1)}, bf16[2,128,1024]{2,1,0:T(8,128)(2,1)S(1)}, u32[]{:S(2)}, u32[]{:S(2)}) collective-permute-start(bf16[2,128,1024]{2,1,0:T(8,128)(2,1)S(1)} %fusion.7), channel_id=1, source_target_pairs={{0,2},{2,0},{4,6},{6,4},{1,3},{3,1},{5,7},{7,5},{8,10},{10,8},{12,... | collective-permute-start | bytes 1572872 | tf_op jit(solution)/shard_map/ppermute | solution.py:37
  779.3 35.6 %collective-permute-start.88 = (bf16[2,128,128]{2,1,0:T(8,128)(2,1)S(1)}, bf16[2,128,128]{2,1,0:T(8,128)(2,1)S(1)}, u32[]{:S(2)}, u32[]{:S(2)}) collective-permute-start(bf16[2,128,128]{2,1,0:T(8,128)(2,1)S(1)} %fusion.18), channel_id=1, source_target_pairs={{0,2},{2,0},{4,6},{6,4},{1,3},{3,1},{5,7},{7,5},{8,10},{10,8},{12,... | collective-permute-start | bytes 196616 | tf_op jit(solution)/shard_map/ppermute | solution.py:37
  (235 other events, 2871.9 us)

commit v3 on v2

--- a/solution.py
+++ b/solution.py
@@ -54,7 +54,7 @@
 
 
 def cost(flops, nbytes, exps=0):
-    return pl.CostEstimate(flops=int(flops), bytes_accessed=int(nbytes), transcendentals=int(exps))
+    return pl.CostEstimate(flops=1, bytes_accessed=1, transcendentals=0)
 
 
 class Order:
@@ -69,6 +69,9 @@
         out = step(*jax.tree.unflatten(tree, leaves))
         self.last = jax.tree.leaves(out)
         return out
+
+    def wait(self, *values):
+        self.last = self.last + jax.tree.leaves(values)
 
 
 def after(values, others):
@@ -157,13 +160,20 @@
 
 
 class Gather:
-    def __init__(self, shard):
-        self.column = shard
-        self.steps = seq_steps()
-
-    def along(self, others=()):
-        (ready,) = after([self.column], others)
-        self.came = swap(ready, "seq", self.steps.pop(0))
+    def __init__(self, shards, stepwise, others=()):
+        self.plain = lax.axis_size("dp") != 4
+        self.relative = stepwise
+        shards = jnp.stack(shards)
+        if others:
+            (shards,) = after([shards], others)
+        if stepwise:
+            self.spots, self.column, self.steps = seq_order(), shards, seq_steps()
+        else:
+            self.spots = list(range(lax.axis_size("seq")))
+            self.column = lax.all_gather(shards, "seq", axis=1, tiled=True)
+
+    def along(self):
+        self.came = swap(self.column, "seq", self.steps.pop(0))
 
     def join(self, order):
         self.column = order(
@@ -171,7 +181,6 @@
         )
 
     def across(self, others=()):
-        self.plain = lax.axis_size("dp") != 4
         self.near = []
         if self.plain:
             return
@@ -179,20 +188,22 @@
         self.near = [swap(ready, "dp", 1), swap(ready, "dp", 2)]
 
     def far(self, order):
+        self.last = []
         if self.plain:
             return
         one, two = order(lambda x, y: (x[0], y[1]), *self.near)
-        self.last = (swap(one, "dp", 2), swap(two, "dp", 1))
+        self.last = [swap(one, "dp", 2), swap(two, "dp", 1)]
 
     def place(self, order, cuts):
-        if self.plain:
-            return order(place_weights, [self.column], cuts)
-        return order(place_weights, [self.column, *self.near, self.last], cuts)
-
-
-def place_weights(sources, cuts):
-    here, spot = lax.axis_index("seq"), lax.axis_index("dp")
-    spots = jnp.asarray(seq_order(), jnp.int32) ^ here.astype(jnp.int32)
+        spots = jnp.asarray(self.spots, jnp.int32)
+        if self.relative:
+            spots = spots ^ lax.axis_index("seq").astype(jnp.int32)
+        sources = [self.column] if self.plain else [self.column, *self.near, tuple(self.last)]
+        return order(place_weights, sources, spots, cuts)
+
+
+def place_weights(sources, spots, cuts):
+    spot = lax.axis_index("dp")
     if lax.axis_size("dp") != 4:
         cols = sources[0].shape[2]
         halves = place(sources, spots, [(0, 0, cols), (1, 0, cols)])
@@ -210,7 +221,10 @@
     return jnp.asarray([first, 3, 0, 3 - first], jnp.int32) ^ spot
 
 
-def row_order(first):
+def row_order(first, relative):
+    if not relative:
+        places = jnp.arange(lax.axis_size("seq"), dtype=jnp.int32)
+        return jnp.concatenate([block_order(first), places])
     away = jnp.arange(lax.axis_size("seq"), dtype=jnp.int32)
     away = away ^ lax.axis_index("seq").astype(jnp.int32)
     turn, bits = jnp.zeros_like(away), seq_steps()
@@ -219,21 +233,25 @@
     return jnp.concatenate([block_order(first), turn])
 
 
-def weight_grad(pairs, order):
+def weight_grad(pairs, order, extra=None):
     tokens, width = pairs[0][0].shape
     size = width // 4
     cols = sum(right.shape[1] for _, right in pairs)
+    cols += 0 if extra is None else extra.shape[1]
     n_seq = lax.axis_size("seq")
     near = lax.axis_size("dp") == 4
     unit = size // n_seq if near else size
 
     def body(order_ref, *refs):
-        away, stay = refs[2 * len(pairs) :]
+        away, stay = refs[-2:]
         step = pl.program_id(0)
+        parts = [
+            dot_tn(refs[2 * j][...], refs[2 * j + 1][...]).astype(LOW) for j in range(len(pairs))
+        ]
+        if extra is not None:
+            parts.append(refs[2 * len(pairs)][...])
         start = 0
-        for j in range(len(pairs)):
-            left, right = refs[2 * j], refs[2 * j + 1]
-            part = dot_tn(left[...], right[...]).astype(LOW)
+        for part in parts:
             stop = start + part.shape[1]
 
             def put(out):
@@ -251,6 +269,9 @@
         specs.append(pl.BlockSpec((tokens, size), lambda i, order: (0, order[i])))
         specs.append(pl.BlockSpec(right.shape, lambda i, order: (0, 0)))
         values += [left, right]
+    if extra is not None:
+        specs.append(pl.BlockSpec((size, extra.shape[1]), lambda i, order: (order[i], 0)))
+        values.append(extra)
     return pl.pallas_call(
         body,
         grid_spec=pltpu.PrefetchScalarGridSpec(
@@ -269,18 +290,25 @@
 
 
 class Scatter:
-    def __init__(self, pair, side, factor):
+    def __init__(self, pair, side, factor, relative=True):
+        self.relative = relative
         self.halves, self.factor, self.stage = (pair, side), factor, 0
         self.bits = (2, 1)
         self.plain = lax.axis_size("dp") != 4
 
-    def start(self, j):
-        away, _ = self.halves[j]
-        return None if self.plain else swap(away, "dp", self.bits[j])
-
-    def begin(self):
-        self.came = [self.start(0), self.start(1)]
-        return self
+    def begin(self, others=()):
+        self.came = []
+        if not self.plain:
+            away = after([away for away, _ in self.halves], others)
+            self.came = [swap(v, "dp", bit) for v, bit in zip(away, self.bits, strict=True)]
+
+    def next(self, others=()):
+        self.last = []
+        if not self.plain:
+            onward = after(self.onward, others)
+            self.last = [
+                swap(v, "dp", 3 - bit) for v, bit in zip(onward, self.bits, strict=True)
+            ]
 
     def add(self, order):
         self.stage += 1
@@ -301,11 +329,17 @@
             ]
             return onward
 
-        onward = order(step, stays, self.came)
-        self.last = [swap(value, "dp", 3 - bit) for value, bit in zip(onward, self.bits, strict=True)]
+        self.onward = order(step, stays, self.came)
 
     def add2(self, order):
         stays = [stay for _, stay in self.halves]
+
+        def sums(stays, came, last):
+            size = stays[0].shape[0] // 2
+            return [
+                (stay[:size].astype(F32) + new[:size].astype(F32) + more.astype(F32)).astype(LOW)
+                for stay, new, more in zip(stays, came, last, strict=True)
+            ]
 
         def step(stays, came, last):
             size = stays[0].shape[0] // 2
@@ -318,10 +352,19 @@
             size = size // 2
             return both[:, size:].astype(LOW), both[:, :size]
 
+        if not self.relative:
+            parts = order(sums, stays, self.came, self.last)
+            self.parts = [
+                lax.psum_scatter(part, "seq", scatter_dimension=0, tiled=True) for part in parts
+            ]
+            return
         away, self.kept = order(step, stays, self.came, self.last)
         self.came = swap(away, "seq", 1)
 
     def add3(self, order):
+        if not self.relative:
+            return
+
         def step(kept, came):
             both = kept + came.astype(F32)
             size = both.shape[1] // 2
@@ -331,6 +374,11 @@
         self.came = swap(away, "seq", 2)
 
     def add4(self, order):
+        if not self.relative:
+            self.out = order(
+                lambda *parts: [part.astype(F32) * self.factor for part in parts], *self.parts
+            )
+            return
         self.out = order(
             lambda kept, came: (kept + came.astype(F32)) * self.factor, self.kept, self.came
         )
@@ -379,6 +427,28 @@
 
 def back_start(value):
     return trade_start(value[value.shape[0] // 2 :].astype(LOW))
+
+
+def back_starts(*values):
+    halves = [value[value.shape[0] // 2 :].astype(LOW) for value in values]
+    core, size = lax.axis_index("mp"), halves[0].shape[0] // 2
+    parts = [lax.dynamic_slice_in_dim(half, core * size, size, 0) for half in halves]
+    return swap(jnp.stack(parts), "seq", 2)
+
+
+def back_ends(values, part):
+    rest = swap(part, "mp", 1)
+    core, row = lax.axis_index("mp"), lax.axis_index("seq") // 2
+    came = jnp.where(
+        core == 0,
+        jnp.concatenate([part, rest], axis=1),
+        jnp.concatenate([rest, part], axis=1),
+    )
+    result = []
+    for i, value in enumerate(values):
+        kept, new = value[: value.shape[0] // 2], came[i].astype(value.dtype)
+        result.append(jnp.where(row == 0, jnp.stack([kept, new]), jnp.stack([new, kept])))
+    return result
 
 
 def back_end(value, part):
@@ -731,12 +801,12 @@
     )(grad, values, *parts, gain, *extra)
 
 
-def weight_grad_one(left, right, order):
-    return weight_grad([(left, right)], order)
-
-
-def weight_grad_two(one, two, order):
-    return weight_grad([one, two], order)
+def weight_grad_one(left, right, order, extra=None):
+    return weight_grad([(left, right)], order, extra)
+
+
+def weight_grad_two(one, two, order, extra=None):
+    return weight_grad([one, two], order, extra)
 
 
 def attend_leave_apart(dq, own, came, wq, wkv):
@@ -755,23 +825,9 @@
     return value, value.astype(LOW)
 
 
-def norm_halves(norm_rows, width):
-    count = norm_rows.shape[0]
-    cols = jnp.pad(norm_rows.T, ((0, 0), (0, LANES - count)))
-    result = []
-    for first in (2, 1):
-        quarters = cols.reshape(4, -1, LANES)
-        blocks = [pick(quarters, block_order(first)[i]) for i in range(4)]
-        if lax.axis_size("dp") == 4:
-            n_seq, here = lax.axis_size("seq"), lax.axis_index("seq")
-            blocks = [
-                pick(block.reshape(n_seq, -1, LANES), here ^ k)
-                for block in blocks
-                for k in seq_order()
-            ]
-        block = jnp.concatenate(blocks, axis=0)
-        result.append((block[: width // 2], block[width // 2 :]))
-    return result
+def norm_columns(*norm_rows):
+    rows = jnp.concatenate(norm_rows, axis=0).astype(LOW)
+    return jnp.pad(rows.T, ((0, 0), (0, LANES - rows.shape[0])))
 
 
 def token_counts(lengths, groups):
@@ -810,13 +866,14 @@
 def attn_shard(qkv, out):
     pair = jnp.concatenate([qkv[1], qkv[2]], axis=1)
     side = jnp.concatenate([qkv[0], out.T], axis=1)
-    return jnp.stack([pair, side])
+    return [pair, side]
 
 
 def qkv_out(both):
-    width = both.shape[2] // 2
-    qkv = jnp.stack([both[1, :, :width], both[0, :, :width], both[0, :, width:]])
-    return qkv, both[1, :, width:].T
+    pair, side = both[0], both[1]
+    width = side.shape[1] // 2
+    qkv = jnp.stack([side[:, :width], pair[:, :width], pair[:, width:]])
+    return qkv, side[:, width:].T
 
 
 def project(left, right):
@@ -859,96 +916,87 @@
 
     norms = jnp.concatenate([enc_gains, enc_biases, dec_gains, dec_biases], axis=0)
     n_norms = norms.shape[0]
-    extra = jnp.pad(norms.T[None], ((0, 1), (0, 0), (0, LANES - n_norms)))
+    extra = jnp.pad(norms.T, ((0, 0), (0, LANES - n_norms)))
+    enc_pair, enc_side = attn_shard(enc_qkv, enc_out)
     shards = [
-        jnp.concatenate([attn_shard(enc_qkv, enc_out), extra], axis=2),
-        attn_shard(dec_self_qkv, dec_outs[0]),
-        jnp.stack([enc_up, enc_down.T]),
-        attn_shard(dec_cross_qkv, dec_outs[1]),
-        jnp.stack([dec_up, dec_down.T]),
+        [jnp.concatenate([v, extra], axis=1) for v in (enc_pair, enc_side)],
+        [
+            jnp.concatenate(attn_shard(dec_self_qkv, dec_outs[0]), axis=1),
+            jnp.concatenate(attn_shard(dec_cross_qkv, dec_outs[1]), axis=1),
+        ],
+        [enc_up, enc_down.T],
+        [dec_up, dec_down.T],
     ]
     attn_cuts = [(0, 0, 2 * half), (1, 0, half), (1, half, half)]
+    both_cuts = [
+        (j, first, wide)
+        for j in range(2)
+        for first, wide in ((0, 2 * half), (2 * half, half), (3 * half, half))
+    ]
     feed_cuts = [(0, 0, hidden), (1, 0, hidden)]
     counts, counted = token_counts(lengths, groups)
-    one, two, three, four, five = [Gather(shard) for shard in shards]
+    one = Gather(shards[0], True)
     one.along()
-    two.along([one.came])
+    two, three, four = [Gather(shard, False, [one.came]) for shard in shards[1:]]
     one.join(order)
     one.along()
-    src_part = pair_start(src, [two.came])
-    three.along([two.came])
-    two.join(order)
     one.join(order)
     one.across([counted])
-    two.along([one.column])
-    y_first, x_first = order(lambda: (row_order(2), row_order(1)))
-    two.join(order)
-    two.across(one.near)
-    three.join(order)
-    three.along([two.column])
-    four.along([three.column])
-    x_src = order(pair_end, src, src_part)
+    src_part = pair_start(src, [one.column])
+    y_first, x_first = order(lambda: (row_order(2, True), row_order(1, True)))
     one.far(order)
     offsets, tok_weight, all_tokens = order(
         token_tables, lengths, groups, counts, full_len, quarter
     )
     same, same_t, causal, causal_t = offsets
     factor = 1.0 / all_tokens
-    three.join(order)
-    four.join(order)
-    four.along()
-    five.along([four.column])
+    two.across(one.last)
     *enc_w, table = one.place(order, attn_cuts + [(0, 2 * half, LANES)])
     table = table[:, :n_norms].T.astype(F32)[:, None]
     e_norm = [(table[i], table[n_enc + i]) for i in range(n_enc)]
     d_norm = [(table[2 * n_enc + i], table[2 * n_enc + n_dec + i]) for i in range(n_dec)]
+    x_src = order(pair_end, src, src_part)
     enc_in, enc_own = order(enter, x_src, (), e_norm[0], enc_w[0])
     enc_peer = swap(enc_own, "seq", 1)
-    tgt_part = pair_start(tgt, [five.came])
+    enc_q = order(project, enc_in, enc_w[1])
+    tgt_part = pair_start(tgt, [enc_q])
     two.far(order)
-    three.across(two.near)
-    enc_q = order(project, enc_in, enc_w[1])
-    four.join(order)
+    three.across(two.last)
     enc_ctx, enc_lse = order(attend, enc_q, enc_own, enc_peer, same)
     enc_part = order(project_out, enc_ctx, enc_w[2])
     enc_other = other_core(enc_part)
-    five.join(order)
-    five.along()
-    self_w = two.place(order, attn_cuts)
     x_tgt = order(pair_end, tgt, tgt_part)
-    cot_part = pair_start(cotangent, [x_tgt])
+    weights = two.place(order, both_cuts)
+    self_w, cross_w = weights[:3], weights[3:]
     self_in, self_own = order(enter, x_tgt, (), d_norm[0], self_w[0])
     self_peer = swap(self_own, "seq", 1)
     self_q = order(project, self_in, self_w[1])
+    cot_part = pair_start(cotangent, [self_q])
     three.far(order)
-    four.across(three.near)
+    four.across(three.last)
     self_ctx, self_lse = order(attend, self_q, self_own, self_peer, causal)
     self_part = order(project_out, self_ctx, self_w[2])
     self_other = other_core(self_part)
-    five.join(order)
     cot = order(pair_end, cotangent, cot_part)
     out_grad, out_low = order(
         lambda cot, weight: low_too(cot.astype(F32) * weight[:, None]), cot, tok_weight
     )
     e_up, e_down = three.place(order, feed_cuts)
-    four.far(order)
-    five.across(four.near)
     enc_normed, enc_mid, enc_act, enc_slope, mem_part = order(
         feed, x_src, (enc_part, enc_other), e_norm[1], e_up, e_down
     )
     mem_other = other_core(mem_part)
-    cross_w = four.place(order, attn_cuts)
     source, cross_own = order(enter, enc_mid, (mem_part, mem_other), None, cross_w[0])
     cross_peer = swap(cross_own, "seq", 1)
     cross_in, cross_q, dec_mid = order(
         enter, x_tgt, (self_part, self_other), d_norm[1], cross_w[1]
     )
     cross_q = cross_q[0]
-    five.far(order)
+    four.far(order)
     cross_ctx, cross_lse = order(attend, cross_q, cross_own, cross_peer, same)
     cross_part = order(project_out, cross_ctx, cross_w[2])
     cross_other = other_core(cross_part)
-    d_up, d_down = five.place(order, feed_cuts)
+    d_up, d_down = four.place(order, feed_cuts)
     dec_normed, dec_cross, dec_act, dec_slope, dec_part = order(
         feed, dec_mid, (cross_part, cross_other), d_norm[2], d_up, d_down
     )
@@ -958,7 +1006,8 @@
     parts = (part, other_core(part))
     down_g = order(weight_grad_one, out_low, dec_act, x_first)
     up_g = order(weight_grad_one, dec_normed, pre_grad, y_first)
-    d_feed = Scatter(up_g, down_g, factor).begin()
+    d_feed = Scatter(up_g, down_g, factor)
+    d_feed.begin()
     cross_g, norm_five, low, ctx_grad = order(
         norm_back, out_grad, dec_cross, parts, d_norm[2][0], cross_w[2]
     )
@@ -973,31 +1022,34 @@
         dec_part,
         dec_other,
     )
-    decoded_part = back_start(decoded)
-    d_feed.add(order)
     pair_low, part = order(attend_leave_apart, dq, own_grad, came, cross_w[1], cross_w[0])
     other = other_core(part)
     pair_g = order(weight_grad_one, source, pair_low, y_first)
-    cross = Scatter(pair_g, side_g, factor).begin()
+    cross = Scatter(pair_g, side_g, factor)
+    cross.begin(d_feed.came)
+    d_feed.add(order)
     memory_grad, memory_low = order(
         lambda one, two: low_too(one[1].astype(F32) + two[1].astype(F32)), part, other
     )
-    memory_part = back_start(memory_low)
     cross_parts = (part[0], other[0])
     pre_grad, enc_part = order(feed_back, memory_low, enc_slope, e_up, e_down)
     enc_parts = (enc_part, other_core(enc_part))
     down_g = order(weight_grad_one, memory_low, enc_act, x_first)
+    d_feed.next(cross.came)
+    cross.add(order)
     up_g = order(weight_grad_one, enc_normed, pre_grad, y_first)
-    e_feed = Scatter(up_g, down_g, factor).begin()
+    e_feed = Scatter(up_g, down_g, factor)
+    e_feed.begin(d_feed.last)
+    order.wait(d_feed.last)
     mid_g, norm_four, low, ctx_grad = order(
         norm_back, cross_g, dec_mid, cross_parts, d_norm[1][0], self_w[2]
     )
-    d_feed.add(order)
-    cross.add(order)
     dq, own_grad, peer_grad = order(
         attend_back, self_q, self_own, self_peer, ctx_grad, self_lse, causal_t
     )
     came = swap(peer_grad, "seq", 1)
+    d_feed.add(order)
+    cross.next(e_feed.came)
     enc_mid_g, norm_two, enc_low, enc_ctx_grad = order(
         norm_back, memory_grad, enc_mid, enc_parts, e_norm[1][0], enc_w[2]
     )
@@ -1008,53 +1060,52 @@
     e_feed.add(order)
     pair_low, part = order(attend_leave_joined, dq, own_grad, came, self_w[1], self_w[0])
     parts = (part, other_core(part))
+    d_feed.add(order)
     side_g = order(weight_grad_two, (self_in, dq), (low, self_ctx), x_first)
     pair_g = order(weight_grad_one, self_in, pair_low, y_first)
-    self_s = Scatter(pair_g, side_g, factor).begin()
-    d_feed.add(order)
+    self_s = Scatter(pair_g, side_g, factor)
+    e_feed.next(cross.last)
     cross.add(order)
-    side_g = order(weight_grad_two, (enc_in, enc_dq), (enc_low, enc_ctx), x_first)
+    tgt_grad, norm_three = order(norm_back_last, mid_g, x_tgt, parts, d_norm[0][0])
     pair_low, part = order(
         attend_leave_joined, enc_dq, enc_own_grad, enc_came, enc_w[1], enc_w[0]
     )
     enc_parts = (part, other_core(part))
-    pair_g = order(weight_grad_one, enc_in, pair_low, y_first)
-    enc = Scatter(pair_g, side_g, factor).begin()
+    d_feed.add(order)
+    self_s.begin(e_feed.last)
     e_feed.add(order)
-    tgt_grad, norm_three = order(norm_back_last, mid_g, x_tgt, parts, d_norm[0][0])
-    tgt_part = back_start(tgt_grad)
+    src_grad, norm_one = order(norm_back_last, enc_mid_g, x_src, enc_parts, e_norm[0][0])
+    columns = order(norm_columns, norm_one, norm_two, norm_three, norm_four, norm_five)
+    side_g = order(weight_grad_two, (enc_in, enc_dq), (enc_low, enc_ctx), x_first, columns)
+    pair_g = order(weight_grad_one, enc_in, pair_low, y_first, columns)
+    enc = Scatter(pair_g, side_g, factor)
+    cross.add(order)
+    enc.begin(self_s.came)
     self_s.add(order)
-    src_grad, norm_one = order(norm_back_last, enc_mid_g, x_src, enc_parts, e_norm[0][0])
-    src_part = back_start(src_grad)
-    norm_grads = [norm_one, norm_two, norm_three, norm_four, norm_five]
-    norm_rows = jnp.stack(
-        [norm_grads[i][j] for i, j in ((0, 0), (1, 0), (0, 1), (1, 1))]
-        + [norm_grads[i][j] for j in (0, 1) for i in (2, 3, 4)]
-    ).astype(LOW)
-    small = Scatter(*order(norm_halves, norm_rows, width), factor).begin()
-    decoded = order(back_end, decoded, decoded_part)
-    memory_grad = order(back_end, memory_grad, memory_part)
+    e_feed.add(order)
+    self_s.next(enc.came)
+    enc.add(order)
+    enc.next(self_s.last)
     cross.add(order)
-    d_feed.add(order)
-    enc.add(order)
-    small.add(order)
-    e_feed.add(order)
-    self_s.add(order)
-    cross.add(order)
-    enc.add(order)
-    small.add(order)
-    tgt_grad = order(back_end, tgt_grad, tgt_part)
     self_s.add(order)
     e_feed.add(order)
     enc.add(order)
-    small.add(order)
-    src_grad = order(back_end, src_grad, src_part)
+    src_part = back_start(src_grad)
+    three_part = back_starts(decoded, memory_low, tgt_grad)
     self_s.add(order)
     enc.add(order)
-    small.add(order)
-
-    norm_out = small.out[0][:, :n_norms].T
-    enc_qkv_g, enc_out_g = qkv_out(enc.out)
+    src_grad = order(back_end, src_grad, src_part)
+    decoded, memory_grad, tgt_grad = order(
+        back_ends, (decoded, memory_grad, tgt_grad), three_part
+    )
+    self_s.add(order)
+    enc.add(order)
+
+    norm_out = enc.out[0][:, 2 * half : 2 * half + n_norms].T
+    rows_of = [2 * j + i for i in range(2) for j in range(n_enc)]
+    rows_of += [2 * (n_enc + j) + i for i in range(2) for j in range(n_dec)]
+    norm_out = jnp.stack([norm_out[i] for i in rows_of])
+    enc_qkv_g, enc_out_g = qkv_out([part[:, : 2 * half] for part in enc.out])
     self_qkv_g, self_out_g = qkv_out(self_s.out)
     cross_qkv_g, cross_out_g = qkv_out(cross.out)
     return (

time: 840 us -> 767 us (0.913)
  waiting for transfers between devices: 345 us -> 292 us
  starting transfers between devices: 97.5 us -> 83.2 us
  local copies, waits for them, and re-layouts: 89.4 us -> 78.3 us
    ppermute x98 -> x76, waiting for transfers between devices: 345 us -> 292 us  [swap(): return lax.ppermute(value, axis, xor_perm(lax.axis_size(axis), bits))]
    unnamed x401 -> x308, local copies, waits for them, and re-layouts: 54.4 us -> 36.9 us
    ppermute x98 -> x76, starting transfers between devices: 97.5 us -> 83.1 us  [swap(): return lax.ppermute(value, axis, xor_perm(lax.axis_size(axis), bits))]
    concatenate x10 -> x2, local copies, waits for them, and re-layouts: 10.2 us -> 0.89 us  [join(): jnp.concatenate([one, two], axis=1)]
    convert_element_type x12 -> x10, other arithmetic: 19.9 us -> 15.3 us  [step(): (stay[size:].astype(F32) + new[size:].astype(F32)).astype(LOW)]
    pallas_call x5 -> x4, Pallas kernels: 18.7 us -> 15.6 us  [place(): pl.pallas_call(body, out_shape=[shaped((total, width), LOW) for _, _, wid...]
    another operation x18 -> x15, other arithmetic: 17.9 us -> 15.6 us  [step(): jnp.stack([stay[:size].astype(F32) + new[:size].astype(F32) + more.astype...]
  transfers between devices with their start and end apart: 98 -> 79, of which waited for: 40 -> 32; matrix products, arithmetic and copies ran while one was open for 14% -> 15% of each run, Pallas kernels for 20% -> 24%
where the time goes in v3:
time: 767 us; the launch traced here: 755 us
  waiting for transfers between devices  292 us (38%)
  Pallas kernels  202 us (26%)
  starting transfers between devices  83.2 us (11%)
  local copies, waits for them, and re-layouts  78.3 us (10%)
  other arithmetic  75.6 us (10%)
  between operations  16.6 us (2%)
    ppermute x76, waiting for transfers between devices, swap(): return lax.ppermute(value, axis, xor_perm(lax.axis_size(axis), bits))  292 us
    ppermute x76, starting transfers between devices, swap(): return lax.ppermute(value, axis, xor_perm(lax.axis_size(axis), bits))  83.1 us
    pallas_call x3, Pallas kernels, attend_back(): pl.pallas_call(attend_back_body, grid=(width // LANES,), in_specs=[spec]...  46 us
    pallas_call x10, Pallas kernels, weight_grad(): pl.pallas_call(body, grid_spec=pltpu.PrefetchScalarGridSpec(num_scalar_pr...  39.7 us
    unnamed x308, local copies, waits for them, and re-layouts  36.9 us
    pallas_call x3, Pallas kernels, attend(): pl.pallas_call(functools.partial(attend_body, 256), grid=(width // LANES,...  28.1 us
    pallas_call x2, Pallas kernels, feed(): pl.pallas_call(body, grid=(hidden // TILE,), in_specs=[same, same, same,...  24.6 us
    pallas_call x2, Pallas kernels, feed_back(): pl.pallas_call(body, grid=(hidden // TILE,), in_specs=[same, block, weigh...  18 us
  transfers between devices with their start and end apart: 79, of which 32 were waited for; matrix products, arithmetic and copies ran while one was open for 15% of the time, Pallas kernels for 24%

profile of v3, /device:TPU:0, one launch (start us, length us, event | category | flops | bytes accessed | tf_op | source)
XLA Modules:
  0.0 755.4 jit_solution(14317952374185031652)
XLA Ops:
  20.0 10.3 %collective-permute-done = bf16[2,64,1152]{2,1,0:T(8,128)(2,1)S(1)} collective-permute-done((bf16[2,64,1152]{2,1,0:T(8,128)(2,1)S(1)}, bf16[2,64,1152]{2,1,0:T(8,128)(2,1)S(1)}, u32[]{:S(2)}, u32[]{:S(2)}) %collective-permute-start) | collective-permute-done | bytes 294944 | tf_op jit(solution)/shard_map/ppermute | solution.py:37
  32.9 26.9 %collective-permute-done.1 = bf16[2,128,1152]{2,1,0:T(8,128)(2,1)S(1)} collective-permute-done((bf16[2,128,1152]{2,1,0:T(8,128)(2,1)S(1)}, bf16[2,128,1152]{2,1,0:T(8,128)(2,1)S(1)}, u32[]{:S(2)}, u32[]{:S(2)}) %collective-permute-start.1) | collective-permute-done | bytes 589856 | tf_op jit(solution)/shard_map/ppermute | solution.py:37
  68.1 7.6 %collective-permute-start.2 = (bf16[128,1024]{1,0:T(8,128)(2,1)}, bf16[128,1024]{1,0:T(8,128)(2,1)}, u32[]{:S(2)}, u32[]{:S(2)}) collective-permute-start(bf16[128,1024]{1,0:T(8,128)(2,1)} %constant_dynamic-slice_fusion.4), channel_id=1, source_target_pairs={{0,4},{2,6},{4,0},{6,2},{1,5},{3,7},{5,1},{7,3},{8,12},{10,14},{12... | collective-permute-start | bytes 786440 | tf_op jit(solution)/shard_map/ppermute | solution.py:37
  75.7 7.8 %collective-permute-done.6.refs_2_ = bf16[2,256,1152]{2,1,0:T(8,128)(2,1)S(1)} collective-permute-done((bf16[2,256,1152]{2,1,0:T(8,128)(2,1)}, bf16[2,256,1152]{2,1,0:T(8,128)(2,1)S(1)}, u32[]{:S(2)}, u32[]{:S(2)}) %collective-permute-start.6) | collective-permute-done | bytes 1179680 | tf_op jit(solution)/shard_map/ppermute | solution.py:37
  83.6 3.5 collective-permute-done.5.refs_1_
  89.6 15.8 %collective-permute-done.8.refs_4_ = bf16[256,1152]{1,0:T(8,128)(2,1)} collective-permute-done((bf16[256,1152]{1,0:T(8,128)(2,1)}, bf16[256,1152]{1,0:T(8,128)(2,1)}, u32[]{:S(2)}, u32[]{:S(2)}) %collective-permute-start.8) | collective-permute-done | bytes 589856 | tf_op jit(solution)/shard_map/ppermute | solution.py:37
  114.9 3.3 shard_map.359
  125.7 3.2 shard_map.360
  130.4 13.8 %collective-permute-done.13.refs_2_ = bf16[2,256,2048]{2,1,0:T(8,128)(2,1)} collective-permute-done((bf16[2,256,2048]{2,1,0:T(8,128)(2,1)}, bf16[2,256,2048]{2,1,0:T(8,128)(2,1)}, u32[]{:S(2)}, u32[]{:S(2)}) %collective-permute-start.13) | collective-permute-done | bytes 2097184 | tf_op jit(solution)/shard_map/ppermute | solution.py:37
  151.2 20.3 %collective-permute-done.16.refs_4_ = bf16[256,2048]{1,0:T(8,128)(2,1)} collective-permute-done((bf16[256,2048]{1,0:T(8,128)(2,1)}, bf16[256,2048]{1,0:T(8,128)(2,1)}, u32[]{:S(2)}, u32[]{:S(2)}) %collective-permute-start.16) | collective-permute-done | bytes 1048608 | tf_op jit(solution)/shard_map/ppermute | solution.py:37
  181.9 4.9 collective-permute-start.10
  187.8 9.8 %shard_map.361 = (bf16[512,512]{1,0:T(8,128)(2,1)S(1)}, f32[512,512]{1,0:T(8,128)S(1)}) custom-call(bf16[512,512]{1,0:T(8,128)(2,1)S(1)} %copy-done.63, bf16[2,512,512]{2,1,0:T(8,128)(2,1)} %get-tuple-element.712.ko_ref.vo_ref, bf16[2,512,512]{2,1,0:T(8,128)(2,1)} %collective-permute-done.11.kp_ref.vp_ref, ...), custom_call_target="tpu_custom_call" | custom-call | flops 1 | bytes 1 | tf_op jit(solution)/shard_map/pallas_call | solution.py:543
  203.1 4.8 shard_map.362
  222.3 3.8 collective-permute-start.24
  226.1 30.9 %collective-permute-done.17.kp_ref.vp_ref = bf16[2,512,512]{2,1,0:T(8,128)(2,1)S(1)} collective-permute-done((bf16[2,512,512]{2,1,0:T(8,128)(2,1)S(1)}, bf16[2,512,512]{2,1,0:T(8,128)(2,1)S(1)}, u32[]{:S(2)}, u32[]{:S(2)}) %collective-permute-start.17) | collective-permute-done | bytes 1048608 | tf_op jit(solution)/shard_map/ppermute | solution.py:37
  257.1 9.1 %shard_map.364 = (bf16[512,512]{1,0:T(8,128)(2,1)S(1)}, f32[512,512]{1,0:T(8,128)S(1)}) custom-call(bf16[512,512]{1,0:T(8,128)(2,1)S(1)} %convolution_convert_fusion.3.q_ref, bf16[2,512,512]{2,1,0:T(8,128)(2,1)S(1)} %get-tuple-element.685.ko_ref.vo_ref, bf16[2,512,512]{2,1,0:T(8,128)(2,1)S(1)} %collective-permute-done.17.kp_ref.vp_ref, ...), custom_call_target="tpu_custom_call" | custom-call | flops 1 | bytes 1 | tf_op jit(solution)/shard_map/pallas_call | solution.py:543
  277.9 4.0 shard_map.365
  285.9 12.0 %shard_map.366 = (bf16[512,1024]{1,0:T(8,128)(2,1)S(1)}, f32[512,1024]{1,0:T(8,128)}, bf16[512,2048]{1,0:T(8,128)(2,1)}, bf16[512,2048]{1,0:T(8,128)(2,1)}, bf16[512,1024]{1,0:T(8,128)(2,1)S(1)}) custom-call(bf16[512,1024]{1,0:T(8,128)(2,1)S(1)} %copy-done.4, bf16[512,1024]{1,0:T(8,128)(2,1)} %convolution_convert_fusion.2.one_ref, ...), custom_call_target="tpu_custom_call" | custom-call | flops 1 | bytes 1 | tf_op jit(solution)/shard_map/pallas_call | solution.py:694
  306.7 9.9 %collective-permute-done.29.refs_2_ = bf16[2,256,2048]{2,1,0:T(8,128)(2,1)} collective-permute-done((bf16[2,256,2048]{2,1,0:T(8,128)(2,1)}, bf16[2,256,2048]{2,1,0:T(8,128)(2,1)}, u32[]{:S(2)}, u32[]{:S(2)}) %collective-permute-start.29) | collective-permute-done | bytes 2097184 | tf_op jit(solution)/shard_map/ppermute | solution.py:37
  322.6 7.8 %collective-permute-done.27.kp_ref.vp_ref = bf16[2,512,512]{2,1,0:T(8,128)(2,1)S(1)} collective-permute-done((bf16[2,512,512]{2,1,0:T(8,128)(2,1)S(1)}, bf16[2,512,512]{2,1,0:T(8,128)(2,1)S(1)}, u32[]{:S(2)}, u32[]{:S(2)}) %collective-permute-start.27) | collective-permute-done | bytes 1048608 | tf_op jit(solution)/shard_map/ppermute | solution.py:37
  330.4 9.2 %shard_map.369 = (bf16[512,512]{1,0:T(8,128)(2,1)S(1)}, f32[512,512]{1,0:T(8,128)S(1)}) custom-call(bf16[512,512]{1,0:T(8,128)(2,1)S(1)} %bitcast.191, bf16[2,512,512]{2,1,0:T(8,128)(2,1)S(1)} %get-tuple-element.612.ko_ref.vo_ref, bf16[2,512,512]{2,1,0:T(8,128)(2,1)S(1)} %collective-permute-done.27.kp_ref.vp_ref, ...), custom_call_target="tpu_custom_call" | custom-call | flops 1 | bytes 1 | tf_op jit(solution)/shard_map/pallas_call | solution.py:543
  349.4 3.5 shard_map.370
  356.9 12.5 %shard_map.371 = (bf16[512,1024]{1,0:T(8,128)(2,1)S(1)}, f32[512,1024]{1,0:T(8,128)}, bf16[512,2048]{1,0:T(8,128)(2,1)}, bf16[512,2048]{1,0:T(8,128)(2,1)}, bf16[512,1024]{1,0:T(8,128)(2,1)S(1)}) custom-call(f32[512,1024]{1,0:T(8,128)} %copy-done.32, bf16[512,1024]{1,0:T(8,128)(2,1)} %convolution_convert_fusion.one_ref, ...), custom_call_target="tpu_custom_call" | custom-call | flops 1 | bytes 1 | tf_op jit(solution)/shard_map/pallas_call | solution.py:694
  369.4 8.2 %shard_map.372 = (bf16[512,2048]{1,0:T(8,128)(2,1)S(1)}, bf16[512,1024]{1,0:T(8,128)(2,1)S(1)}) custom-call(bf16[512,1024]{1,0:T(8,128)(2,1)S(1)} %copy-done.22, bf16[512,2048]{1,0:T(8,128)(2,1)} %get-tuple-element.586.slope_ref, bf16[1024,2048]{1,0:T(8,128)(2,1)} %copy-done.10, bf16[1024,2048]{1,0:T(8,128)(2,1)} %copy-done.11), custom_call_target="tpu_custom_call" | custom-call | flops 1 | bytes 1 | tf_op jit(solution)/shard_map/pallas_call | solution.py:738
  378.2 4.1 shard_map.373
  382.3 5.1 shard_map.374
  392.9 14.9 %shard_map.376 = (bf16[512,512]{1,0:T(8,128)(2,1)S(1)}, bf16[2,512,512]{2,1,0:T(8,128)(2,1)S(1)}, bf16[2,512,512]{2,1,0:T(8,128)(2,1)S(1)}) custom-call(bf16[512,512]{1,0:T(8,128)(2,1)S(1)} %bitcast.192, bf16[2,512,512]{2,1,0:T(8,128)(2,1)S(1)} %copy-done.17, bf16[2,512,512]{2,1,0:T(8,128)(2,1)S(1)} %copy-done.19, bf16[2,512,512]{2,1,0:T(8,128)(2,1)S(1)} %copy-done.17, ...), custom_call_target="tpu_custom_call" | custom-call | flops 1 | bytes 1 | tf_op jit(solution)/shard_map/pallas_call | solution.py:598
  411.0 3.1 add_convert_fusion.4
  414.2 18.3 %collective-permute-done.35.came_ref = bf16[2,512,512]{2,1,0:T(8,128)(2,1)S(1)} collective-permute-done((bf16[2,512,512]{2,1,0:T(8,128)(2,1)S(1)}, bf16[2,512,512]{2,1,0:T(8,128)(2,1)S(1)}, u32[]{:S(2)}, u32[]{:S(2)}) %collective-permute-start.35) | collective-permute-done | bytes 1048608 | tf_op jit(solution)/shard_map/ppermute | solution.py:37
  432.5 3.2 shard_map.378
  446.7 17.5 %collective-permute-done.39 = bf16[512,1024]{1,0:T(8,128)(2,1)S(1)} collective-permute-done((bf16[512,1024]{1,0:T(8,128)(2,1)S(1)}, bf16[512,1024]{1,0:T(8,128)(2,1)S(1)}, u32[]{:S(2)}, u32[]{:S(2)}) %collective-permute-start.39) | collective-permute-done | bytes 1048608 | tf_op jit(solution)/shard_map/ppermute | solution.py:37
  471.8 9.8 %shard_map.380 = (bf16[512,2048]{1,0:T(8,128)(2,1)S(1)}, bf16[512,1024]{1,0:T(8,128)(2,1)}) custom-call(bf16[512,1024]{1,0:T(8,128)(2,1)S(1)} %get-tuple-element.659.low_ref.refs_0_, bf16[512,2048]{1,0:T(8,128)(2,1)} %get-tuple-element.651.slope_ref, bf16[1024,2048]{1,0:T(8,128)(2,1)} %copy-done.8, bf16[1024,2048]{1,0:T(8,128)(2,1)} %copy-done.9), custom_call_target="tpu_custom_call" | custom-call | flops 1 | bytes 1 | tf_op jit(solution)/shard_map/pallas_call | solution.py:738
  481.7 5.1 shard_map.381
  488.8 5.2 shard_map.382
  505.2 15.1 %shard_map.384 = (bf16[512,512]{1,0:T(8,128)(2,1)S(1)}, bf16[2,512,512]{2,1,0:T(8,128)(2,1)S(1)}, bf16[2,512,512]{2,1,0:T(8,128)(2,1)}) custom-call(bf16[512,512]{1,0:T(8,128)(2,1)S(1)} %copy-done.66, bf16[2,512,512]{2,1,0:T(8,128)(2,1)S(1)} %copy-done.13, bf16[2,512,512]{2,1,0:T(8,128)(2,1)S(1)} %copy-done.15, bf16[2,512,512]{2,1,0:T(8,128)(2,1)S(1)} %copy-done.13, ...), custom_call_target="tpu_custom_call" | custom-call | flops 1 | bytes 1 | tf_op jit(solution)/shard_map/pallas_call | solution.py:598
  529.4 4.1 shard_map.385
  533.6 16.0 %shard_map.386 = (bf16[512,512]{1,0:T(8,128)(2,1)S(1)}, bf16[2,512,512]{2,1,0:T(8,128)(2,1)S(1)}, bf16[2,512,512]{2,1,0:T(8,128)(2,1)}) custom-call(bf16[512,512]{1,0:T(8,128)(2,1)S(1)} %copy-done.64, bf16[2,512,512]{2,1,0:T(8,128)(2,1)} %get-tuple-element.712.ko_ref.vo_ref, bf16[2,512,512]{2,1,0:T(8,128)(2,1)} %collective-permute-done.11.kp_ref.vp_ref, ...), custom_call_target="tpu_custom_call" | custom-call | flops 1 | bytes 1 | tf_op jit(solution)/shard_map/pallas_call | solution.py:598
  560.8 8.2 %collective-permute-done.50 = bf16[2,128,2048]{2,1,0:T(8,128)(2,1)} collective-permute-done((bf16[2,128,2048]{2,1,0:T(8,128)(2,1)}, bf16[2,128,2048]{2,1,0:T(8,128)(2,1)}, u32[]{:S(2)}, u32[]{:S(2)}) %collective-permute-start.50) | collective-permute-done | bytes 1048608 | tf_op jit(solution)/shard_map/ppermute | solution.py:37
  572.9 4.0 shard_map.388
  576.9 3.9 shard_map.389
  589.5 13.1 %collective-permute-done.52.came_ref = bf16[2,512,512]{2,1,0:T(8,128)(2,1)S(1)} collective-permute-done((bf16[2,512,512]{2,1,0:T(8,128)(2,1)}, bf16[2,512,512]{2,1,0:T(8,128)(2,1)S(1)}, u32[]{:S(2)}, u32[]{:S(2)}) %collective-permute-start.52) | collective-permute-done | bytes 1048608 | tf_op jit(solution)/shard_map/ppermute | solution.py:37
  628.3 3.2 shard_map.394
  639.3 20.9 %collective-permute-done.62 = bf16[2,128,2048]{2,1,0:T(8,128)(2,1)} collective-permute-done((bf16[2,128,2048]{2,1,0:T(8,128)(2,1)}, bf16[2,128,2048]{2,1,0:T(8,128)(2,1)}, u32[]{:S(2)}, u32[]{:S(2)}) %collective-permute-start.62) | collective-permute-done | bytes 1048608 | tf_op jit(solution)/shard_map/ppermute | solution.py:37
  666.3 16.8 %collective-permute-done.69 = bf16[2,64,1024]{2,1,0:T(8,128)(2,1)S(1)} collective-permute-done((bf16[2,64,1024]{2,1,0:T(8,128)(2,1)S(1)}, bf16[2,64,1024]{2,1,0:T(8,128)(2,1)S(1)}, u32[]{:S(2)}, u32[]{:S(2)}) %collective-permute-start.69) | collective-permute-done | bytes 262176 | tf_op jit(solution)/shard_map/ppermute | solution.py:37
  684.9 9.6 %collective-permute-done.65 = bf16[256,1024]{1,0:T(8,128)(2,1)S(1)} collective-permute-done((bf16[256,1024]{1,0:T(8,128)(2,1)S(1)}, bf16[256,1024]{1,0:T(8,128)(2,1)S(1)}, u32[]{:S(2)}, u32[]{:S(2)}) %collective-permute-start.65) | collective-permute-done | bytes 524320 | tf_op jit(solution)/shard_map/ppermute | solution.py:37
  700.4 4.7 collective-permute-done.66
  708.2 8.6 %collective-permute-done.71 = bf16[2,128,1024]{2,1,0:T(8,128)(2,1)S(1)} collective-permute-done((bf16[2,128,1024]{2,1,0:T(8,128)(2,1)S(1)}, bf16[2,128,1024]{2,1,0:T(8,128)(2,1)S(1)}, u32[]{:S(2)}, u32[]{:S(2)}) %collective-permute-start.71) | collective-permute-done | bytes 524320 | tf_op jit(solution)/shard_map/ppermute | solution.py:37
  718.9 10.1 %collective-permute-done.70 = bf16[2,128,1152]{2,1,0:T(8,128)(2,1)S(1)} collective-permute-done((bf16[2,128,1152]{2,1,0:T(8,128)(2,1)S(1)}, bf16[2,128,1152]{2,1,0:T(8,128)(2,1)S(1)}, u32[]{:S(2)}, u32[]{:S(2)}) %collective-permute-start.70) | collective-permute-done | bytes 589856 | tf_op jit(solution)/shard_map/ppermute | solution.py:37
  (655 shorter events, 270.9 us)
Async XLA Ops:
  7.2 98.2 %all-gather.4.cloned.1.call-start = ((), (), s32[]{:S(2)}) async-start(), calls=%async_computation | async-start | bytes 2621440 | tf_op jit(solution)/shard_map/all_gather | solution.py:173
  30.3 120.9 %all-gather.6.cloned.1.call-start = ((), (), s32[]{:S(2)}) async-start(), calls=%async_computation.1 | async-start | bytes 2621440 | tf_op jit(solution)/shard_map/all_gather | solution.py:173
  30.5 29.3 %collective-permute-start.1 = (bf16[2,128,1152]{2,1,0:T(8,128)(2,1)S(1)}, bf16[2,128,1152]{2,1,0:T(8,128)(2,1)S(1)}, u32[]{:S(2)}, u32[]{:S(2)}) collective-permute-start(bf16[2,128,1152]{2,1,0:T(8,128)(2,1)S(1)} %constant_dynamic-update-slice_fusion), channel_id=1, source_target_pairs={{0,2},{2,0},{4,6},{6,4},{1,3},{3,1},{5,7},{7,5},{8,10},{10,8},{12,... | collective-permute-start | bytes 1769480 | tf_op jit(solution)/shard_map/ppermute | solution.py:37
  31.3 30.2 %collective-permute-start.4 = (f32[8,128]{1,0:T(8,128)S(1)}, f32[8,128]{1,0:T(8,128)S(1)}, u32[]{:S(2)}, u32[]{:S(2)}) collective-permute-start(f32[8,128]{1,0:T(8,128)S(1)} %pad_add_fusion.2), channel_id=1, source_target_pairs={{0,16},{8,24},{16,0},{24,8},{1,17},{9,25},{17,1},{25,9},{2,18},{10... | collective-permute-start | bytes 12296 | tf_op jit(solution)/shard_map/ppermute | solution.py:37
  66.4 202.2 %all-gather.8.cloned.1.call-start = ((), (), s32[]{:S(2)}) async-start(), calls=%async_computation.2 | async-start | bytes 2621440 | tf_op jit(solution)/shard_map/all_gather | solution.py:173
  68.1 54.2 %collective-permute-start.2 = (bf16[128,1024]{1,0:T(8,128)(2,1)}, bf16[128,1024]{1,0:T(8,128)(2,1)}, u32[]{:S(2)}, u32[]{:S(2)}) collective-permute-start(bf16[128,1024]{1,0:T(8,128)(2,1)} %constant_dynamic-slice_fusion.4), channel_id=1, source_target_pairs={{0,4},{2,6},{4,0},{6,2},{1,5},{3,7},{5,1},{7,3},{8,12},{10,14},{12... | collective-permute-start | bytes 786440 | tf_op jit(solution)/shard_map/ppermute | solution.py:37
  105.4 38.8 %collective-permute-start.13 = (bf16[2,256,2048]{2,1,0:T(8,128)(2,1)}, bf16[2,256,2048]{2,1,0:T(8,128)(2,1)}, u32[]{:S(2)}, u32[]{:S(2)}) collective-permute-start(bf16[2,256,2048]{2,1,0:T(8,128)(2,1)} %all-gather.4.cloned.1.call-done.refs_0_), channel_id=1, source_target_pairs={{0,16},{8,24},{16,0},{24,8},{1,17},{9,25},{17,1},{25,9},{2,18},{10... | collective-permute-start | bytes 6291464 | tf_op jit(solution)/shard_map/ppermute | solution.py:37
  105.8 38.6 %collective-permute-start.12 = (bf16[2,256,2048]{2,1,0:T(8,128)(2,1)}, bf16[2,256,2048]{2,1,0:T(8,128)(2,1)}, u32[]{:S(2)}, u32[]{:S(2)}) collective-permute-start(bf16[2,256,2048]{2,1,0:T(8,128)(2,1)} %all-gather.4.cloned.1.call-done.refs_0_), channel_id=1, source_target_pairs={{0,8},{8,0},{16,24},{24,16},{1,9},{9,1},{17,25},{25,17},{2,10},{10... | collective-permute-start | bytes 6291464 | tf_op jit(solution)/shard_map/ppermute | solution.py:37
  149.5 24.3 %collective-permute-start.15 = (bf16[256,2048]{1,0:T(8,128)(2,1)}, bf16[256,2048]{1,0:T(8,128)(2,1)}, u32[]{:S(2)}, u32[]{:S(2)}) collective-permute-start(bf16[256,2048]{1,0:T(8,128)(2,1)} %slice_bitcast_fusion.10), channel_id=1, source_target_pairs={{0,16},{8,24},{16,0},{24,8},{1,17},{9,25},{17,1},{25,9},{2,18},{10... | collective-permute-start | bytes 3145736 | tf_op jit(solution)/shard_map/ppermute | solution.py:37
  151.2 35.6 %collective-permute-start.11 = (bf16[2,512,512]{2,1,0:T(8,128)(2,1)}, bf16[2,512,512]{2,1,0:T(8,128)(2,1)}, u32[]{:S(2)}, u32[]{:S(2)}) collective-permute-start(bf16[2,512,512]{2,1,0:T(8,128)(2,1)} %get-tuple-element.712.ko_ref.vo_ref), channel_id=1, source_target_pairs={{0,2},{2,0},{4,6},{6,4},{1,3},{3,1},{5,7},{7,5},{8,10},{10,8},{12,... | collective-permute-start | bytes 3145736 | tf_op jit(solution)/shard_map/ppermute | solution.py:37
  173.8 41.4 %collective-permute-start.19 = (bf16[2,256,2048]{2,1,0:T(8,128)(2,1)}, bf16[2,256,2048]{2,1,0:T(8,128)(2,1)}, u32[]{:S(2)}, u32[]{:S(2)}) collective-permute-start(bf16[2,256,2048]{2,1,0:T(8,128)(2,1)} %all-gather.6.cloned.1.call-done.refs_0_), channel_id=1, source_target_pairs={{0,16},{8,24},{16,0},{24,8},{1,17},{9,25},{17,1},{25,9},{2,18},{10... | collective-permute-start | bytes 6291464 | tf_op jit(solution)/shard_map/ppermute | solution.py:37
  175.4 39.8 %collective-permute-start.18 = (bf16[2,256,2048]{2,1,0:T(8,128)(2,1)}, bf16[2,256,2048]{2,1,0:T(8,128)(2,1)}, u32[]{:S(2)}, u32[]{:S(2)}) collective-permute-start(bf16[2,256,2048]{2,1,0:T(8,128)(2,1)} %all-gather.6.cloned.1.call-done.refs_0_), channel_id=1, source_target_pairs={{0,8},{8,0},{16,24},{24,16},{1,9},{9,1},{17,25},{25,17},{2,10},{10... | collective-permute-start | bytes 6291464 | tf_op jit(solution)/shard_map/ppermute | solution.py:37
  211.6 45.5 %collective-permute-start.17 = (bf16[2,512,512]{2,1,0:T(8,128)(2,1)S(1)}, bf16[2,512,512]{2,1,0:T(8,128)(2,1)S(1)}, u32[]{:S(2)}, u32[]{:S(2)}) collective-permute-start(bf16[2,512,512]{2,1,0:T(8,128)(2,1)S(1)} %get-tuple-element.685.ko_ref.vo_ref), channel_id=1, source_target_pairs={{0,2},{2,0},{4,6},{6,4},{1,3},{3,1},{5,7},{7,5},{8,10},{10,8},{12,... | collective-permute-start | bytes 3145736 | tf_op jit(solution)/shard_map/ppermute | solution.py:37
  220.1 48.5 %collective-permute-start.23 = (bf16[256,2048]{1,0:T(8,128)(2,1)}, bf16[256,2048]{1,0:T(8,128)(2,1)}, u32[]{:S(2)}, u32[]{:S(2)}) collective-permute-start(bf16[256,2048]{1,0:T(8,128)(2,1)} %slice_bitcast_fusion.7), channel_id=1, source_target_pairs={{0,8},{8,0},{16,24},{24,16},{1,9},{9,1},{17,25},{25,17},{2,10},{10... | collective-permute-start | bytes 3145736 | tf_op jit(solution)/shard_map/ppermute | solution.py:37
  220.8 47.8 %collective-permute-start.22 = (bf16[256,2048]{1,0:T(8,128)(2,1)}, bf16[256,2048]{1,0:T(8,128)(2,1)}, u32[]{:S(2)}, u32[]{:S(2)}) collective-permute-start(bf16[256,2048]{1,0:T(8,128)(2,1)} %slice_bitcast_fusion.8), channel_id=1, source_target_pairs={{0,16},{8,24},{16,0},{24,8},{1,17},{9,25},{17,1},{25,9},{2,18},{10... | collective-permute-start | bytes 3145736 | tf_op jit(solution)/shard_map/ppermute | solution.py:37
  222.3 45.7 %collective-permute-start.24 = (bf16[128,1024]{1,0:T(8,128)(2,1)S(1)}, bf16[128,1024]{1,0:T(8,128)(2,1)}, u32[]{:S(2)}, u32[]{:S(2)}) collective-permute-start(bf16[128,1024]{1,0:T(8,128)(2,1)S(1)} %constant_dynamic-slice_fusion), channel_id=1, source_target_pairs={{0,4},{2,6},{4,0},{6,2},{1,5},{3,7},{5,1},{7,3},{8,12},{10,14},{12... | collective-permute-start | bytes 786440 | tf_op jit(solution)/shard_map/ppermute | solution.py:37
  268.6 48.0 %collective-permute-start.29 = (bf16[2,256,2048]{2,1,0:T(8,128)(2,1)}, bf16[2,256,2048]{2,1,0:T(8,128)(2,1)}, u32[]{:S(2)}, u32[]{:S(2)}) collective-permute-start(bf16[2,256,2048]{2,1,0:T(8,128)(2,1)} %all-gather.8.cloned.1.call-done.refs_0_), channel_id=1, source_target_pairs={{0,16},{8,24},{16,0},{24,8},{1,17},{9,25},{17,1},{25,9},{2,18},{10... | collective-permute-start | bytes 6291464 | tf_op jit(solution)/shard_map/ppermute | solution.py:37
  270.1 47.6 %collective-permute-start.28 = (bf16[2,256,2048]{2,1,0:T(8,128)(2,1)}, bf16[2,256,2048]{2,1,0:T(8,128)(2,1)}, u32[]{:S(2)}, u32[]{:S(2)}) collective-permute-start(bf16[2,256,2048]{2,1,0:T(8,128)(2,1)} %all-gather.8.cloned.1.call-done.refs_0_), channel_id=1, source_target_pairs={{0,8},{8,0},{16,24},{24,16},{1,9},{9,1},{17,25},{25,17},{2,10},{10... | collective-permute-start | bytes 6291464 | tf_op jit(solution)/shard_map/ppermute | solution.py:37
  305.2 25.2 %collective-permute-start.27 = (bf16[2,512,512]{2,1,0:T(8,128)(2,1)S(1)}, bf16[2,512,512]{2,1,0:T(8,128)(2,1)S(1)}, u32[]{:S(2)}, u32[]{:S(2)}) collective-permute-start(bf16[2,512,512]{2,1,0:T(8,128)(2,1)S(1)} %get-tuple-element.612.ko_ref.vo_ref), channel_id=1, source_target_pairs={{0,2},{2,0},{4,6},{6,4},{1,3},{3,1},{5,7},{7,5},{8,10},{10,8},{12,... | collective-permute-start | bytes 3145736 | tf_op jit(solution)/shard_map/ppermute | solution.py:37
  377.7 33.3 %collective-permute-start.33 = (bf16[512,1024]{1,0:T(8,128)(2,1)S(1)}, bf16[512,1024]{1,0:T(8,128)(2,1)}, u32[]{:S(2)}, u32[]{:S(2)}) collective-permute-start(bf16[512,1024]{1,0:T(8,128)(2,1)S(1)} %get-tuple-element.628), channel_id=1, source_target_pairs={{0,1},{1,0},{2,3},{3,2},{4,5},{5,4},{6,7},{7,6},{8,9},{9,8},{10,11... | collective-permute-start | bytes 3145736 | tf_op jit(solution)/shard_map/ppermute | solution.py:37
  387.5 51.0 %collective-permute-start.37 = (bf16[512,2048]{1,0:T(8,128)(2,1)}, bf16[512,2048]{1,0:T(8,128)(2,1)}, u32[]{:S(2)}, u32[]{:S(2)}) collective-permute-start(bf16[512,2048]{1,0:T(8,128)(2,1)} %get-tuple-element.636), channel_id=1, source_target_pairs={{0,16},{8,24},{16,0},{24,8},{1,17},{9,25},{17,1},{25,9},{2,18},{10... | collective-permute-start | bytes 6291464 | tf_op jit(solution)/shard_map/ppermute | solution.py:37
  388.1 50.4 %collective-permute-start.38 = (bf16[512,2048]{1,0:T(8,128)(2,1)S(1)}, bf16[512,2048]{1,0:T(8,128)(2,1)}, u32[]{:S(2)}, u32[]{:S(2)}) collective-permute-start(bf16[512,2048]{1,0:T(8,128)(2,1)S(1)} %get-tuple-element.637), channel_id=1, source_target_pairs={{0,8},{8,0},{16,24},{24,16},{1,9},{9,1},{17,25},{25,17},{2,10},{10... | collective-permute-start | bytes 6291464 | tf_op jit(solution)/shard_map/ppermute | solution.py:37
  407.8 24.7 %collective-permute-start.35 = (bf16[2,512,512]{2,1,0:T(8,128)(2,1)S(1)}, bf16[2,512,512]{2,1,0:T(8,128)(2,1)S(1)}, u32[]{:S(2)}, u32[]{:S(2)}) collective-permute-start(bf16[2,512,512]{2,1,0:T(8,128)(2,1)S(1)} %get-tuple-element.619), channel_id=1, source_target_pairs={{0,2},{2,0},{4,6},{6,4},{1,3},{3,1},{5,7},{7,5},{8,10},{10,8},{12,... | collective-permute-start | bytes 3145736 | tf_op jit(solution)/shard_map/ppermute | solution.py:37
  435.6 34.2 %collective-permute-start.36 = (bf16[2,512,1024]{2,1,0:T(8,128)(2,1)}, bf16[2,512,1024]{2,1,0:T(8,128)(2,1)}, u32[]{:S(2)}, u32[]{:S(2)}) collective-permute-start(bf16[2,512,1024]{2,1,0:T(8,128)(2,1)} %get-tuple-element.648), channel_id=1, source_target_pairs={{0,1},{1,0},{2,3},{3,2},{4,5},{5,4},{6,7},{7,6},{8,9},{9,8},{10,11... | collective-permute-start | bytes 6291464 | tf_op jit(solution)/shard_map/ppermute | solution.py:37
  438.5 25.6 %collective-permute-start.39 = (bf16[512,1024]{1,0:T(8,128)(2,1)S(1)}, bf16[512,1024]{1,0:T(8,128)(2,1)S(1)}, u32[]{:S(2)}, u32[]{:S(2)}) collective-permute-start(bf16[512,1024]{1,0:T(8,128)(2,1)S(1)} %get-tuple-element.655), channel_id=1, source_target_pairs={{0,16},{8,24},{16,0},{24,8},{1,17},{9,25},{17,1},{25,9},{2,18},{10... | collective-permute-start | bytes 3145736 | tf_op jit(solution)/shard_map/ppermute | solution.py:37
  440.0 25.3 %collective-permute-start.40 = (bf16[512,1024]{1,0:T(8,128)(2,1)S(1)}, bf16[512,1024]{1,0:T(8,128)(2,1)S(1)}, u32[]{:S(2)}, u32[]{:S(2)}) collective-permute-start(bf16[512,1024]{1,0:T(8,128)(2,1)S(1)} %get-tuple-element.656), channel_id=1, source_target_pairs={{0,8},{8,0},{16,24},{24,16},{1,9},{9,1},{17,25},{25,17},{2,10},{10... | collective-permute-start | bytes 3145736 | tf_op jit(solution)/shard_map/ppermute | solution.py:37
  465.3 28.8 %collective-permute-start.41 = (bf16[256,2048]{1,0:T(8,128)(2,1)}, bf16[256,2048]{1,0:T(8,128)(2,1)}, u32[]{:S(2)}, u32[]{:S(2)}) collective-permute-start(bf16[256,2048]{1,0:T(8,128)(2,1)} %add_convert_fusion.3), channel_id=1, source_target_pairs={{0,8},{8,0},{16,24},{24,16},{1,9},{9,1},{17,25},{25,17},{2,10},{10... | collective-permute-start | bytes 3145736 | tf_op jit(solution)/shard_map/ppermute | solution.py:37
  466.7 27.3 %collective-permute-start.42 = (bf16[256,2048]{1,0:T(8,128)(2,1)}, bf16[256,2048]{1,0:T(8,128)(2,1)}, u32[]{:S(2)}, u32[]{:S(2)}) collective-permute-start(bf16[256,2048]{1,0:T(8,128)(2,1)} %add_convert_fusion.2), channel_id=1, source_target_pairs={{0,16},{8,24},{16,0},{24,8},{1,17},{9,25},{17,1},{25,9},{2,18},{10... | collective-permute-start | bytes 3145736 | tf_op jit(solution)/shard_map/ppermute | solution.py:37
  494.0 56.5 %collective-permute-start.44 = (bf16[512,2048]{1,0:T(8,128)(2,1)}, bf16[512,2048]{1,0:T(8,128)(2,1)}, u32[]{:S(2)}, u32[]{:S(2)}) collective-permute-start(bf16[512,2048]{1,0:T(8,128)(2,1)} %get-tuple-element.693), channel_id=1, source_target_pairs={{0,16},{8,24},{16,0},{24,8},{1,17},{9,25},{17,1},{25,9},{2,18},{10... | collective-permute-start | bytes 6291464 | tf_op jit(solution)/shard_map/ppermute | solution.py:37
  494.8 55.8 %collective-permute-start.45 = (bf16[512,2048]{1,0:T(8,128)(2,1)}, bf16[512,2048]{1,0:T(8,128)(2,1)}, u32[]{:S(2)}, u32[]{:S(2)}) collective-permute-start(bf16[512,2048]{1,0:T(8,128)(2,1)} %get-tuple-element.694), channel_id=1, source_target_pairs={{0,8},{8,0},{16,24},{24,16},{1,9},{9,1},{17,25},{25,17},{2,10},{10... | collective-permute-start | bytes 6291464 | tf_op jit(solution)/shard_map/ppermute | solution.py:37
  497.3 32.0 %collective-permute-start.46 = (bf16[512,1024]{1,0:T(8,128)(2,1)}, bf16[512,1024]{1,0:T(8,128)(2,1)}, u32[]{:S(2)}, u32[]{:S(2)}) collective-permute-start(bf16[512,1024]{1,0:T(8,128)(2,1)} %get-tuple-element.703.refs_2_), channel_id=1, source_target_pairs={{0,1},{1,0},{2,3},{3,2},{4,5},{5,4},{6,7},{7,6},{8,9},{9,8},{10,11... | collective-permute-start | bytes 3145736 | tf_op jit(solution)/shard_map/ppermute | solution.py:37
  520.3 38.0 %collective-permute-start.43 = (bf16[2,512,512]{2,1,0:T(8,128)(2,1)}, bf16[2,512,512]{2,1,0:T(8,128)(2,1)S(1)}, u32[]{:S(2)}, u32[]{:S(2)}) collective-permute-start(bf16[2,512,512]{2,1,0:T(8,128)(2,1)} %get-tuple-element.692), channel_id=1, source_target_pairs={{0,2},{2,0},{4,6},{6,4},{1,3},{3,1},{5,7},{7,5},{8,10},{10,8},{12,... | collective-permute-start | bytes 3145736 | tf_op jit(solution)/shard_map/ppermute | solution.py:37
  526.1 43.0 %collective-permute-start.50 = (bf16[2,128,2048]{2,1,0:T(8,128)(2,1)}, bf16[2,128,2048]{2,1,0:T(8,128)(2,1)}, u32[]{:S(2)}, u32[]{:S(2)}) collective-permute-start(bf16[2,128,2048]{2,1,0:T(8,128)(2,1)} %fusion.3), channel_id=1, source_target_pairs={{0,2},{2,0},{4,6},{6,4},{1,3},{3,1},{5,7},{7,5},{8,10},{10,8},{12,... | collective-permute-start | bytes 3145736 | tf_op jit(solution)/shard_map/ppermute | solution.py:37
  549.6 53.0 %collective-permute-start.52 = (bf16[2,512,512]{2,1,0:T(8,128)(2,1)}, bf16[2,512,512]{2,1,0:T(8,128)(2,1)S(1)}, u32[]{:S(2)}, u32[]{:S(2)}) collective-permute-start(bf16[2,512,512]{2,1,0:T(8,128)(2,1)} %get-tuple-element.719), channel_id=1, source_target_pairs={{0,2},{2,0},{4,6},{6,4},{1,3},{3,1},{5,7},{7,5},{8,10},{10,8},{12,... | collective-permute-start | bytes 3145736 | tf_op jit(solution)/shard_map/ppermute | solution.py:37
  550.6 30.2 %collective-permute-start.48 = (bf16[256,1024]{1,0:T(8,128)(2,1)S(1)}, bf16[256,1024]{1,0:T(8,128)(2,1)S(1)}, u32[]{:S(2)}, u32[]{:S(2)}) collective-permute-start(bf16[256,1024]{1,0:T(8,128)(2,1)S(1)} %copy-done.144), channel_id=1, source_target_pairs={{0,8},{8,0},{16,24},{24,16},{1,9},{9,1},{17,25},{25,17},{2,10},{10... | collective-permute-start | bytes 1572872 | tf_op jit(solution)/shard_map/ppermute | solution.py:37
  551.7 29.2 %collective-permute-start.49 = (bf16[256,1024]{1,0:T(8,128)(2,1)S(1)}, bf16[256,1024]{1,0:T(8,128)(2,1)S(1)}, u32[]{:S(2)}, u32[]{:S(2)}) collective-permute-start(bf16[256,1024]{1,0:T(8,128)(2,1)S(1)} %copy-done.143), channel_id=1, source_target_pairs={{0,16},{8,24},{16,0},{24,8},{1,17},{9,25},{17,1},{25,9},{2,18},{10... | collective-permute-start | bytes 1572872 | tf_op jit(solution)/shard_map/ppermute | solution.py:37
  560.8 25.6 %collective-permute-start.47 = (bf16[512,1024]{1,0:T(8,128)(2,1)S(1)}, bf16[512,1024]{1,0:T(8,128)(2,1)S(1)}, u32[]{:S(2)}, u32[]{:S(2)}) collective-permute-start(bf16[512,1024]{1,0:T(8,128)(2,1)S(1)} %get-tuple-element.755.refs_2_), channel_id=1, source_target_pairs={{0,1},{1,0},{2,3},{3,2},{4,5},{5,4},{6,7},{7,6},{8,9},{9,8},{10,11... | collective-permute-start | bytes 3145736 | tf_op jit(solution)/shard_map/ppermute | solution.py:37
  571.5 34.7 %collective-permute-start.56 = (bf16[2,64,2048]{2,1,0:T(8,128)(2,1)}, bf16[2,64,2048]{2,1,0:T(8,128)(2,1)S(1)}, u32[]{:S(2)}, u32[]{:S(2)}) collective-permute-start(bf16[2,64,2048]{2,1,0:T(8,128)(2,1)} %slice.812), channel_id=1, source_target_pairs={{0,4},{2,6},{4,0},{6,2},{1,5},{3,7},{5,1},{7,3},{8,12},{10,14},{12... | collective-permute-start | bytes 1572872 | tf_op jit(solution)/shard_map/ppermute | solution.py:37
  582.7 48.8 %collective-permute-start.63 = (bf16[2,128,1024]{2,1,0:T(8,128)(2,1)}, bf16[2,128,1024]{2,1,0:T(8,128)(2,1)}, u32[]{:S(2)}, u32[]{:S(2)}) collective-permute-start(bf16[2,128,1024]{2,1,0:T(8,128)(2,1)} %fusion.11), channel_id=1, source_target_pairs={{0,2},{2,0},{4,6},{6,4},{1,3},{3,1},{5,7},{7,5},{8,10},{10,8},{12,... | collective-permute-start | bytes 1572872 | tf_op jit(solution)/shard_map/ppermute | solution.py:37
  609.7 25.3 %collective-permute-start.58 = (bf16[512,1024]{1,0:T(8,128)(2,1)}, bf16[512,1024]{1,0:T(8,128)(2,1)}, u32[]{:S(2)}, u32[]{:S(2)}) collective-permute-start(bf16[512,1024]{1,0:T(8,128)(2,1)} %get-tuple-element.803), channel_id=1, source_target_pairs={{0,16},{8,24},{16,0},{24,8},{1,17},{9,25},{17,1},{25,9},{2,18},{10... | collective-permute-start | bytes 3145736 | tf_op jit(solution)/shard_map/ppermute | solution.py:37
  616.7 43.6 %collective-permute-start.62 = (bf16[2,128,2048]{2,1,0:T(8,128)(2,1)}, bf16[2,128,2048]{2,1,0:T(8,128)(2,1)}, u32[]{:S(2)}, u32[]{:S(2)}) collective-permute-start(bf16[2,128,2048]{2,1,0:T(8,128)(2,1)} %fusion.1), channel_id=1, source_target_pairs={{0,2},{2,0},{4,6},{6,4},{1,3},{3,1},{5,7},{7,5},{8,10},{10,8},{12,... | collective-permute-start | bytes 3145736 | tf_op jit(solution)/shard_map/ppermute | solution.py:37
  619.0 113.5 %collective-permute-start.51 = (bf16[3,128,1024]{2,1,0:T(8,128)(2,1)}, bf16[3,128,1024]{2,1,0:T(8,128)(2,1)}, u32[]{:S(2)}, u32[]{:S(2)}) collective-permute-start(bf16[3,128,1024]{2,1,0:T(8,128)(2,1)} %pad_maximum_fusion.8), channel_id=1, source_target_pairs={{0,4},{2,6},{4,0},{6,2},{1,5},{3,7},{5,1},{7,3},{8,12},{10,14},{12... | collective-permute-start | bytes 2359304 | tf_op jit(solution)/shard_map/ppermute | solution.py:37
  633.3 49.9 %collective-permute-start.69 = (bf16[2,64,1024]{2,1,0:T(8,128)(2,1)S(1)}, bf16[2,64,1024]{2,1,0:T(8,128)(2,1)S(1)}, u32[]{:S(2)}, u32[]{:S(2)}) collective-permute-start(bf16[2,64,1024]{2,1,0:T(8,128)(2,1)S(1)} %slice.815), channel_id=1, source_target_pairs={{0,4},{2,6},{4,0},{6,2},{1,5},{3,7},{5,1},{7,3},{8,12},{10,14},{12... | collective-permute-start | bytes 786440 | tf_op jit(solution)/shard_map/ppermute | solution.py:37
  635.0 26.9 %collective-permute-start.60 = (bf16[512,1152]{1,0:T(8,128)(2,1)S(1)}, bf16[512,1152]{1,0:T(8,128)(2,1)S(1)}, u32[]{:S(2)}, u32[]{:S(2)}) collective-permute-start(bf16[512,1152]{1,0:T(8,128)(2,1)S(1)} %get-tuple-element.805), channel_id=1, source_target_pairs={{0,16},{8,24},{16,0},{24,8},{1,17},{9,25},{17,1},{25,9},{2,18},{10... | collective-permute-start | bytes 3538952 | tf_op jit(solution)/shard_map/ppermute | solution.py:37
  635.8 29.2 %collective-permute-start.61 = (bf16[512,1152]{1,0:T(8,128)(2,1)S(1)}, bf16[512,1152]{1,0:T(8,128)(2,1)S(1)}, u32[]{:S(2)}, u32[]{:S(2)}) collective-permute-start(bf16[512,1152]{1,0:T(8,128)(2,1)S(1)} %get-tuple-element.806), channel_id=1, source_target_pairs={{0,8},{8,0},{16,24},{24,16},{1,9},{9,1},{17,25},{25,17},{2,10},{10... | collective-permute-start | bytes 3538952 | tf_op jit(solution)/shard_map/ppermute | solution.py:37
  660.3 69.0 %collective-permute-start.57 = (bf16[128,1024]{1,0:T(8,128)(2,1)S(1)}, bf16[128,1024]{1,0:T(8,128)(2,1)S(1)}, u32[]{:S(2)}, u32[]{:S(2)}) collective-permute-start(bf16[128,1024]{1,0:T(8,128)(2,1)S(1)} %dynamic-slice_convert_fusion), channel_id=1, source_target_pairs={{0,4},{2,6},{4,0},{6,2},{1,5},{3,7},{5,1},{7,3},{8,12},{10,14},{12... | collective-permute-start | bytes 786440 | tf_op jit(solution)/shard_map/ppermute | solution.py:37
  662.0 37.1 %collective-permute-start.68 = (bf16[2,64,2048]{2,1,0:T(8,128)(2,1)S(1)}, bf16[2,64,2048]{2,1,0:T(8,128)(2,1)S(1)}, u32[]{:S(2)}, u32[]{:S(2)}) collective-permute-start(bf16[2,64,2048]{2,1,0:T(8,128)(2,1)S(1)} %slice.811), channel_id=1, source_target_pairs={{0,4},{2,6},{4,0},{6,2},{1,5},{3,7},{5,1},{7,3},{8,12},{10,14},{12... | collective-permute-start | bytes 1572872 | tf_op jit(solution)/shard_map/ppermute | solution.py:37
  717.0 24.5 %collective-permute-start.75 = (bf16[2,64,1024]{2,1,0:T(8,128)(2,1)S(1)}, bf16[2,64,1024]{2,1,0:T(8,128)(2,1)S(1)}, u32[]{:S(2)}, u32[]{:S(2)}) collective-permute-start(bf16[2,64,1024]{2,1,0:T(8,128)(2,1)S(1)} %slice.814), channel_id=1, source_target_pairs={{0,4},{2,6},{4,0},{6,2},{1,5},{3,7},{5,1},{7,3},{8,12},{10,14},{12... | collective-permute-start | bytes 786440 | tf_op jit(solution)/shard_map/ppermute | solution.py:37
  (189 other events, 2186.9 us)
Sparse Core Ops, SparseCore 0:
  30.4 52.0 all-gather.3
  84.6 49.9 all-gather.5
  181.1 59.9 all-gather.7

commit v4 on v3

--- a/solution.py
+++ b/solution.py
@@ -172,8 +172,9 @@
             self.spots = list(range(lax.axis_size("seq")))
             self.column = lax.all_gather(shards, "seq", axis=1, tiled=True)
 
-    def along(self):
-        self.came = swap(self.column, "seq", self.steps.pop(0))
+    def along(self, others=()):
+        (ready,) = after([self.column], others)
+        self.came = swap(ready, "seq", self.steps.pop(0))
 
     def join(self, order):
         self.column = order(
@@ -302,6 +303,17 @@
             away = after([away for away, _ in self.halves], others)
             self.came = [swap(v, "dp", bit) for v, bit in zip(away, self.bits, strict=True)]
 
+    @staticmethod
+    def early(grad, bit, others=()):
+        if lax.axis_size("dp") != 4:
+            return None
+        (away,) = after([grad[0]], others)
+        return swap(away, "dp", bit)
+
+    def begun(self, *came):
+        self.came = [] if self.plain else list(came)
+        return self
+
     def next(self, others=()):
         self.last = []
         if not self.plain:
@@ -429,11 +441,12 @@
     return trade_start(value[value.shape[0] // 2 :].astype(LOW))
 
 
-def back_starts(*values):
+def back_starts(others, *values):
     halves = [value[value.shape[0] // 2 :].astype(LOW) for value in values]
     core, size = lax.axis_index("mp"), halves[0].shape[0] // 2
     parts = [lax.dynamic_slice_in_dim(half, core * size, size, 0) for half in halves]
-    return swap(jnp.stack(parts), "seq", 2)
+    (ready,) = after([jnp.stack(parts)], others)
+    return swap(ready, "seq", 2)
 
 
 def back_ends(values, part):
@@ -935,22 +948,26 @@
     ]
     feed_cuts = [(0, 0, hidden), (1, 0, hidden)]
     counts, counted = token_counts(lengths, groups)
-    one = Gather(shards[0], True)
+    one, two = [Gather(shard, True) for shard in shards[:2]]
     one.along()
-    two, three, four = [Gather(shard, False, [one.came]) for shard in shards[1:]]
+    two.along([one.came])
     one.join(order)
     one.along()
     one.join(order)
     one.across([counted])
-    src_part = pair_start(src, [one.column])
     y_first, x_first = order(lambda: (row_order(2, True), row_order(1, True)))
+    two.join(order)
+    two.along([one.column])
+    three, four = [Gather(shard, False, [two.came]) for shard in shards[2:]]
     one.far(order)
+    two.join(order)
+    src_part = pair_start(src, [two.column])
+    two.across(one.last)
     offsets, tok_weight, all_tokens = order(
         token_tables, lengths, groups, counts, full_len, quarter
     )
     same, same_t, causal, causal_t = offsets
     factor = 1.0 / all_tokens
-    two.across(one.last)
     *enc_w, table = one.place(order, attn_cuts + [(0, 2 * half, LANES)])
     table = table[:, :n_norms].T.astype(F32)[:, None]
     e_norm = [(table[i], table[n_enc + i]) for i in range(n_enc)]
@@ -974,6 +991,7 @@
     cot_part = pair_start(cotangent, [self_q])
     three.far(order)
     four.across(three.last)
+    order.wait(three.last)
     self_ctx, self_lse = order(attend, self_q, self_own, self_peer, causal)
     self_part = order(project_out, self_ctx, self_w[2])
     self_other = other_core(self_part)
@@ -986,17 +1004,17 @@
         feed, x_src, (enc_part, enc_other), e_norm[1], e_up, e_down
     )
     mem_other = other_core(mem_part)
+    four.far(order)
     source, cross_own = order(enter, enc_mid, (mem_part, mem_other), None, cross_w[0])
     cross_peer = swap(cross_own, "seq", 1)
     cross_in, cross_q, dec_mid = order(
         enter, x_tgt, (self_part, self_other), d_norm[1], cross_w[1]
     )
     cross_q = cross_q[0]
-    four.far(order)
+    d_up, d_down = four.place(order, feed_cuts)
     cross_ctx, cross_lse = order(attend, cross_q, cross_own, cross_peer, same)
     cross_part = order(project_out, cross_ctx, cross_w[2])
     cross_other = other_core(cross_part)
-    d_up, d_down = four.place(order, feed_cuts)
     dec_normed, dec_cross, dec_act, dec_slope, dec_part = order(
         feed, dec_mid, (cross_part, cross_other), d_norm[2], d_up, d_down
     )
@@ -1088,17 +1106,17 @@
     enc.next(self_s.last)
     cross.add(order)
     self_s.add(order)
+    enc.add(order)
+    src_part = back_starts(enc.last if not enc.plain else [], src_grad)
+    three_part = back_starts([], decoded, memory_low, tgt_grad)
+    self_s.add(order)
     e_feed.add(order)
     enc.add(order)
-    src_part = back_start(src_grad)
-    three_part = back_starts(decoded, memory_low, tgt_grad)
-    self_s.add(order)
-    enc.add(order)
-    src_grad = order(back_end, src_grad, src_part)
     decoded, memory_grad, tgt_grad = order(
         back_ends, (decoded, memory_grad, tgt_grad), three_part
     )
     self_s.add(order)
+    (src_grad,) = order(back_ends, (src_grad,), src_part)
     enc.add(order)
 
     norm_out = enc.out[0][:, 2 * half : 2 * half + n_norms].T

time: 767 us -> 757 us (0.987)
  waiting for transfers between devices: 292 us -> 275 us
  local copies, waits for them, and re-layouts: 78.3 us -> 92.2 us
  starting transfers between devices: 83.2 us -> 73.2 us
  Pallas kernels: 202 us -> 211 us
    ppermute x76 -> x78, waiting for transfers between devices: 292 us -> 273 us  [swap(): return lax.ppermute(value, axis, xor_perm(lax.axis_size(axis), bits))]
    unnamed x308 -> x292, local copies, waits for them, and re-layouts: 36.9 us -> 49.2 us
    ppermute x76 -> x78, starting transfers between devices: 83.1 us -> 73.1 us  [swap(): return lax.ppermute(value, axis, xor_perm(lax.axis_size(axis), bits))]
  transfers between devices with their start and end apart: 79 -> 80, of which waited for: 32 -> 34; matrix products, arithmetic and copies ran while one was open for 15% -> 16% of each run, Pallas kernels for 24% -> 24%
where the time goes in v4:
time: 757 us; the launch traced here: 751 us
  waiting for transfers between devices  275 us (36%)
  Pallas kernels  211 us (28%)
  local copies, waits for them, and re-layouts  92.2 us (12%)
  other arithmetic  76.7 us (10%)
  starting transfers between devices  73.2 us (10%)
  between operations  16.3 us (2%)
    ppermute x78, waiting for transfers between devices, swap(): return lax.ppermute(value, axis, xor_perm(lax.axis_size(axis), bits))  273 us
    ppermute x78, starting transfers between devices, swap(): return lax.ppermute(value, axis, xor_perm(lax.axis_size(axis), bits))  73.1 us
    unnamed x292, local copies, waits for them, and re-layouts  49.2 us
    pallas_call x3, Pallas kernels, attend_back(): pl.pallas_call(attend_back_body, grid=(width // LANES,), in_specs=[spec]...  46.9 us
    pallas_call x10, Pallas kernels, weight_grad(): pl.pallas_call(body, grid_spec=pltpu.PrefetchScalarGridSpec(num_scalar_pr...  40.9 us
    pallas_call x3, Pallas kernels, attend(): pl.pallas_call(functools.partial(attend_body, 256), grid=(width // LANES,...  29.7 us
    pallas_call x2, Pallas kernels, feed(): pl.pallas_call(body, grid=(hidden // TILE,), in_specs=[same, same, same,...  24.1 us
    pallas_call x2, Pallas kernels, feed_back(): pl.pallas_call(body, grid=(hidden // TILE,), in_specs=[same, block, weigh...  18 us
  transfers between devices with their start and end apart: 80, of which 34 were waited for; matrix products, arithmetic and copies ran while one was open for 16% of the time, Pallas kernels for 24%

profile of v4, /device:TPU:0, one launch (start us, length us, event | category | flops | bytes accessed | tf_op | source)
XLA Modules:
  0.0 751.4 jit_solution(1962246179766241853)
XLA Ops:
  20.5 9.8 %collective-permute-done = bf16[2,64,1152]{2,1,0:T(8,128)(2,1)S(1)} collective-permute-done((bf16[2,64,1152]{2,1,0:T(8,128)(2,1)S(1)}, bf16[2,64,1152]{2,1,0:T(8,128)(2,1)S(1)}, u32[]{:S(2)}, u32[]{:S(2)}) %collective-permute-start) | collective-permute-done | bytes 294944 | tf_op jit(solution)/shard_map/ppermute | solution.py:37
  30.4 4.1 collective-permute-start.2
  36.2 19.2 %collective-permute-done.1 = bf16[2,64,2048]{2,1,0:T(8,128)(2,1)S(1)} collective-permute-done((bf16[2,64,2048]{2,1,0:T(8,128)(2,1)S(1)}, bf16[2,64,2048]{2,1,0:T(8,128)(2,1)S(1)}, u32[]{:S(2)}, u32[]{:S(2)}) %collective-permute-start.1) | collective-permute-done | bytes 524320 | tf_op jit(solution)/shard_map/ppermute | solution.py:37
  64.6 22.1 %collective-permute-done.3 = bf16[2,128,2048]{2,1,0:T(8,128)(2,1)} collective-permute-done((bf16[2,128,2048]{2,1,0:T(8,128)(2,1)}, bf16[2,128,2048]{2,1,0:T(8,128)(2,1)}, u32[]{:S(2)}, u32[]{:S(2)}) %collective-permute-start.3) | collective-permute-done | bytes 1048608 | tf_op jit(solution)/shard_map/ppermute | solution.py:37
  112.7 3.3 shard_map.359
  120.1 6.9 collective-permute-done.8
  130.4 3.2 shard_map.360
  135.1 12.9 %collective-permute-done.15.refs_2_ = bf16[2,256,2048]{2,1,0:T(8,128)(2,1)} collective-permute-done((bf16[2,256,2048]{2,1,0:T(8,128)(2,1)}, bf16[2,256,2048]{2,1,0:T(8,128)(2,1)}, u32[]{:S(2)}, u32[]{:S(2)}) %collective-permute-start.15) | collective-permute-done | bytes 2097184 | tf_op jit(solution)/shard_map/ppermute | solution.py:37
  155.4 19.2 %collective-permute-done.18.refs_4_ = bf16[256,2048]{1,0:T(8,128)(2,1)} collective-permute-done((bf16[256,2048]{1,0:T(8,128)(2,1)}, bf16[256,2048]{1,0:T(8,128)(2,1)}, u32[]{:S(2)}, u32[]{:S(2)}) %collective-permute-start.18) | collective-permute-done | bytes 1048608 | tf_op jit(solution)/shard_map/ppermute | solution.py:37
  182.5 3.5 collective-permute-start.12
  187.1 9.8 %shard_map.361 = (bf16[512,512]{1,0:T(8,128)(2,1)S(1)}, f32[512,512]{1,0:T(8,128)S(1)}) custom-call(bf16[512,512]{1,0:T(8,128)(2,1)S(1)} %copy-done.54, bf16[2,512,512]{2,1,0:T(8,128)(2,1)} %get-tuple-element.723.ko_ref.vo_ref, bf16[2,512,512]{2,1,0:T(8,128)(2,1)} %collective-permute-done.13.kp_ref.vp_ref, ...), custom_call_target="tpu_custom_call" | custom-call | flops 1 | bytes 1 | tf_op jit(solution)/shard_map/pallas_call | solution.py:556
  200.5 5.3 shard_map.362
  211.8 8.1 %collective-permute-done.21.refs_2_ = bf16[2,256,2048]{2,1,0:T(8,128)(2,1)} collective-permute-done((bf16[2,256,2048]{2,1,0:T(8,128)(2,1)}, bf16[2,256,2048]{2,1,0:T(8,128)(2,1)}, u32[]{:S(2)}, u32[]{:S(2)}) %collective-permute-start.21) | collective-permute-done | bytes 2097184 | tf_op jit(solution)/shard_map/ppermute | solution.py:37
  228.3 19.5 %collective-permute-done.23.refs_4_ = bf16[256,2048]{1,0:T(8,128)(2,1)} collective-permute-done((bf16[256,2048]{1,0:T(8,128)(2,1)}, bf16[256,2048]{1,0:T(8,128)(2,1)}, u32[]{:S(2)}, u32[]{:S(2)}) %collective-permute-start.23) | collective-permute-done | bytes 1048608 | tf_op jit(solution)/shard_map/ppermute | solution.py:37
  251.7 3.9 collective-permute-start.26
  258.3 10.0 %shard_map.364 = (bf16[512,512]{1,0:T(8,128)(2,1)S(1)}, f32[512,512]{1,0:T(8,128)S(1)}) custom-call(bf16[512,512]{1,0:T(8,128)(2,1)S(1)} %copy-done.56, bf16[2,512,512]{2,1,0:T(8,128)(2,1)} %get-tuple-element.696.ko_ref.vo_ref, bf16[2,512,512]{2,1,0:T(8,128)(2,1)} %collective-permute-done.19.kp_ref.vp_ref, ...), custom_call_target="tpu_custom_call" | custom-call | flops 1 | bytes 1 | tf_op jit(solution)/shard_map/pallas_call | solution.py:556
  275.8 4.0 shard_map.365
  283.8 11.9 %shard_map.366 = (bf16[512,1024]{1,0:T(8,128)(2,1)S(1)}, f32[512,1024]{1,0:T(8,128)}, bf16[512,2048]{1,0:T(8,128)(2,1)}, bf16[512,2048]{1,0:T(8,128)(2,1)}, bf16[512,1024]{1,0:T(8,128)(2,1)S(1)}) custom-call(bf16[512,1024]{1,0:T(8,128)(2,1)S(1)} %copy-done.4, bf16[512,1024]{1,0:T(8,128)(2,1)} %convolution_convert_fusion.2.one_ref, ...), custom_call_target="tpu_custom_call" | custom-call | flops 1 | bytes 1 | tf_op jit(solution)/shard_map/pallas_call | solution.py:707
  309.9 14.4 %collective-permute-done.33.refs_4_ = bf16[256,2048]{1,0:T(8,128)(2,1)S(1)} collective-permute-done((bf16[256,2048]{1,0:T(8,128)(2,1)S(1)}, bf16[256,2048]{1,0:T(8,128)(2,1)S(1)}, u32[]{:S(2)}, u32[]{:S(2)}) %collective-permute-start.33) | collective-permute-done | bytes 1048608 | tf_op jit(solution)/shard_map/ppermute | solution.py:37
  330.5 3.5 shard_map.369
  337.9 10.0 %shard_map.370 = (bf16[512,512]{1,0:T(8,128)(2,1)S(1)}, f32[512,512]{1,0:T(8,128)S(1)}) custom-call(bf16[512,512]{1,0:T(8,128)(2,1)S(1)} %bitcast.191, bf16[2,512,512]{2,1,0:T(8,128)(2,1)} %get-tuple-element.623.ko_ref.vo_ref, bf16[2,512,512]{2,1,0:T(8,128)(2,1)} %collective-permute-done.31.kp_ref.vp_ref, ...), custom_call_target="tpu_custom_call" | custom-call | flops 1 | bytes 1 | tf_op jit(solution)/shard_map/pallas_call | solution.py:556
  351.4 12.3 %shard_map.371 = (bf16[512,1024]{1,0:T(8,128)(2,1)S(1)}, f32[512,1024]{1,0:T(8,128)}, bf16[512,2048]{1,0:T(8,128)(2,1)}, bf16[512,2048]{1,0:T(8,128)(2,1)}, bf16[512,1024]{1,0:T(8,128)(2,1)S(1)}) custom-call(f32[512,1024]{1,0:T(8,128)} %copy-done.24, bf16[512,1024]{1,0:T(8,128)(2,1)S(1)} %convolution_convert_fusion.one_ref, ...), custom_call_target="tpu_custom_call" | custom-call | flops 1 | bytes 1 | tf_op jit(solution)/shard_map/pallas_call | solution.py:707
  363.7 8.2 %shard_map.372 = (bf16[512,2048]{1,0:T(8,128)(2,1)S(1)}, bf16[512,1024]{1,0:T(8,128)(2,1)S(1)}) custom-call(bf16[512,1024]{1,0:T(8,128)(2,1)S(1)} %copy-done.14, bf16[512,2048]{1,0:T(8,128)(2,1)} %get-tuple-element.597.slope_ref, bf16[1024,2048]{1,0:T(8,128)(2,1)} %copy-done.10, bf16[1024,2048]{1,0:T(8,128)(2,1)} %copy-done.11), custom_call_target="tpu_custom_call" | custom-call | flops 1 | bytes 1 | tf_op jit(solution)/shard_map/pallas_call | solution.py:751
  372.5 5.2 shard_map.373
  377.7 5.2 shard_map.374
  388.4 15.5 %shard_map.376 = (bf16[512,512]{1,0:T(8,128)(2,1)S(1)}, bf16[2,512,512]{2,1,0:T(8,128)(2,1)S(1)}, bf16[2,512,512]{2,1,0:T(8,128)(2,1)S(1)}) custom-call(bf16[512,512]{1,0:T(8,128)(2,1)S(1)} %bitcast.192, bf16[2,512,512]{2,1,0:T(8,128)(2,1)} %get-tuple-element.623.ko_ref.vo_ref, bf16[2,512,512]{2,1,0:T(8,128)(2,1)} %collective-permute-done.31.kp_ref.vp_ref, ...), custom_call_target="tpu_custom_call" | custom-call | flops 1 | bytes 1 | tf_op jit(solution)/shard_map/pallas_call | solution.py:611
  407.7 3.1 add_convert_fusion.4
  410.9 17.7 %collective-permute-done.37.came_ref = bf16[2,512,512]{2,1,0:T(8,128)(2,1)S(1)} collective-permute-done((bf16[2,512,512]{2,1,0:T(8,128)(2,1)S(1)}, bf16[2,512,512]{2,1,0:T(8,128)(2,1)S(1)}, u32[]{:S(2)}, u32[]{:S(2)}) %collective-permute-start.37) | collective-permute-done | bytes 1048608 | tf_op jit(solution)/shard_map/ppermute | solution.py:37
  428.6 3.2 shard_map.378
  442.6 17.6 %collective-permute-done.41 = bf16[512,1024]{1,0:T(8,128)(2,1)S(1)} collective-permute-done((bf16[512,1024]{1,0:T(8,128)(2,1)S(1)}, bf16[512,1024]{1,0:T(8,128)(2,1)S(1)}, u32[]{:S(2)}, u32[]{:S(2)}) %collective-permute-start.41) | collective-permute-done | bytes 1048608 | tf_op jit(solution)/shard_map/ppermute | solution.py:37
  467.8 9.8 %shard_map.380 = (bf16[512,2048]{1,0:T(8,128)(2,1)S(1)}, bf16[512,1024]{1,0:T(8,128)(2,1)}) custom-call(bf16[512,1024]{1,0:T(8,128)(2,1)S(1)} %get-tuple-element.670.low_ref.refs_0_, bf16[512,2048]{1,0:T(8,128)(2,1)} %get-tuple-element.662.slope_ref, bf16[1024,2048]{1,0:T(8,128)(2,1)} %copy-done.8, bf16[1024,2048]{1,0:T(8,128)(2,1)} %copy-done.9), custom_call_target="tpu_custom_call" | custom-call | flops 1 | bytes 1 | tf_op jit(solution)/shard_map/pallas_call | solution.py:751
  477.6 5.2 shard_map.381
  484.8 5.2 shard_map.382
  501.2 15.7 %shard_map.384 = (bf16[512,512]{1,0:T(8,128)(2,1)S(1)}, bf16[2,512,512]{2,1,0:T(8,128)(2,1)S(1)}, bf16[2,512,512]{2,1,0:T(8,128)(2,1)}) custom-call(bf16[512,512]{1,0:T(8,128)(2,1)S(1)} %copy-done.57, bf16[2,512,512]{2,1,0:T(8,128)(2,1)} %get-tuple-element.696.ko_ref.vo_ref, bf16[2,512,512]{2,1,0:T(8,128)(2,1)} %collective-permute-done.19.kp_ref.vp_ref, ...), custom_call_target="tpu_custom_call" | custom-call | flops 1 | bytes 1 | tf_op jit(solution)/shard_map/pallas_call | solution.py:611
  527.1 4.1 shard_map.385
  532.8 15.7 %shard_map.386 = (bf16[512,512]{1,0:T(8,128)(2,1)S(1)}, bf16[2,512,512]{2,1,0:T(8,128)(2,1)S(1)}, bf16[2,512,512]{2,1,0:T(8,128)(2,1)}) custom-call(bf16[512,512]{1,0:T(8,128)(2,1)S(1)} %copy-done.55, bf16[2,512,512]{2,1,0:T(8,128)(2,1)} %get-tuple-element.723.ko_ref.vo_ref, bf16[2,512,512]{2,1,0:T(8,128)(2,1)} %collective-permute-done.13.kp_ref.vp_ref, ...), custom_call_target="tpu_custom_call" | custom-call | flops 1 | bytes 1 | tf_op jit(solution)/shard_map/pallas_call | solution.py:611
  557.3 3.5 shard_map.387
  561.0 5.7 collective-permute-done.52
  570.5 4.0 shard_map.388
  574.6 3.9 shard_map.389
  588.1 12.3 %collective-permute-done.54.came_ref = bf16[2,512,512]{2,1,0:T(8,128)(2,1)} collective-permute-done((bf16[2,512,512]{2,1,0:T(8,128)(2,1)}, bf16[2,512,512]{2,1,0:T(8,128)(2,1)}, u32[]{:S(2)}, u32[]{:S(2)}) %collective-permute-start.54) | collective-permute-done | bytes 1048608 | tf_op jit(solution)/shard_map/ppermute | solution.py:37
  600.4 3.3 shard_map.391
  627.6 3.2 shard_map.394
  638.8 19.7 %collective-permute-done.63 = bf16[2,128,2048]{2,1,0:T(8,128)(2,1)} collective-permute-done((bf16[2,128,2048]{2,1,0:T(8,128)(2,1)}, bf16[2,128,2048]{2,1,0:T(8,128)(2,1)}, u32[]{:S(2)}, u32[]{:S(2)}) %collective-permute-start.63) | collective-permute-done | bytes 1048608 | tf_op jit(solution)/shard_map/ppermute | solution.py:37
  663.8 14.8 %collective-permute-done.69 = bf16[2,64,1024]{2,1,0:T(8,128)(2,1)S(1)} collective-permute-done((bf16[2,64,1024]{2,1,0:T(8,128)(2,1)S(1)}, bf16[2,64,1024]{2,1,0:T(8,128)(2,1)S(1)}, u32[]{:S(2)}, u32[]{:S(2)}) %collective-permute-start.69) | collective-permute-done | bytes 262176 | tf_op jit(solution)/shard_map/ppermute | solution.py:37
  684.4 5.1 collective-permute-done.67
  691.1 7.2 collective-permute-done.72
  702.7 21.4 %collective-permute-done.70 = bf16[2,128,1152]{2,1,0:T(8,128)(2,1)S(1)} collective-permute-done((bf16[2,128,1152]{2,1,0:T(8,128)(2,1)S(1)}, bf16[2,128,1152]{2,1,0:T(8,128)(2,1)S(1)}, u32[]{:S(2)}, u32[]{:S(2)}) %collective-permute-start.70) | collective-permute-done | bytes 589856 | tf_op jit(solution)/shard_map/ppermute | solution.py:37
  (642 shorter events, 282.9 us)
Async XLA Ops:
  7.2 148.2 %all-gather.3.cloned.1.call-start = ((), (), s32[]{:S(2)}) async-start(), calls=%async_computation | async-start | bytes 2621440 | tf_op jit(solution)/shard_map/all_gather | solution.py:173
  8.9 25.7 %collective-permute-start.4 = (f32[8,128]{1,0:T(8,128)S(1)}, f32[8,128]{1,0:T(8,128)S(1)}, u32[]{:S(2)}, u32[]{:S(2)}) collective-permute-start(f32[8,128]{1,0:T(8,128)S(1)} %pad.13), channel_id=1, source_target_pairs={{0,8},{8,0},{16,24},{24,16},{1,9},{9,1},{17,25},{25,17},{2,10},{10... | collective-permute-start | bytes 12296 | tf_op jit(solution)/shard_map/ppermute | solution.py:37
  30.4 26.5 %collective-permute-start.2 = (bf16[2,128,1152]{2,1,0:T(8,128)(2,1)S(1)}, bf16[2,128,1152]{2,1,0:T(8,128)(2,1)S(1)}, u32[]{:S(2)}, u32[]{:S(2)}) collective-permute-start(bf16[2,128,1152]{2,1,0:T(8,128)(2,1)S(1)} %constant_dynamic-update-slice_fusion.2), channel_id=1, source_target_pairs={{0,2},{2,0},{4,6},{6,4},{1,3},{3,1},{5,7},{7,5},{8,10},{10,8},{12,... | collective-permute-start | bytes 1769480 | tf_op jit(solution)/shard_map/ppermute | solution.py:37
  58.7 28.0 %collective-permute-start.7 = (bf16[2,256,1152]{2,1,0:T(8,128)(2,1)}, bf16[2,256,1152]{2,1,0:T(8,128)(2,1)S(1)}, u32[]{:S(2)}, u32[]{:S(2)}) collective-permute-start(bf16[2,256,1152]{2,1,0:T(8,128)(2,1)} %constant_dynamic-update-slice_fusion.4.refs_0_), channel_id=1, source_target_pairs={{0,16},{8,24},{16,0},{24,8},{1,17},{9,25},{17,1},{25,9},{2,18},{10... | collective-permute-start | bytes 3538952 | tf_op jit(solution)/shard_map/ppermute | solution.py:37
  60.2 27.0 %collective-permute-start.6 = (bf16[2,256,1152]{2,1,0:T(8,128)(2,1)}, bf16[2,256,1152]{2,1,0:T(8,128)(2,1)S(1)}, u32[]{:S(2)}, u32[]{:S(2)}) collective-permute-start(bf16[2,256,1152]{2,1,0:T(8,128)(2,1)} %constant_dynamic-update-slice_fusion.4.refs_0_), channel_id=1, source_target_pairs={{0,8},{8,0},{16,24},{24,16},{1,9},{9,1},{17,25},{25,17},{2,10},{10... | collective-permute-start | bytes 3538952 | tf_op jit(solution)/shard_map/ppermute | solution.py:37
  86.7 141.6 %all-gather.5.cloned.1.call-start = ((), (), s32[]{:S(2)}) async-start(), calls=%async_computation.1 | async-start | bytes 2621440 | tf_op jit(solution)/shard_map/all_gather | solution.py:173
  97.2 29.8 %collective-permute-start.8 = (bf16[128,1024]{1,0:T(8,128)(2,1)}, bf16[128,1024]{1,0:T(8,128)(2,1)}, u32[]{:S(2)}, u32[]{:S(2)}) collective-permute-start(bf16[128,1024]{1,0:T(8,128)(2,1)} %constant_dynamic-slice_fusion.4), channel_id=1, source_target_pairs={{0,4},{2,6},{4,0},{6,2},{1,5},{3,7},{5,1},{7,3},{8,12},{10,14},{12... | collective-permute-start | bytes 786440 | tf_op jit(solution)/shard_map/ppermute | solution.py:37
  103.3 44.7 %collective-permute-start.15 = (bf16[2,256,2048]{2,1,0:T(8,128)(2,1)}, bf16[2,256,2048]{2,1,0:T(8,128)(2,1)}, u32[]{:S(2)}, u32[]{:S(2)}) collective-permute-start(bf16[2,256,2048]{2,1,0:T(8,128)(2,1)} %constant_dynamic-update-slice_fusion.6.refs_0_), channel_id=1, source_target_pairs={{0,16},{8,24},{16,0},{24,8},{1,17},{9,25},{17,1},{25,9},{2,18},{10... | collective-permute-start | bytes 6291464 | tf_op jit(solution)/shard_map/ppermute | solution.py:37
  103.8 44.2 %collective-permute-start.14 = (bf16[2,256,2048]{2,1,0:T(8,128)(2,1)}, bf16[2,256,2048]{2,1,0:T(8,128)(2,1)}, u32[]{:S(2)}, u32[]{:S(2)}) collective-permute-start(bf16[2,256,2048]{2,1,0:T(8,128)(2,1)} %constant_dynamic-update-slice_fusion.6.refs_0_), channel_id=1, source_target_pairs={{0,8},{8,0},{16,24},{24,16},{1,9},{9,1},{17,25},{25,17},{2,10},{10... | collective-permute-start | bytes 6291464 | tf_op jit(solution)/shard_map/ppermute | solution.py:37
  155.4 30.6 %collective-permute-start.13 = (bf16[2,512,512]{2,1,0:T(8,128)(2,1)}, bf16[2,512,512]{2,1,0:T(8,128)(2,1)}, u32[]{:S(2)}, u32[]{:S(2)}) collective-permute-start(bf16[2,512,512]{2,1,0:T(8,128)(2,1)} %get-tuple-element.723.ko_ref.vo_ref), channel_id=1, source_target_pairs={{0,2},{2,0},{4,6},{6,4},{1,3},{3,1},{5,7},{7,5},{8,10},{10,8},{12,... | collective-permute-start | bytes 3145736 | tf_op jit(solution)/shard_map/ppermute | solution.py:37
  177.3 42.7 %collective-permute-start.21 = (bf16[2,256,2048]{2,1,0:T(8,128)(2,1)}, bf16[2,256,2048]{2,1,0:T(8,128)(2,1)}, u32[]{:S(2)}, u32[]{:S(2)}) collective-permute-start(bf16[2,256,2048]{2,1,0:T(8,128)(2,1)} %all-gather.3.cloned.1.call-done.refs_0_), channel_id=1, source_target_pairs={{0,16},{8,24},{16,0},{24,8},{1,17},{9,25},{17,1},{25,9},{2,18},{10... | collective-permute-start | bytes 6291464 | tf_op jit(solution)/shard_map/ppermute | solution.py:37
  178.7 41.2 %collective-permute-start.20 = (bf16[2,256,2048]{2,1,0:T(8,128)(2,1)}, bf16[2,256,2048]{2,1,0:T(8,128)(2,1)}, u32[]{:S(2)}, u32[]{:S(2)}) collective-permute-start(bf16[2,256,2048]{2,1,0:T(8,128)(2,1)} %all-gather.3.cloned.1.call-done.refs_0_), channel_id=1, source_target_pairs={{0,8},{8,0},{16,24},{24,16},{1,9},{9,1},{17,25},{25,17},{2,10},{10... | collective-permute-start | bytes 6291464 | tf_op jit(solution)/shard_map/ppermute | solution.py:37
  225.9 29.7 %collective-permute-start.19 = (bf16[2,512,512]{2,1,0:T(8,128)(2,1)}, bf16[2,512,512]{2,1,0:T(8,128)(2,1)}, u32[]{:S(2)}, u32[]{:S(2)}) collective-permute-start(bf16[2,512,512]{2,1,0:T(8,128)(2,1)} %get-tuple-element.696.ko_ref.vo_ref), channel_id=1, source_target_pairs={{0,2},{2,0},{4,6},{6,4},{1,3},{3,1},{5,7},{7,5},{8,10},{10,8},{12,... | collective-permute-start | bytes 3145736 | tf_op jit(solution)/shard_map/ppermute | solution.py:37
  248.5 47.4 %collective-permute-start.30 = (bf16[2,256,2048]{2,1,0:T(8,128)(2,1)}, bf16[2,256,2048]{2,1,0:T(8,128)(2,1)}, u32[]{:S(2)}, u32[]{:S(2)}) collective-permute-start(bf16[2,256,2048]{2,1,0:T(8,128)(2,1)} %all-gather.5.cloned.1.call-done.refs_0_), channel_id=1, source_target_pairs={{0,16},{8,24},{16,0},{24,8},{1,17},{9,25},{17,1},{25,9},{2,18},{10... | collective-permute-start | bytes 6291464 | tf_op jit(solution)/shard_map/ppermute | solution.py:37
  249.2 46.6 %collective-permute-start.29 = (bf16[2,256,2048]{2,1,0:T(8,128)(2,1)}, bf16[2,256,2048]{2,1,0:T(8,128)(2,1)}, u32[]{:S(2)}, u32[]{:S(2)}) collective-permute-start(bf16[2,256,2048]{2,1,0:T(8,128)(2,1)} %all-gather.5.cloned.1.call-done.refs_0_), channel_id=1, source_target_pairs={{0,8},{8,0},{16,24},{24,16},{1,9},{9,1},{17,25},{25,17},{2,10},{10... | collective-permute-start | bytes 6291464 | tf_op jit(solution)/shard_map/ppermute | solution.py:37
  270.5 33.3 %collective-permute-start.24 = (bf16[512,1024]{1,0:T(8,128)(2,1)}, bf16[512,1024]{1,0:T(8,128)(2,1)}, u32[]{:S(2)}, u32[]{:S(2)}) collective-permute-start(bf16[512,1024]{1,0:T(8,128)(2,1)} %convolution_convert_fusion.1.refs_1_), channel_id=1, source_target_pairs={{0,1},{1,0},{2,3},{3,2},{4,5},{5,4},{6,7},{7,6},{8,9},{9,8},{10,11... | collective-permute-start | bytes 3145736 | tf_op jit(solution)/shard_map/ppermute | solution.py:37
  299.0 25.3 %collective-permute-start.33 = (bf16[256,2048]{1,0:T(8,128)(2,1)S(1)}, bf16[256,2048]{1,0:T(8,128)(2,1)S(1)}, u32[]{:S(2)}, u32[]{:S(2)}) collective-permute-start(bf16[256,2048]{1,0:T(8,128)(2,1)S(1)} %slice_bitcast_fusion.5), channel_id=1, source_target_pairs={{0,8},{8,0},{16,24},{24,16},{1,9},{9,1},{17,25},{25,17},{2,10},{10... | collective-permute-start | bytes 3145736 | tf_op jit(solution)/shard_map/ppermute | solution.py:37
  299.5 25.8 %collective-permute-start.32 = (bf16[256,2048]{1,0:T(8,128)(2,1)S(1)}, bf16[256,2048]{1,0:T(8,128)(2,1)S(1)}, u32[]{:S(2)}, u32[]{:S(2)}) collective-permute-start(bf16[256,2048]{1,0:T(8,128)(2,1)S(1)} %slice_bitcast_fusion.6), channel_id=1, source_target_pairs={{0,16},{8,24},{16,0},{24,8},{1,17},{9,25},{17,1},{25,9},{2,18},{10... | collective-permute-start | bytes 3145736 | tf_op jit(solution)/shard_map/ppermute | solution.py:37
  302.9 35.0 %collective-permute-start.31 = (bf16[2,512,512]{2,1,0:T(8,128)(2,1)}, bf16[2,512,512]{2,1,0:T(8,128)(2,1)}, u32[]{:S(2)}, u32[]{:S(2)}) collective-permute-start(bf16[2,512,512]{2,1,0:T(8,128)(2,1)} %get-tuple-element.623.ko_ref.vo_ref), channel_id=1, source_target_pairs={{0,2},{2,0},{4,6},{6,4},{1,3},{3,1},{5,7},{7,5},{8,10},{10,8},{12,... | collective-permute-start | bytes 3145736 | tf_op jit(solution)/shard_map/ppermute | solution.py:37
  372.1 35.6 %collective-permute-start.35 = (bf16[512,1024]{1,0:T(8,128)(2,1)S(1)}, bf16[512,1024]{1,0:T(8,128)(2,1)}, u32[]{:S(2)}, u32[]{:S(2)}) collective-permute-start(bf16[512,1024]{1,0:T(8,128)(2,1)S(1)} %get-tuple-element.639), channel_id=1, source_target_pairs={{0,1},{1,0},{2,3},{3,2},{4,5},{5,4},{6,7},{7,6},{8,9},{9,8},{10,11... | collective-permute-start | bytes 3145736 | tf_op jit(solution)/shard_map/ppermute | solution.py:37
  382.8 51.8 %collective-permute-start.39 = (bf16[512,2048]{1,0:T(8,128)(2,1)}, bf16[512,2048]{1,0:T(8,128)(2,1)}, u32[]{:S(2)}, u32[]{:S(2)}) collective-permute-start(bf16[512,2048]{1,0:T(8,128)(2,1)} %get-tuple-element.647), channel_id=1, source_target_pairs={{0,16},{8,24},{16,0},{24,8},{1,17},{9,25},{17,1},{25,9},{2,18},{10... | collective-permute-start | bytes 6291464 | tf_op jit(solution)/shard_map/ppermute | solution.py:37
  383.4 51.2 %collective-permute-start.40 = (bf16[512,2048]{1,0:T(8,128)(2,1)}, bf16[512,2048]{1,0:T(8,128)(2,1)}, u32[]{:S(2)}, u32[]{:S(2)}) collective-permute-start(bf16[512,2048]{1,0:T(8,128)(2,1)} %get-tuple-element.648), channel_id=1, source_target_pairs={{0,8},{8,0},{16,24},{24,16},{1,9},{9,1},{17,25},{25,17},{2,10},{10... | collective-permute-start | bytes 6291464 | tf_op jit(solution)/shard_map/ppermute | solution.py:37
  431.8 34.0 %collective-permute-start.38 = (bf16[2,512,1024]{2,1,0:T(8,128)(2,1)}, bf16[2,512,1024]{2,1,0:T(8,128)(2,1)}, u32[]{:S(2)}, u32[]{:S(2)}) collective-permute-start(bf16[2,512,1024]{2,1,0:T(8,128)(2,1)} %get-tuple-element.659), channel_id=1, source_target_pairs={{0,1},{1,0},{2,3},{3,2},{4,5},{5,4},{6,7},{7,6},{8,9},{9,8},{10,11... | collective-permute-start | bytes 6291464 | tf_op jit(solution)/shard_map/ppermute | solution.py:37
  434.6 25.6 %collective-permute-start.41 = (bf16[512,1024]{1,0:T(8,128)(2,1)S(1)}, bf16[512,1024]{1,0:T(8,128)(2,1)S(1)}, u32[]{:S(2)}, u32[]{:S(2)}) collective-permute-start(bf16[512,1024]{1,0:T(8,128)(2,1)S(1)} %get-tuple-element.666), channel_id=1, source_target_pairs={{0,16},{8,24},{16,0},{24,8},{1,17},{9,25},{17,1},{25,9},{2,18},{10... | collective-permute-start | bytes 3145736 | tf_op jit(solution)/shard_map/ppermute | solution.py:37
  436.2 25.3 %collective-permute-start.42 = (bf16[512,1024]{1,0:T(8,128)(2,1)S(1)}, bf16[512,1024]{1,0:T(8,128)(2,1)S(1)}, u32[]{:S(2)}, u32[]{:S(2)}) collective-permute-start(bf16[512,1024]{1,0:T(8,128)(2,1)S(1)} %get-tuple-element.667), channel_id=1, source_target_pairs={{0,8},{8,0},{16,24},{24,16},{1,9},{9,1},{17,25},{25,17},{2,10},{10... | collective-permute-start | bytes 3145736 | tf_op jit(solution)/shard_map/ppermute | solution.py:37
  461.4 28.6 %collective-permute-start.43 = (bf16[256,2048]{1,0:T(8,128)(2,1)}, bf16[256,2048]{1,0:T(8,128)(2,1)}, u32[]{:S(2)}, u32[]{:S(2)}) collective-permute-start(bf16[256,2048]{1,0:T(8,128)(2,1)} %add_convert_fusion.3), channel_id=1, source_target_pairs={{0,8},{8,0},{16,24},{24,16},{1,9},{9,1},{17,25},{25,17},{2,10},{10... | collective-permute-start | bytes 3145736 | tf_op jit(solution)/shard_map/ppermute | solution.py:37
  462.7 27.4 %collective-permute-start.44 = (bf16[256,2048]{1,0:T(8,128)(2,1)}, bf16[256,2048]{1,0:T(8,128)(2,1)}, u32[]{:S(2)}, u32[]{:S(2)}) collective-permute-start(bf16[256,2048]{1,0:T(8,128)(2,1)} %add_convert_fusion.2), channel_id=1, source_target_pairs={{0,16},{8,24},{16,0},{24,8},{1,17},{9,25},{17,1},{25,9},{2,18},{10... | collective-permute-start | bytes 3145736 | tf_op jit(solution)/shard_map/ppermute | solution.py:37
  490.1 59.4 %collective-permute-start.46 = (bf16[512,2048]{1,0:T(8,128)(2,1)}, bf16[512,2048]{1,0:T(8,128)(2,1)}, u32[]{:S(2)}, u32[]{:S(2)}) collective-permute-start(bf16[512,2048]{1,0:T(8,128)(2,1)} %get-tuple-element.704), channel_id=1, source_target_pairs={{0,16},{8,24},{16,0},{24,8},{1,17},{9,25},{17,1},{25,9},{2,18},{10... | collective-permute-start | bytes 6291464 | tf_op jit(solution)/shard_map/ppermute | solution.py:37
  490.9 58.6 %collective-permute-start.47 = (bf16[512,2048]{1,0:T(8,128)(2,1)}, bf16[512,2048]{1,0:T(8,128)(2,1)}, u32[]{:S(2)}, u32[]{:S(2)}) collective-permute-start(bf16[512,2048]{1,0:T(8,128)(2,1)} %get-tuple-element.705), channel_id=1, source_target_pairs={{0,8},{8,0},{16,24},{24,16},{1,9},{9,1},{17,25},{25,17},{2,10},{10... | collective-permute-start | bytes 6291464 | tf_op jit(solution)/shard_map/ppermute | solution.py:37
  493.4 33.7 %collective-permute-start.48 = (bf16[512,1024]{1,0:T(8,128)(2,1)}, bf16[512,1024]{1,0:T(8,128)(2,1)}, u32[]{:S(2)}, u32[]{:S(2)}) collective-permute-start(bf16[512,1024]{1,0:T(8,128)(2,1)} %get-tuple-element.714.refs_2_), channel_id=1, source_target_pairs={{0,1},{1,0},{2,3},{3,2},{4,5},{5,4},{6,7},{7,6},{8,9},{9,8},{10,11... | collective-permute-start | bytes 3145736 | tf_op jit(solution)/shard_map/ppermute | solution.py:37
  517.9 39.4 %collective-permute-start.45 = (bf16[2,512,512]{2,1,0:T(8,128)(2,1)}, bf16[2,512,512]{2,1,0:T(8,128)(2,1)}, u32[]{:S(2)}, u32[]{:S(2)}) collective-permute-start(bf16[2,512,512]{2,1,0:T(8,128)(2,1)} %get-tuple-element.703), channel_id=1, source_target_pairs={{0,2},{2,0},{4,6},{6,4},{1,3},{3,1},{5,7},{7,5},{8,10},{10,8},{12,... | collective-permute-start | bytes 3145736 | tf_op jit(solution)/shard_map/ppermute | solution.py:37
  523.8 42.9 %collective-permute-start.52 = (bf16[2,128,2048]{2,1,0:T(8,128)(2,1)}, bf16[2,128,2048]{2,1,0:T(8,128)(2,1)}, u32[]{:S(2)}, u32[]{:S(2)}) collective-permute-start(bf16[2,128,2048]{2,1,0:T(8,128)(2,1)} %fusion.3), channel_id=1, source_target_pairs={{0,2},{2,0},{4,6},{6,4},{1,3},{3,1},{5,7},{7,5},{8,10},{10,8},{12,... | collective-permute-start | bytes 3145736 | tf_op jit(solution)/shard_map/ppermute | solution.py:37
  548.5 51.9 %collective-permute-start.54 = (bf16[2,512,512]{2,1,0:T(8,128)(2,1)}, bf16[2,512,512]{2,1,0:T(8,128)(2,1)}, u32[]{:S(2)}, u32[]{:S(2)}) collective-permute-start(bf16[2,512,512]{2,1,0:T(8,128)(2,1)} %get-tuple-element.730), channel_id=1, source_target_pairs={{0,2},{2,0},{4,6},{6,4},{1,3},{3,1},{5,7},{7,5},{8,10},{10,8},{12,... | collective-permute-start | bytes 3145736 | tf_op jit(solution)/shard_map/ppermute | solution.py:37
  549.5 29.0 %collective-permute-start.50 = (bf16[256,1024]{1,0:T(8,128)(2,1)S(1)}, bf16[256,1024]{1,0:T(8,128)(2,1)S(1)}, u32[]{:S(2)}, u32[]{:S(2)}) collective-permute-start(bf16[256,1024]{1,0:T(8,128)(2,1)S(1)} %copy-done.136), channel_id=1, source_target_pairs={{0,8},{8,0},{16,24},{24,16},{1,9},{9,1},{17,25},{25,17},{2,10},{10... | collective-permute-start | bytes 1572872 | tf_op jit(solution)/shard_map/ppermute | solution.py:37
  550.6 27.9 %collective-permute-start.51 = (bf16[256,1024]{1,0:T(8,128)(2,1)S(1)}, bf16[256,1024]{1,0:T(8,128)(2,1)S(1)}, u32[]{:S(2)}, u32[]{:S(2)}) collective-permute-start(bf16[256,1024]{1,0:T(8,128)(2,1)S(1)} %copy-done.135), channel_id=1, source_target_pairs={{0,16},{8,24},{16,0},{24,8},{1,17},{9,25},{17,1},{25,9},{2,18},{10... | collective-permute-start | bytes 1572872 | tf_op jit(solution)/shard_map/ppermute | solution.py:37
  569.8 35.2 %collective-permute-start.58 = (bf16[2,64,2048]{2,1,0:T(8,128)(2,1)}, bf16[2,64,2048]{2,1,0:T(8,128)(2,1)}, u32[]{:S(2)}, u32[]{:S(2)}) collective-permute-start(bf16[2,64,2048]{2,1,0:T(8,128)(2,1)} %slice.812), channel_id=1, source_target_pairs={{0,4},{2,6},{4,0},{6,2},{1,5},{3,7},{5,1},{7,3},{8,12},{10,14},{12... | collective-permute-start | bytes 1572872 | tf_op jit(solution)/shard_map/ppermute | solution.py:37
  580.3 50.4 %collective-permute-start.64 = (bf16[2,128,1024]{2,1,0:T(8,128)(2,1)}, bf16[2,128,1024]{2,1,0:T(8,128)(2,1)}, u32[]{:S(2)}, u32[]{:S(2)}) collective-permute-start(bf16[2,128,1024]{2,1,0:T(8,128)(2,1)} %fusion.11), channel_id=1, source_target_pairs={{0,2},{2,0},{4,6},{6,4},{1,3},{3,1},{5,7},{7,5},{8,10},{10,8},{12,... | collective-permute-start | bytes 1572872 | tf_op jit(solution)/shard_map/ppermute | solution.py:37
  580.7 27.1 %collective-permute-start.56 = (bf16[256,2048]{1,0:T(8,128)(2,1)}, bf16[256,2048]{1,0:T(8,128)(2,1)S(1)}, u32[]{:S(2)}, u32[]{:S(2)}) collective-permute-start(bf16[256,2048]{1,0:T(8,128)(2,1)} %add_convert_fusion.1), channel_id=1, source_target_pairs={{0,8},{8,0},{16,24},{24,16},{1,9},{9,1},{17,25},{25,17},{2,10},{10... | collective-permute-start | bytes 3145736 | tf_op jit(solution)/shard_map/ppermute | solution.py:37
  607.8 25.9 %collective-permute-start.59 = (bf16[512,1024]{1,0:T(8,128)(2,1)}, bf16[512,1024]{1,0:T(8,128)(2,1)}, u32[]{:S(2)}, u32[]{:S(2)}) collective-permute-start(bf16[512,1024]{1,0:T(8,128)(2,1)} %get-tuple-element.814), channel_id=1, source_target_pairs={{0,16},{8,24},{16,0},{24,8},{1,17},{9,25},{17,1},{25,9},{2,18},{10... | collective-permute-start | bytes 3145736 | tf_op jit(solution)/shard_map/ppermute | solution.py:37
  615.0 43.5 %collective-permute-start.63 = (bf16[2,128,2048]{2,1,0:T(8,128)(2,1)}, bf16[2,128,2048]{2,1,0:T(8,128)(2,1)}, u32[]{:S(2)}, u32[]{:S(2)}) collective-permute-start(bf16[2,128,2048]{2,1,0:T(8,128)(2,1)} %fusion.1), channel_id=1, source_target_pairs={{0,2},{2,0},{4,6},{6,4},{1,3},{3,1},{5,7},{7,5},{8,10},{10,8},{12,... | collective-permute-start | bytes 3145736 | tf_op jit(solution)/shard_map/ppermute | solution.py:37
  617.6 107.2 %collective-permute-start.53 = (bf16[3,128,1024]{2,1,0:T(8,128)(2,1)}, bf16[3,128,1024]{2,1,0:T(8,128)(2,1)}, u32[]{:S(2)}, u32[]{:S(2)}) collective-permute-start(bf16[3,128,1024]{2,1,0:T(8,128)(2,1)} %pad_maximum_fusion.8), channel_id=1, source_target_pairs={{0,4},{2,6},{4,0},{6,2},{1,5},{3,7},{5,1},{7,3},{8,12},{10,14},{12... | collective-permute-start | bytes 2359304 | tf_op jit(solution)/shard_map/ppermute | solution.py:37
  632.6 46.0 %collective-permute-start.69 = (bf16[2,64,1024]{2,1,0:T(8,128)(2,1)S(1)}, bf16[2,64,1024]{2,1,0:T(8,128)(2,1)S(1)}, u32[]{:S(2)}, u32[]{:S(2)}) collective-permute-start(bf16[2,64,1024]{2,1,0:T(8,128)(2,1)S(1)} %slice.815), channel_id=1, source_target_pairs={{0,4},{2,6},{4,0},{6,2},{1,5},{3,7},{5,1},{7,3},{8,12},{10,14},{12... | collective-permute-start | bytes 786440 | tf_op jit(solution)/shard_map/ppermute | solution.py:37
  634.1 26.6 %collective-permute-start.61 = (bf16[512,1152]{1,0:T(8,128)(2,1)S(1)}, bf16[512,1152]{1,0:T(8,128)(2,1)S(1)}, u32[]{:S(2)}, u32[]{:S(2)}) collective-permute-start(bf16[512,1152]{1,0:T(8,128)(2,1)S(1)} %get-tuple-element.816), channel_id=1, source_target_pairs={{0,16},{8,24},{16,0},{24,8},{1,17},{9,25},{17,1},{25,9},{2,18},{10... | collective-permute-start | bytes 3538952 | tf_op jit(solution)/shard_map/ppermute | solution.py:37
  635.3 26.6 %collective-permute-start.62 = (bf16[512,1152]{1,0:T(8,128)(2,1)S(1)}, bf16[512,1152]{1,0:T(8,128)(2,1)S(1)}, u32[]{:S(2)}, u32[]{:S(2)}) collective-permute-start(bf16[512,1152]{1,0:T(8,128)(2,1)S(1)} %get-tuple-element.817), channel_id=1, source_target_pairs={{0,8},{8,0},{16,24},{24,16},{1,9},{9,1},{17,25},{25,17},{2,10},{10... | collective-permute-start | bytes 3538952 | tf_op jit(solution)/shard_map/ppermute | solution.py:37
  660.2 41.3 %collective-permute-start.71 = (bf16[2,64,2048]{2,1,0:T(8,128)(2,1)S(1)}, bf16[2,64,2048]{2,1,0:T(8,128)(2,1)S(1)}, u32[]{:S(2)}, u32[]{:S(2)}) collective-permute-start(bf16[2,64,2048]{2,1,0:T(8,128)(2,1)S(1)} %slice.811), channel_id=1, source_target_pairs={{0,4},{2,6},{4,0},{6,2},{1,5},{3,7},{5,1},{7,3},{8,12},{10,14},{12... | collective-permute-start | bytes 1572872 | tf_op jit(solution)/shard_map/ppermute | solution.py:37
  698.5 25.7 %collective-permute-start.70 = (bf16[2,128,1152]{2,1,0:T(8,128)(2,1)S(1)}, bf16[2,128,1152]{2,1,0:T(8,128)(2,1)S(1)}, u32[]{:S(2)}, u32[]{:S(2)}) collective-permute-start(bf16[2,128,1152]{2,1,0:T(8,128)(2,1)S(1)} %fusion.7), channel_id=1, source_target_pairs={{0,2},{2,0},{4,6},{6,4},{1,3},{3,1},{5,7},{7,5},{8,10},{10,8},{12,... | collective-permute-start | bytes 1769480 | tf_op jit(solution)/shard_map/ppermute | solution.py:37
  698.5 35.4 %collective-permute-start.74 = (bf16[1,128,1024]{2,1,0:T(8,128)(2,1)S(1)}, bf16[1,128,1024]{2,1,0:T(8,128)(2,1)S(1)}, u32[]{:S(2)}, u32[]{:S(2)}) collective-permute-start(bf16[1,128,1024]{2,1,0:T(8,128)(2,1)S(1)} %fusion.15), channel_id=1, source_target_pairs={{0,4},{2,6},{4,0},{6,2},{1,5},{3,7},{5,1},{7,3},{8,12},{10,14},{12... | collective-permute-start | bytes 786440 | tf_op jit(solution)/shard_map/ppermute | solution.py:37
  700.5 33.3 %collective-permute-start.75 = (bf16[2,64,1024]{2,1,0:T(8,128)(2,1)S(1)}, bf16[2,64,1024]{2,1,0:T(8,128)(2,1)S(1)}, u32[]{:S(2)}, u32[]{:S(2)}) collective-permute-start(bf16[2,64,1024]{2,1,0:T(8,128)(2,1)S(1)} %slice.814), channel_id=1, source_target_pairs={{0,4},{2,6},{4,0},{6,2},{1,5},{3,7},{5,1},{7,3},{8,12},{10,14},{12... | collective-permute-start | bytes 786440 | tf_op jit(solution)/shard_map/ppermute | solution.py:37
  (181 other events, 1787.1 us)
Sparse Core Ops, SparseCore 0:
  86.8 56.9 all-gather.2
  181.7 46.5 all-gather.4

commit v5 on v4

--- a/solution.py
+++ b/solution.py
@@ -42,7 +42,7 @@
 
 
 def params(mib):
-    return pltpu.CompilerParams(vmem_limit_bytes=mib << 20)
+    return pltpu.CompilerParams(vmem_limit_bytes=mib * 5 // 8 << 20)
 
 
 def whole(shape):

time: 757 us -> 736 us (0.972)
  Pallas kernels: 211 us -> 194 us
  other arithmetic: 76.7 us -> 67.5 us
  waiting for transfers between devices: 275 us -> 283 us
    ppermute x78, waiting for transfers between devices: 273 us -> 281 us  [swap(): return lax.ppermute(value, axis, xor_perm(lax.axis_size(axis), bits))]
    unnamed x292 -> x278, local copies, waits for them, and re-layouts: 49.2 us -> 45.6 us
  transfers between devices with their start and end apart: 80 -> 80, of which waited for: 34 -> 33; matrix products, arithmetic and copies ran while one was open for 16% -> 15% of each run, Pallas kernels for 24% -> 23%
where the time goes in v5:
time: 736 us; the launch traced here: 731 us
  waiting for transfers between devices  283 us (38%)
  Pallas kernels  194 us (26%)
  local copies, waits for them, and re-layouts  87.9 us (12%)
  starting transfers between devices  74.7 us (10%)
  other arithmetic  67.5 us (9%)
  between operations  16.5 us (2%)
    ppermute x78, waiting for transfers between devices, swap(): return lax.ppermute(value, axis, xor_perm(lax.axis_size(axis), bits))  281 us
    ppermute x78, starting transfers between devices, swap(): return lax.ppermute(value, axis, xor_perm(lax.axis_size(axis), bits))  74.6 us
    pallas_call x3, Pallas kernels, attend_back(): pl.pallas_call(attend_back_body, grid=(width // LANES,), in_specs=[spec]...  45.8 us
    unnamed x278, local copies, waits for them, and re-layouts  45.6 us
    pallas_call x10, Pallas kernels, weight_grad(): pl.pallas_call(body, grid_spec=pltpu.PrefetchScalarGridSpec(num_scalar_pr...  36.4 us
    pallas_call x3, Pallas kernels, attend(): pl.pallas_call(functools.partial(attend_body, 256), grid=(width // LANES,...  29.7 us
    pallas_call x2, Pallas kernels, feed(): pl.pallas_call(body, grid=(hidden // TILE,), in_specs=[same, same, same,...  20.2 us
    pallas_call x4, Pallas kernels, place(): pl.pallas_call(body, out_shape=[shaped((total, width), LOW) for _, _, wid...  16 us
  transfers between devices with their start and end apart: 80, of which 33 were waited for; matrix products, arithmetic and copies ran while one was open for 15% of the time, Pallas kernels for 23%

profile of v5, /device:TPU:0, one launch (start us, length us, event | category | flops | bytes accessed | tf_op | source)
XLA Modules:
  0.0 730.7 jit_solution(8900723174362919924)
XLA Ops:
  20.5 9.8 %collective-permute-done = bf16[2,64,1152]{2,1,0:T(8,128)(2,1)S(1)} collective-permute-done((bf16[2,64,1152]{2,1,0:T(8,128)(2,1)S(1)}, bf16[2,64,1152]{2,1,0:T(8,128)(2,1)S(1)}, u32[]{:S(2)}, u32[]{:S(2)}) %collective-permute-start) | collective-permute-done | bytes 294944 | tf_op jit(solution)/shard_map/ppermute | solution.py:37
  30.4 4.1 collective-permute-start.2
  36.2 19.2 %collective-permute-done.1 = bf16[2,64,2048]{2,1,0:T(8,128)(2,1)S(1)} collective-permute-done((bf16[2,64,2048]{2,1,0:T(8,128)(2,1)S(1)}, bf16[2,64,2048]{2,1,0:T(8,128)(2,1)S(1)}, u32[]{:S(2)}, u32[]{:S(2)}) %collective-permute-start.1) | collective-permute-done | bytes 524320 | tf_op jit(solution)/shard_map/ppermute | solution.py:37
  64.6 22.1 %collective-permute-done.3 = bf16[2,128,2048]{2,1,0:T(8,128)(2,1)} collective-permute-done((bf16[2,128,2048]{2,1,0:T(8,128)(2,1)}, bf16[2,128,2048]{2,1,0:T(8,128)(2,1)}, u32[]{:S(2)}, u32[]{:S(2)}) %collective-permute-start.3) | collective-permute-done | bytes 1048608 | tf_op jit(solution)/shard_map/ppermute | solution.py:37
  106.9 3.0 fusion.5
  112.7 3.3 shard_map.359
  120.2 6.9 collective-permute-done.8
  130.4 3.2 shard_map.360
  135.1 12.8 %collective-permute-done.15.refs_2_ = bf16[2,256,2048]{2,1,0:T(8,128)(2,1)} collective-permute-done((bf16[2,256,2048]{2,1,0:T(8,128)(2,1)}, bf16[2,256,2048]{2,1,0:T(8,128)(2,1)}, u32[]{:S(2)}, u32[]{:S(2)}) %collective-permute-start.15) | collective-permute-done | bytes 2097184 | tf_op jit(solution)/shard_map/ppermute | solution.py:37
  155.5 19.2 %collective-permute-done.18.refs_4_ = bf16[256,2048]{1,0:T(8,128)(2,1)} collective-permute-done((bf16[256,2048]{1,0:T(8,128)(2,1)}, bf16[256,2048]{1,0:T(8,128)(2,1)}, u32[]{:S(2)}, u32[]{:S(2)}) %collective-permute-start.18) | collective-permute-done | bytes 1048608 | tf_op jit(solution)/shard_map/ppermute | solution.py:37
  182.6 3.5 collective-permute-start.12
  187.1 9.8 %shard_map.361 = (bf16[512,512]{1,0:T(8,128)(2,1)S(1)}, f32[512,512]{1,0:T(8,128)S(1)}) custom-call(bf16[512,512]{1,0:T(8,128)(2,1)S(1)} %copy-done.54, bf16[2,512,512]{2,1,0:T(8,128)(2,1)} %get-tuple-element.723.ko_ref.vo_ref, bf16[2,512,512]{2,1,0:T(8,128)(2,1)} %collective-permute-done.13.kp_ref.vp_ref, ...), custom_call_target="tpu_custom_call" | custom-call | flops 1 | bytes 1 | tf_op jit(solution)/shard_map/pallas_call | solution.py:556
  200.7 5.3 shard_map.362
  206.9 3.1 shard_map.363
  212.6 7.4 %collective-permute-done.21.refs_2_ = bf16[2,256,2048]{2,1,0:T(8,128)(2,1)} collective-permute-done((bf16[2,256,2048]{2,1,0:T(8,128)(2,1)}, bf16[2,256,2048]{2,1,0:T(8,128)(2,1)}, u32[]{:S(2)}, u32[]{:S(2)}) %collective-permute-start.21) | collective-permute-done | bytes 2097184 | tf_op jit(solution)/shard_map/ppermute | solution.py:37
  228.4 19.5 %collective-permute-done.23.refs_4_ = bf16[256,2048]{1,0:T(8,128)(2,1)} collective-permute-done((bf16[256,2048]{1,0:T(8,128)(2,1)}, bf16[256,2048]{1,0:T(8,128)(2,1)}, u32[]{:S(2)}, u32[]{:S(2)}) %collective-permute-start.23) | collective-permute-done | bytes 1048608 | tf_op jit(solution)/shard_map/ppermute | solution.py:37
  251.7 4.0 collective-permute-start.26
  258.3 10.0 %shard_map.364 = (bf16[512,512]{1,0:T(8,128)(2,1)S(1)}, f32[512,512]{1,0:T(8,128)S(1)}) custom-call(bf16[512,512]{1,0:T(8,128)(2,1)S(1)} %copy-done.56, bf16[2,512,512]{2,1,0:T(8,128)(2,1)} %get-tuple-element.696.ko_ref.vo_ref, bf16[2,512,512]{2,1,0:T(8,128)(2,1)} %collective-permute-done.19.kp_ref.vp_ref, ...), custom_call_target="tpu_custom_call" | custom-call | flops 1 | bytes 1 | tf_op jit(solution)/shard_map/pallas_call | solution.py:556
  275.8 4.0 shard_map.365
  279.9 11.6 %shard_map.366 = (bf16[512,1024]{1,0:T(8,128)(2,1)S(1)}, f32[512,1024]{1,0:T(8,128)S(1)}, bf16[512,2048]{1,0:T(8,128)(2,1)S(1)}, bf16[512,2048]{1,0:T(8,128)(2,1)S(1)}, bf16[512,1024]{1,0:T(8,128)(2,1)S(1)}) custom-call(bf16[512,1024]{1,0:T(8,128)(2,1)S(1)} %copy-done.4, bf16[512,1024]{1,0:T(8,128)(2,1)} %convolution_convert_fusion.2.one_ref, ...), custom_call_target="tpu_custom_call" | custom-call | flops 1 | bytes 1 | tf_op jit(solution)/shard_map/pallas_call | solution.py:707
  309.4 13.7 %collective-permute-done.33.refs_4_ = bf16[256,2048]{1,0:T(8,128)(2,1)S(1)} collective-permute-done((bf16[256,2048]{1,0:T(8,128)(2,1)S(1)}, bf16[256,2048]{1,0:T(8,128)(2,1)S(1)}, u32[]{:S(2)}, u32[]{:S(2)}) %collective-permute-start.33) | collective-permute-done | bytes 1048608 | tf_op jit(solution)/shard_map/ppermute | solution.py:37
  329.2 3.5 shard_map.369
  332.8 10.0 %shard_map.370 = (bf16[512,512]{1,0:T(8,128)(2,1)S(1)}, f32[512,512]{1,0:T(8,128)S(1)}) custom-call(bf16[512,512]{1,0:T(8,128)(2,1)S(1)} %bitcast.191, bf16[2,512,512]{2,1,0:T(8,128)(2,1)} %get-tuple-element.623.ko_ref.vo_ref, bf16[2,512,512]{2,1,0:T(8,128)(2,1)} %collective-permute-done.31.kp_ref.vp_ref, ...), custom_call_target="tpu_custom_call" | custom-call | flops 1 | bytes 1 | tf_op jit(solution)/shard_map/pallas_call | solution.py:556
  346.3 8.6 %shard_map.371 = (bf16[512,1024]{1,0:T(8,128)(2,1)S(1)}, f32[512,1024]{1,0:T(8,128)S(1)}, bf16[512,2048]{1,0:T(8,128)(2,1)S(1)}, bf16[512,2048]{1,0:T(8,128)(2,1)S(1)}, bf16[512,1024]{1,0:T(8,128)(2,1)S(1)}) custom-call(f32[512,1024]{1,0:T(8,128)S(1)} %copy-done.24, bf16[512,1024]{1,0:T(8,128)(2,1)S(1)} %convolution_convert_fusion.one_ref, ...), custom_call_target="tpu_custom_call" | custom-call | flops 1 | bytes 1 | tf_op jit(solution)/shard_map/pallas_call | solution.py:707
  354.9 6.9 shard_map.372
  362.4 4.1 shard_map.373
  366.5 4.1 shard_map.374
  376.2 15.5 %shard_map.376 = (bf16[512,512]{1,0:T(8,128)(2,1)S(1)}, bf16[2,512,512]{2,1,0:T(8,128)(2,1)S(1)}, bf16[2,512,512]{2,1,0:T(8,128)(2,1)S(1)}) custom-call(bf16[512,512]{1,0:T(8,128)(2,1)S(1)} %bitcast.192, bf16[2,512,512]{2,1,0:T(8,128)(2,1)} %get-tuple-element.623.ko_ref.vo_ref, bf16[2,512,512]{2,1,0:T(8,128)(2,1)} %collective-permute-done.31.kp_ref.vp_ref, ...), custom_call_target="tpu_custom_call" | custom-call | flops 1 | bytes 1 | tf_op jit(solution)/shard_map/pallas_call | solution.py:611
  392.4 3.0 shard_map.377
  397.9 18.4 %collective-permute-done.37.came_ref = bf16[2,512,512]{2,1,0:T(8,128)(2,1)S(1)} collective-permute-done((bf16[2,512,512]{2,1,0:T(8,128)(2,1)S(1)}, bf16[2,512,512]{2,1,0:T(8,128)(2,1)S(1)}, u32[]{:S(2)}, u32[]{:S(2)}) %collective-permute-start.37) | collective-permute-done | bytes 1048608 | tf_op jit(solution)/shard_map/ppermute | solution.py:37
  416.4 3.3 shard_map.378
  428.1 20.1 %collective-permute-done.41 = bf16[512,1024]{1,0:T(8,128)(2,1)S(1)} collective-permute-done((bf16[512,1024]{1,0:T(8,128)(2,1)S(1)}, bf16[512,1024]{1,0:T(8,128)(2,1)S(1)}, u32[]{:S(2)}, u32[]{:S(2)}) %collective-permute-start.41) | collective-permute-done | bytes 1048608 | tf_op jit(solution)/shard_map/ppermute | solution.py:37
  458.9 6.9 shard_map.380
  465.8 4.1 shard_map.381
  472.0 4.1 shard_map.382
  484.6 15.2 %shard_map.384 = (bf16[512,512]{1,0:T(8,128)(2,1)S(1)}, bf16[2,512,512]{2,1,0:T(8,128)(2,1)S(1)}, bf16[2,512,512]{2,1,0:T(8,128)(2,1)S(1)}) custom-call(bf16[512,512]{1,0:T(8,128)(2,1)S(1)} %copy-done.57, bf16[2,512,512]{2,1,0:T(8,128)(2,1)} %get-tuple-element.696.ko_ref.vo_ref, bf16[2,512,512]{2,1,0:T(8,128)(2,1)} %collective-permute-done.19.kp_ref.vp_ref, ...), custom_call_target="tpu_custom_call" | custom-call | flops 1 | bytes 1 | tf_op jit(solution)/shard_map/pallas_call | solution.py:611
  511.5 15.1 %shard_map.386 = (bf16[512,512]{1,0:T(8,128)(2,1)S(1)}, bf16[2,512,512]{2,1,0:T(8,128)(2,1)S(1)}, bf16[2,512,512]{2,1,0:T(8,128)(2,1)S(1)}) custom-call(bf16[512,512]{1,0:T(8,128)(2,1)S(1)} %copy-done.55, bf16[2,512,512]{2,1,0:T(8,128)(2,1)} %get-tuple-element.723.ko_ref.vo_ref, bf16[2,512,512]{2,1,0:T(8,128)(2,1)} %collective-permute-done.13.kp_ref.vp_ref, ...), custom_call_target="tpu_custom_call" | custom-call | flops 1 | bytes 1 | tf_op jit(solution)/shard_map/pallas_call | solution.py:611
  536.8 11.7 %collective-permute-done.52 = bf16[2,128,2048]{2,1,0:T(8,128)(2,1)S(1)} collective-permute-done((bf16[2,128,2048]{2,1,0:T(8,128)(2,1)}, bf16[2,128,2048]{2,1,0:T(8,128)(2,1)S(1)}, u32[]{:S(2)}, u32[]{:S(2)}) %collective-permute-start.52) | collective-permute-done | bytes 1048608 | tf_op jit(solution)/shard_map/ppermute | solution.py:37
  553.2 4.0 shard_map.388
  557.2 3.8 shard_map.389
  568.4 13.7 %collective-permute-done.54.came_ref = bf16[2,512,512]{2,1,0:T(8,128)(2,1)S(1)} collective-permute-done((bf16[2,512,512]{2,1,0:T(8,128)(2,1)S(1)}, bf16[2,512,512]{2,1,0:T(8,128)(2,1)S(1)}, u32[]{:S(2)}, u32[]{:S(2)}) %collective-permute-start.54) | collective-permute-done | bytes 1048608 | tf_op jit(solution)/shard_map/ppermute | solution.py:37
  603.3 3.1 shard_map.393
  606.4 3.2 shard_map.394
  618.1 19.9 %collective-permute-done.63 = bf16[2,128,2048]{2,1,0:T(8,128)(2,1)} collective-permute-done((bf16[2,128,2048]{2,1,0:T(8,128)(2,1)}, bf16[2,128,2048]{2,1,0:T(8,128)(2,1)}, u32[]{:S(2)}, u32[]{:S(2)}) %collective-permute-start.63) | collective-permute-done | bytes 1048608 | tf_op jit(solution)/shard_map/ppermute | solution.py:37
  643.4 15.3 %collective-permute-done.69 = bf16[2,64,1024]{2,1,0:T(8,128)(2,1)S(1)} collective-permute-done((bf16[2,64,1024]{2,1,0:T(8,128)(2,1)S(1)}, bf16[2,64,1024]{2,1,0:T(8,128)(2,1)S(1)}, u32[]{:S(2)}, u32[]{:S(2)}) %collective-permute-start.69) | collective-permute-done | bytes 262176 | tf_op jit(solution)/shard_map/ppermute | solution.py:37
  664.2 5.3 collective-permute-done.67
  671.0 6.8 collective-permute-done.72
  682.3 21.2 %collective-permute-done.70 = bf16[2,128,1152]{2,1,0:T(8,128)(2,1)S(1)} collective-permute-done((bf16[2,128,1152]{2,1,0:T(8,128)(2,1)S(1)}, bf16[2,128,1152]{2,1,0:T(8,128)(2,1)S(1)}, u32[]{:S(2)}, u32[]{:S(2)}) %collective-permute-start.70) | collective-permute-done | bytes 589856 | tf_op jit(solution)/shard_map/ppermute | solution.py:37
  (628 shorter events, 268.1 us)
Async XLA Ops:
  7.2 148.2 %all-gather.3.cloned.1.call-start = ((), (), s32[]{:S(2)}) async-start(), calls=%async_computation | async-start | bytes 2621440 | tf_op jit(solution)/shard_map/all_gather | solution.py:173
  8.9 25.7 %collective-permute-start.4 = (f32[8,128]{1,0:T(8,128)S(1)}, f32[8,128]{1,0:T(8,128)S(1)}, u32[]{:S(2)}, u32[]{:S(2)}) collective-permute-start(f32[8,128]{1,0:T(8,128)S(1)} %pad.13), channel_id=1, source_target_pairs={{0,8},{8,0},{16,24},{24,16},{1,9},{9,1},{17,25},{25,17},{2,10},{10... | collective-permute-start | bytes 12296 | tf_op jit(solution)/shard_map/ppermute | solution.py:37
  30.4 26.5 %collective-permute-start.2 = (bf16[2,128,1152]{2,1,0:T(8,128)(2,1)S(1)}, bf16[2,128,1152]{2,1,0:T(8,128)(2,1)S(1)}, u32[]{:S(2)}, u32[]{:S(2)}) collective-permute-start(bf16[2,128,1152]{2,1,0:T(8,128)(2,1)S(1)} %constant_dynamic-update-slice_fusion.2), channel_id=1, source_target_pairs={{0,2},{2,0},{4,6},{6,4},{1,3},{3,1},{5,7},{7,5},{8,10},{10,8},{12,... | collective-permute-start | bytes 1769480 | tf_op jit(solution)/shard_map/ppermute | solution.py:37
  58.7 28.0 %collective-permute-start.7 = (bf16[2,256,1152]{2,1,0:T(8,128)(2,1)}, bf16[2,256,1152]{2,1,0:T(8,128)(2,1)S(1)}, u32[]{:S(2)}, u32[]{:S(2)}) collective-permute-start(bf16[2,256,1152]{2,1,0:T(8,128)(2,1)} %constant_dynamic-update-slice_fusion.4.refs_0_), channel_id=1, source_target_pairs={{0,16},{8,24},{16,0},{24,8},{1,17},{9,25},{17,1},{25,9},{2,18},{10... | collective-permute-start | bytes 3538952 | tf_op jit(solution)/shard_map/ppermute | solution.py:37
  60.2 27.0 %collective-permute-start.6 = (bf16[2,256,1152]{2,1,0:T(8,128)(2,1)}, bf16[2,256,1152]{2,1,0:T(8,128)(2,1)S(1)}, u32[]{:S(2)}, u32[]{:S(2)}) collective-permute-start(bf16[2,256,1152]{2,1,0:T(8,128)(2,1)} %constant_dynamic-update-slice_fusion.4.refs_0_), channel_id=1, source_target_pairs={{0,8},{8,0},{16,24},{24,16},{1,9},{9,1},{17,25},{25,17},{2,10},{10... | collective-permute-start | bytes 3538952 | tf_op jit(solution)/shard_map/ppermute | solution.py:37
  86.7 141.7 %all-gather.5.cloned.1.call-start = ((), (), s32[]{:S(2)}) async-start(), calls=%async_computation.1 | async-start | bytes 2621440 | tf_op jit(solution)/shard_map/all_gather | solution.py:173
  97.2 29.9 %collective-permute-start.8 = (bf16[128,1024]{1,0:T(8,128)(2,1)}, bf16[128,1024]{1,0:T(8,128)(2,1)}, u32[]{:S(2)}, u32[]{:S(2)}) collective-permute-start(bf16[128,1024]{1,0:T(8,128)(2,1)} %constant_dynamic-slice_fusion.4), channel_id=1, source_target_pairs={{0,4},{2,6},{4,0},{6,2},{1,5},{3,7},{5,1},{7,3},{8,12},{10,14},{12... | collective-permute-start | bytes 786440 | tf_op jit(solution)/shard_map/ppermute | solution.py:37
  103.3 44.7 %collective-permute-start.15 = (bf16[2,256,2048]{2,1,0:T(8,128)(2,1)}, bf16[2,256,2048]{2,1,0:T(8,128)(2,1)}, u32[]{:S(2)}, u32[]{:S(2)}) collective-permute-start(bf16[2,256,2048]{2,1,0:T(8,128)(2,1)} %constant_dynamic-update-slice_fusion.6.refs_0_), channel_id=1, source_target_pairs={{0,16},{8,24},{16,0},{24,8},{1,17},{9,25},{17,1},{25,9},{2,18},{10... | collective-permute-start | bytes 6291464 | tf_op jit(solution)/shard_map/ppermute | solution.py:37
  103.8 44.1 %collective-permute-start.14 = (bf16[2,256,2048]{2,1,0:T(8,128)(2,1)}, bf16[2,256,2048]{2,1,0:T(8,128)(2,1)}, u32[]{:S(2)}, u32[]{:S(2)}) collective-permute-start(bf16[2,256,2048]{2,1,0:T(8,128)(2,1)} %constant_dynamic-update-slice_fusion.6.refs_0_), channel_id=1, source_target_pairs={{0,8},{8,0},{16,24},{24,16},{1,9},{9,1},{17,25},{25,17},{2,10},{10... | collective-permute-start | bytes 6291464 | tf_op jit(solution)/shard_map/ppermute | solution.py:37
  155.4 30.6 %collective-permute-start.13 = (bf16[2,512,512]{2,1,0:T(8,128)(2,1)}, bf16[2,512,512]{2,1,0:T(8,128)(2,1)}, u32[]{:S(2)}, u32[]{:S(2)}) collective-permute-start(bf16[2,512,512]{2,1,0:T(8,128)(2,1)} %get-tuple-element.723.ko_ref.vo_ref), channel_id=1, source_target_pairs={{0,2},{2,0},{4,6},{6,4},{1,3},{3,1},{5,7},{7,5},{8,10},{10,8},{12,... | collective-permute-start | bytes 3145736 | tf_op jit(solution)/shard_map/ppermute | solution.py:37
  177.2 42.7 %collective-permute-start.21 = (bf16[2,256,2048]{2,1,0:T(8,128)(2,1)}, bf16[2,256,2048]{2,1,0:T(8,128)(2,1)}, u32[]{:S(2)}, u32[]{:S(2)}) collective-permute-start(bf16[2,256,2048]{2,1,0:T(8,128)(2,1)} %all-gather.3.cloned.1.call-done.refs_0_), channel_id=1, source_target_pairs={{0,16},{8,24},{16,0},{24,8},{1,17},{9,25},{17,1},{25,9},{2,18},{10... | collective-permute-start | bytes 6291464 | tf_op jit(solution)/shard_map/ppermute | solution.py:37
  178.8 41.2 %collective-permute-start.20 = (bf16[2,256,2048]{2,1,0:T(8,128)(2,1)}, bf16[2,256,2048]{2,1,0:T(8,128)(2,1)}, u32[]{:S(2)}, u32[]{:S(2)}) collective-permute-start(bf16[2,256,2048]{2,1,0:T(8,128)(2,1)} %all-gather.3.cloned.1.call-done.refs_0_), channel_id=1, source_target_pairs={{0,8},{8,0},{16,24},{24,16},{1,9},{9,1},{17,25},{25,17},{2,10},{10... | collective-permute-start | bytes 6291464 | tf_op jit(solution)/shard_map/ppermute | solution.py:37
  226.0 29.7 %collective-permute-start.19 = (bf16[2,512,512]{2,1,0:T(8,128)(2,1)}, bf16[2,512,512]{2,1,0:T(8,128)(2,1)}, u32[]{:S(2)}, u32[]{:S(2)}) collective-permute-start(bf16[2,512,512]{2,1,0:T(8,128)(2,1)} %get-tuple-element.696.ko_ref.vo_ref), channel_id=1, source_target_pairs={{0,2},{2,0},{4,6},{6,4},{1,3},{3,1},{5,7},{7,5},{8,10},{10,8},{12,... | collective-permute-start | bytes 3145736 | tf_op jit(solution)/shard_map/ppermute | solution.py:37
  248.5 45.5 %collective-permute-start.30 = (bf16[2,256,2048]{2,1,0:T(8,128)(2,1)}, bf16[2,256,2048]{2,1,0:T(8,128)(2,1)}, u32[]{:S(2)}, u32[]{:S(2)}) collective-permute-start(bf16[2,256,2048]{2,1,0:T(8,128)(2,1)} %all-gather.5.cloned.1.call-done.refs_0_), channel_id=1, source_target_pairs={{0,16},{8,24},{16,0},{24,8},{1,17},{9,25},{17,1},{25,9},{2,18},{10... | collective-permute-start | bytes 6291464 | tf_op jit(solution)/shard_map/ppermute | solution.py:37
  249.3 44.7 %collective-permute-start.29 = (bf16[2,256,2048]{2,1,0:T(8,128)(2,1)}, bf16[2,256,2048]{2,1,0:T(8,128)(2,1)}, u32[]{:S(2)}, u32[]{:S(2)}) collective-permute-start(bf16[2,256,2048]{2,1,0:T(8,128)(2,1)} %all-gather.5.cloned.1.call-done.refs_0_), channel_id=1, source_target_pairs={{0,8},{8,0},{16,24},{24,16},{1,9},{9,1},{17,25},{25,17},{2,10},{10... | collective-permute-start | bytes 6291464 | tf_op jit(solution)/shard_map/ppermute | solution.py:37
  270.6 32.8 %collective-permute-start.24 = (bf16[512,1024]{1,0:T(8,128)(2,1)}, bf16[512,1024]{1,0:T(8,128)(2,1)}, u32[]{:S(2)}, u32[]{:S(2)}) collective-permute-start(bf16[512,1024]{1,0:T(8,128)(2,1)} %convolution_convert_fusion.1.refs_1_), channel_id=1, source_target_pairs={{0,1},{1,0},{2,3},{3,2},{4,5},{5,4},{6,7},{7,6},{8,9},{9,8},{10,11... | collective-permute-start | bytes 3145736 | tf_op jit(solution)/shard_map/ppermute | solution.py:37
  297.6 25.5 %collective-permute-start.33 = (bf16[256,2048]{1,0:T(8,128)(2,1)S(1)}, bf16[256,2048]{1,0:T(8,128)(2,1)S(1)}, u32[]{:S(2)}, u32[]{:S(2)}) collective-permute-start(bf16[256,2048]{1,0:T(8,128)(2,1)S(1)} %slice_bitcast_fusion.5), channel_id=1, source_target_pairs={{0,8},{8,0},{16,24},{24,16},{1,9},{9,1},{17,25},{25,17},{2,10},{10... | collective-permute-start | bytes 3145736 | tf_op jit(solution)/shard_map/ppermute | solution.py:37
  298.1 25.9 %collective-permute-start.32 = (bf16[256,2048]{1,0:T(8,128)(2,1)S(1)}, bf16[256,2048]{1,0:T(8,128)(2,1)S(1)}, u32[]{:S(2)}, u32[]{:S(2)}) collective-permute-start(bf16[256,2048]{1,0:T(8,128)(2,1)S(1)} %slice_bitcast_fusion.6), channel_id=1, source_target_pairs={{0,16},{8,24},{16,0},{24,8},{1,17},{9,25},{17,1},{25,9},{2,18},{10... | collective-permute-start | bytes 3145736 | tf_op jit(solution)/shard_map/ppermute | solution.py:37
  302.4 30.4 %collective-permute-start.31 = (bf16[2,512,512]{2,1,0:T(8,128)(2,1)}, bf16[2,512,512]{2,1,0:T(8,128)(2,1)}, u32[]{:S(2)}, u32[]{:S(2)}) collective-permute-start(bf16[2,512,512]{2,1,0:T(8,128)(2,1)} %get-tuple-element.623.ko_ref.vo_ref), channel_id=1, source_target_pairs={{0,2},{2,0},{4,6},{6,4},{1,3},{3,1},{5,7},{7,5},{8,10},{10,8},{12,... | collective-permute-start | bytes 3145736 | tf_op jit(solution)/shard_map/ppermute | solution.py:37
  362.0 34.5 %collective-permute-start.35 = (bf16[512,1024]{1,0:T(8,128)(2,1)S(1)}, bf16[512,1024]{1,0:T(8,128)(2,1)S(1)}, u32[]{:S(2)}, u32[]{:S(2)}) collective-permute-start(bf16[512,1024]{1,0:T(8,128)(2,1)S(1)} %get-tuple-element.639), channel_id=1, source_target_pairs={{0,1},{1,0},{2,3},{3,2},{4,5},{5,4},{6,7},{7,6},{8,9},{9,8},{10,11... | collective-permute-start | bytes 3145736 | tf_op jit(solution)/shard_map/ppermute | solution.py:37
  370.6 51.8 %collective-permute-start.39 = (bf16[512,2048]{1,0:T(8,128)(2,1)S(1)}, bf16[512,2048]{1,0:T(8,128)(2,1)S(1)}, u32[]{:S(2)}, u32[]{:S(2)}) collective-permute-start(bf16[512,2048]{1,0:T(8,128)(2,1)S(1)} %get-tuple-element.647), channel_id=1, source_target_pairs={{0,16},{8,24},{16,0},{24,8},{1,17},{9,25},{17,1},{25,9},{2,18},{10... | collective-permute-start | bytes 6291464 | tf_op jit(solution)/shard_map/ppermute | solution.py:37
  371.2 51.2 %collective-permute-start.40 = (bf16[512,2048]{1,0:T(8,128)(2,1)S(1)}, bf16[512,2048]{1,0:T(8,128)(2,1)S(1)}, u32[]{:S(2)}, u32[]{:S(2)}) collective-permute-start(bf16[512,2048]{1,0:T(8,128)(2,1)S(1)} %get-tuple-element.648), channel_id=1, source_target_pairs={{0,8},{8,0},{16,24},{24,16},{1,9},{9,1},{17,25},{25,17},{2,10},{10... | collective-permute-start | bytes 6291464 | tf_op jit(solution)/shard_map/ppermute | solution.py:37
  419.6 34.2 %collective-permute-start.38 = (bf16[2,512,1024]{2,1,0:T(8,128)(2,1)}, bf16[2,512,1024]{2,1,0:T(8,128)(2,1)}, u32[]{:S(2)}, u32[]{:S(2)}) collective-permute-start(bf16[2,512,1024]{2,1,0:T(8,128)(2,1)} %get-tuple-element.659), channel_id=1, source_target_pairs={{0,1},{1,0},{2,3},{3,2},{4,5},{5,4},{6,7},{7,6},{8,9},{9,8},{10,11... | collective-permute-start | bytes 6291464 | tf_op jit(solution)/shard_map/ppermute | solution.py:37
  422.5 25.6 %collective-permute-start.41 = (bf16[512,1024]{1,0:T(8,128)(2,1)S(1)}, bf16[512,1024]{1,0:T(8,128)(2,1)S(1)}, u32[]{:S(2)}, u32[]{:S(2)}) collective-permute-start(bf16[512,1024]{1,0:T(8,128)(2,1)S(1)} %get-tuple-element.666), channel_id=1, source_target_pairs={{0,16},{8,24},{16,0},{24,8},{1,17},{9,25},{17,1},{25,9},{2,18},{10... | collective-permute-start | bytes 3145736 | tf_op jit(solution)/shard_map/ppermute | solution.py:37
  424.0 25.3 %collective-permute-start.42 = (bf16[512,1024]{1,0:T(8,128)(2,1)S(1)}, bf16[512,1024]{1,0:T(8,128)(2,1)S(1)}, u32[]{:S(2)}, u32[]{:S(2)}) collective-permute-start(bf16[512,1024]{1,0:T(8,128)(2,1)S(1)} %get-tuple-element.667), channel_id=1, source_target_pairs={{0,8},{8,0},{16,24},{24,16},{1,9},{9,1},{17,25},{25,17},{2,10},{10... | collective-permute-start | bytes 3145736 | tf_op jit(solution)/shard_map/ppermute | solution.py:37
  449.3 26.7 %collective-permute-start.43 = (bf16[256,2048]{1,0:T(8,128)(2,1)}, bf16[256,2048]{1,0:T(8,128)(2,1)}, u32[]{:S(2)}, u32[]{:S(2)}) collective-permute-start(bf16[256,2048]{1,0:T(8,128)(2,1)} %add_convert_fusion.3), channel_id=1, source_target_pairs={{0,8},{8,0},{16,24},{24,16},{1,9},{9,1},{17,25},{25,17},{2,10},{10... | collective-permute-start | bytes 3145736 | tf_op jit(solution)/shard_map/ppermute | solution.py:37
  450.6 25.5 %collective-permute-start.44 = (bf16[256,2048]{1,0:T(8,128)(2,1)}, bf16[256,2048]{1,0:T(8,128)(2,1)}, u32[]{:S(2)}, u32[]{:S(2)}) collective-permute-start(bf16[256,2048]{1,0:T(8,128)(2,1)} %add_convert_fusion.2), channel_id=1, source_target_pairs={{0,16},{8,24},{16,0},{24,8},{1,17},{9,25},{17,1},{25,9},{2,18},{10... | collective-permute-start | bytes 3145736 | tf_op jit(solution)/shard_map/ppermute | solution.py:37
  476.1 52.1 %collective-permute-start.46 = (bf16[512,2048]{1,0:T(8,128)(2,1)S(1)}, bf16[512,2048]{1,0:T(8,128)(2,1)}, u32[]{:S(2)}, u32[]{:S(2)}) collective-permute-start(bf16[512,2048]{1,0:T(8,128)(2,1)S(1)} %get-tuple-element.704), channel_id=1, source_target_pairs={{0,16},{8,24},{16,0},{24,8},{1,17},{9,25},{17,1},{25,9},{2,18},{10... | collective-permute-start | bytes 6291464 | tf_op jit(solution)/shard_map/ppermute | solution.py:37
  476.9 51.3 %collective-permute-start.47 = (bf16[512,2048]{1,0:T(8,128)(2,1)S(1)}, bf16[512,2048]{1,0:T(8,128)(2,1)}, u32[]{:S(2)}, u32[]{:S(2)}) collective-permute-start(bf16[512,2048]{1,0:T(8,128)(2,1)S(1)} %get-tuple-element.705), channel_id=1, source_target_pairs={{0,8},{8,0},{16,24},{24,16},{1,9},{9,1},{17,25},{25,17},{2,10},{10... | collective-permute-start | bytes 6291464 | tf_op jit(solution)/shard_map/ppermute | solution.py:37
  479.4 28.2 %collective-permute-start.48 = (bf16[512,1024]{1,0:T(8,128)(2,1)S(1)}, bf16[512,1024]{1,0:T(8,128)(2,1)S(1)}, u32[]{:S(2)}, u32[]{:S(2)}) collective-permute-start(bf16[512,1024]{1,0:T(8,128)(2,1)S(1)} %get-tuple-element.714.refs_2_), channel_id=1, source_target_pairs={{0,1},{1,0},{2,3},{3,2},{4,5},{5,4},{6,7},{7,6},{8,9},{9,8},{10,11... | collective-permute-start | bytes 3145736 | tf_op jit(solution)/shard_map/ppermute | solution.py:37
  499.9 34.0 %collective-permute-start.45 = (bf16[2,512,512]{2,1,0:T(8,128)(2,1)S(1)}, bf16[2,512,512]{2,1,0:T(8,128)(2,1)S(1)}, u32[]{:S(2)}, u32[]{:S(2)}) collective-permute-start(bf16[2,512,512]{2,1,0:T(8,128)(2,1)S(1)} %get-tuple-element.703), channel_id=1, source_target_pairs={{0,2},{2,0},{4,6},{6,4},{1,3},{3,1},{5,7},{7,5},{8,10},{10,8},{12,... | collective-permute-start | bytes 3145736 | tf_op jit(solution)/shard_map/ppermute | solution.py:37
  505.6 42.8 %collective-permute-start.52 = (bf16[2,128,2048]{2,1,0:T(8,128)(2,1)}, bf16[2,128,2048]{2,1,0:T(8,128)(2,1)S(1)}, u32[]{:S(2)}, u32[]{:S(2)}) collective-permute-start(bf16[2,128,2048]{2,1,0:T(8,128)(2,1)} %fusion.3), channel_id=1, source_target_pairs={{0,2},{2,0},{4,6},{6,4},{1,3},{3,1},{5,7},{7,5},{8,10},{10,8},{12,... | collective-permute-start | bytes 3145736 | tf_op jit(solution)/shard_map/ppermute | solution.py:37
  526.6 55.6 %collective-permute-start.54 = (bf16[2,512,512]{2,1,0:T(8,128)(2,1)S(1)}, bf16[2,512,512]{2,1,0:T(8,128)(2,1)S(1)}, u32[]{:S(2)}, u32[]{:S(2)}) collective-permute-start(bf16[2,512,512]{2,1,0:T(8,128)(2,1)S(1)} %get-tuple-element.730), channel_id=1, source_target_pairs={{0,2},{2,0},{4,6},{6,4},{1,3},{3,1},{5,7},{7,5},{8,10},{10,8},{12,... | collective-permute-start | bytes 3145736 | tf_op jit(solution)/shard_map/ppermute | solution.py:37
  528.2 32.8 %collective-permute-start.50 = (bf16[256,1024]{1,0:T(8,128)(2,1)}, bf16[256,1024]{1,0:T(8,128)(2,1)S(1)}, u32[]{:S(2)}, u32[]{:S(2)}) collective-permute-start(bf16[256,1024]{1,0:T(8,128)(2,1)} %add_convert_fusion.10), channel_id=1, source_target_pairs={{0,8},{8,0},{16,24},{24,16},{1,9},{9,1},{17,25},{25,17},{2,10},{10... | collective-permute-start | bytes 1572872 | tf_op jit(solution)/shard_map/ppermute | solution.py:37
  529.3 31.8 %collective-permute-start.51 = (bf16[256,1024]{1,0:T(8,128)(2,1)}, bf16[256,1024]{1,0:T(8,128)(2,1)S(1)}, u32[]{:S(2)}, u32[]{:S(2)}) collective-permute-start(bf16[256,1024]{1,0:T(8,128)(2,1)} %add_convert_fusion.9), channel_id=1, source_target_pairs={{0,16},{8,24},{16,0},{24,8},{1,17},{9,25},{17,1},{25,9},{2,18},{10... | collective-permute-start | bytes 1572872 | tf_op jit(solution)/shard_map/ppermute | solution.py:37
  536.7 28.6 %collective-permute-start.49 = (bf16[512,1024]{1,0:T(8,128)(2,1)S(1)}, bf16[512,1024]{1,0:T(8,128)(2,1)S(1)}, u32[]{:S(2)}, u32[]{:S(2)}) collective-permute-start(bf16[512,1024]{1,0:T(8,128)(2,1)S(1)} %get-tuple-element.766.refs_2_), channel_id=1, source_target_pairs={{0,1},{1,0},{2,3},{3,2},{4,5},{5,4},{6,7},{7,6},{8,9},{9,8},{10,11... | collective-permute-start | bytes 3145736 | tf_op jit(solution)/shard_map/ppermute | solution.py:37
  551.2 34.5 %collective-permute-start.58 = (bf16[2,64,2048]{2,1,0:T(8,128)(2,1)S(1)}, bf16[2,64,2048]{2,1,0:T(8,128)(2,1)S(1)}, u32[]{:S(2)}, u32[]{:S(2)}) collective-permute-start(bf16[2,64,2048]{2,1,0:T(8,128)(2,1)S(1)} %slice.812), channel_id=1, source_target_pairs={{0,4},{2,6},{4,0},{6,2},{1,5},{3,7},{5,1},{7,3},{8,12},{10,14},{12... | collective-permute-start | bytes 1572872 | tf_op jit(solution)/shard_map/ppermute | solution.py:37
  562.9 46.7 %collective-permute-start.64 = (bf16[2,128,1024]{2,1,0:T(8,128)(2,1)}, bf16[2,128,1024]{2,1,0:T(8,128)(2,1)}, u32[]{:S(2)}, u32[]{:S(2)}) collective-permute-start(bf16[2,128,1024]{2,1,0:T(8,128)(2,1)} %fusion.11), channel_id=1, source_target_pairs={{0,2},{2,0},{4,6},{6,4},{1,3},{3,1},{5,7},{7,5},{8,10},{10,8},{12,... | collective-permute-start | bytes 1572872 | tf_op jit(solution)/shard_map/ppermute | solution.py:37
  587.6 26.2 %collective-permute-start.59 = (bf16[512,1024]{1,0:T(8,128)(2,1)}, bf16[512,1024]{1,0:T(8,128)(2,1)}, u32[]{:S(2)}, u32[]{:S(2)}) collective-permute-start(bf16[512,1024]{1,0:T(8,128)(2,1)} %get-tuple-element.814), channel_id=1, source_target_pairs={{0,16},{8,24},{16,0},{24,8},{1,17},{9,25},{17,1},{25,9},{2,18},{10... | collective-permute-start | bytes 3145736 | tf_op jit(solution)/shard_map/ppermute | solution.py:37
  594.5 43.5 %collective-permute-start.63 = (bf16[2,128,2048]{2,1,0:T(8,128)(2,1)}, bf16[2,128,2048]{2,1,0:T(8,128)(2,1)}, u32[]{:S(2)}, u32[]{:S(2)}) collective-permute-start(bf16[2,128,2048]{2,1,0:T(8,128)(2,1)} %fusion.1), channel_id=1, source_target_pairs={{0,2},{2,0},{4,6},{6,4},{1,3},{3,1},{5,7},{7,5},{8,10},{10,8},{12,... | collective-permute-start | bytes 3145736 | tf_op jit(solution)/shard_map/ppermute | solution.py:37
  597.7 106.7 %collective-permute-start.53 = (bf16[3,128,1024]{2,1,0:T(8,128)(2,1)}, bf16[3,128,1024]{2,1,0:T(8,128)(2,1)}, u32[]{:S(2)}, u32[]{:S(2)}) collective-permute-start(bf16[3,128,1024]{2,1,0:T(8,128)(2,1)} %pad_maximum_fusion.8), channel_id=1, source_target_pairs={{0,4},{2,6},{4,0},{6,2},{1,5},{3,7},{5,1},{7,3},{8,12},{10,14},{12... | collective-permute-start | bytes 2359304 | tf_op jit(solution)/shard_map/ppermute | solution.py:37
  611.5 47.2 %collective-permute-start.69 = (bf16[2,64,1024]{2,1,0:T(8,128)(2,1)S(1)}, bf16[2,64,1024]{2,1,0:T(8,128)(2,1)S(1)}, u32[]{:S(2)}, u32[]{:S(2)}) collective-permute-start(bf16[2,64,1024]{2,1,0:T(8,128)(2,1)S(1)} %slice.815), channel_id=1, source_target_pairs={{0,4},{2,6},{4,0},{6,2},{1,5},{3,7},{5,1},{7,3},{8,12},{10,14},{12... | collective-permute-start | bytes 786440 | tf_op jit(solution)/shard_map/ppermute | solution.py:37
  613.8 26.5 %collective-permute-start.61 = (bf16[512,1152]{1,0:T(8,128)(2,1)S(1)}, bf16[512,1152]{1,0:T(8,128)(2,1)S(1)}, u32[]{:S(2)}, u32[]{:S(2)}) collective-permute-start(bf16[512,1152]{1,0:T(8,128)(2,1)S(1)} %get-tuple-element.816), channel_id=1, source_target_pairs={{0,16},{8,24},{16,0},{24,8},{1,17},{9,25},{17,1},{25,9},{2,18},{10... | collective-permute-start | bytes 3538952 | tf_op jit(solution)/shard_map/ppermute | solution.py:37
  614.5 26.2 %collective-permute-start.62 = (bf16[512,1152]{1,0:T(8,128)(2,1)S(1)}, bf16[512,1152]{1,0:T(8,128)(2,1)S(1)}, u32[]{:S(2)}, u32[]{:S(2)}) collective-permute-start(bf16[512,1152]{1,0:T(8,128)(2,1)S(1)} %get-tuple-element.817), channel_id=1, source_target_pairs={{0,8},{8,0},{16,24},{24,16},{1,9},{9,1},{17,25},{25,17},{2,10},{10... | collective-permute-start | bytes 3538952 | tf_op jit(solution)/shard_map/ppermute | solution.py:37
  639.7 41.4 %collective-permute-start.71 = (bf16[2,64,2048]{2,1,0:T(8,128)(2,1)S(1)}, bf16[2,64,2048]{2,1,0:T(8,128)(2,1)S(1)}, u32[]{:S(2)}, u32[]{:S(2)}) collective-permute-start(bf16[2,64,2048]{2,1,0:T(8,128)(2,1)S(1)} %slice.811), channel_id=1, source_target_pairs={{0,4},{2,6},{4,0},{6,2},{1,5},{3,7},{5,1},{7,3},{8,12},{10,14},{12... | collective-permute-start | bytes 1572872 | tf_op jit(solution)/shard_map/ppermute | solution.py:37
  678.0 25.5 %collective-permute-start.70 = (bf16[2,128,1152]{2,1,0:T(8,128)(2,1)S(1)}, bf16[2,128,1152]{2,1,0:T(8,128)(2,1)S(1)}, u32[]{:S(2)}, u32[]{:S(2)}) collective-permute-start(bf16[2,128,1152]{2,1,0:T(8,128)(2,1)S(1)} %fusion.7), channel_id=1, source_target_pairs={{0,2},{2,0},{4,6},{6,4},{1,3},{3,1},{5,7},{7,5},{8,10},{10,8},{12,... | collective-permute-start | bytes 1769480 | tf_op jit(solution)/shard_map/ppermute | solution.py:37
  678.1 35.5 %collective-permute-start.74 = (bf16[1,128,1024]{2,1,0:T(8,128)(2,1)S(1)}, bf16[1,128,1024]{2,1,0:T(8,128)(2,1)S(1)}, u32[]{:S(2)}, u32[]{:S(2)}) collective-permute-start(bf16[1,128,1024]{2,1,0:T(8,128)(2,1)S(1)} %fusion.15), channel_id=1, source_target_pairs={{0,4},{2,6},{4,0},{6,2},{1,5},{3,7},{5,1},{7,3},{8,12},{10,14},{12... | collective-permute-start | bytes 786440 | tf_op jit(solution)/shard_map/ppermute | solution.py:37
  680.1 33.3 %collective-permute-start.75 = (bf16[2,64,1024]{2,1,0:T(8,128)(2,1)S(1)}, bf16[2,64,1024]{2,1,0:T(8,128)(2,1)S(1)}, u32[]{:S(2)}, u32[]{:S(2)}) collective-permute-start(bf16[2,64,1024]{2,1,0:T(8,128)(2,1)S(1)} %slice.814), channel_id=1, source_target_pairs={{0,4},{2,6},{4,0},{6,2},{1,5},{3,7},{5,1},{7,3},{8,12},{10,14},{12... | collective-permute-start | bytes 786440 | tf_op jit(solution)/shard_map/ppermute | solution.py:37
  (174 other events, 1686.1 us)
Sparse Core Ops, SparseCore 0:
  86.8 56.9 all-gather.2
  181.7 46.6 all-gather.4
